TPU v7x, 128 devices: a whole 4x4x4 slice. The times are simulated.
128 devices in a mesh: dp: 4 (over y_hi, core), row: 4 (over x), col: 8 (over z, y_lo).
Axes of the slice: x: 4, y: 4 (y_hi: 2, y_lo: 2; y = y_hi * 2 + y_lo), z: 4, core: 2. Of those that a mesh axis runs over, the one named last changes fastest.
Arguments:
- input_map: bfloat16 [4, 64, 512, 256], P('dp', 'row', 'col'), may hold values from -6 to 6
- dw_kernel: bfloat16 [3, 3, 256], replicated, may hold values from -2 to 2
- gain_one: float32 [256], replicated, may hold values from 0.1 to 1.9
- w_qkv: bfloat16 [256, 768], replicated, may hold values from -4 to 4
- w_out: bfloat16 [256, 256], replicated, may hold values from -0.375 to 0.375
- gain_two: float32 [256], replicated, may hold values from 0.1 to 1.9
- w_up: bfloat16 [256, 1024], replicated, may hold values from -0.375 to 0.375
- w_down: bfloat16 [1024, 256], replicated, may hold values from -0.1875 to 0.1875
- cotangent: bfloat16 [4, 64, 512, 256], P('dp', 'row', 'col'), may hold values from -6 to 6
Outputs:
- input_grad: float32 [4, 64, 512, 256], P('dp', 'row', 'col')
- kernel_grad: float32 [3, 3, 256], replicated
- gain_one_grad: float32 [256], replicated
- qkv_grad: float32 [256, 768], replicated
- out_grad: float32 [256, 256], replicated
- gain_two_grad: float32 [256], replicated
- up_grad: float32 [256, 1024], replicated
- down_grad: float32 [1024, 256], replicated
All inputs are finite; a program needn't handle non-finite values.
Results may differ from a plain program's by a relative error of at most 0.0085.
The roundings to bfloat16 on the way count: a program that leaves them out, or rounds other values in their place, can miss the bound.
Values may be sent and summed in bfloat16 or wider, within the bound.
No kernel may reach another device: no remote copies, remote signals or barrier semaphores. Data moves between devices by JAX's collectives and lax.ppermute only.
A program may use at most 128 MiB of HBM per device.

v0:
```python
import math

import jax
import jax.numpy as jnp
import numpy as np
from jax import lax
from jax.experimental import pallas as pl
from jax.experimental.pallas import tpu as pltpu
from jax.sharding import Mesh
from jax.sharding import PartitionSpec as P

HEADS = 8
C = 256
FF = 1024
PIECE = 56
norm_eps = 1e-05
gelu_coef = 0.7978845608028654
cubic_coef = 0.044715
HEAD_SCALE = 1.0 / math.sqrt(C // HEADS)
TOKENS = 1024

F32 = jnp.float32
BF16 = jnp.bfloat16


def tile_to_columns():
    out = np.zeros((256, 256), np.float32)
    for col in range(16):
        for row in range(16):
            out[col * 16 + row, row * 16 + col] = 1
    return out


def sources_to_groups():
    out = np.zeros((3, 128, 128), np.float32)
    for p in range(8):
        for a in range(2):
            for e in range(8):
                for variant, shift in enumerate((0, -1, 1)):
                    if 0 <= e + shift < 8:
                        out[variant, p * 16 + a * 8 + e, (e + shift) * 16 + a * 8 + p] = 1
    return out


def groups_to_pieces():
    out = np.zeros((3, 8 * PIECE, 384), np.float32)

    def source(j, row, e):
        if row == 0:
            return 256 + j * 8 + e
        if row == 17:
            return 272 + j * 8 + e
        a, p = divmod(row - 1, 8)
        return (j * 8 + p) * 16 + a * 8 + e

    for c in range(8):
        for row in range(18):
            for slot in range(2):
                out[0, c * PIECE + slot * 18 + row, source(slot, row, c)] = 1
            if c + 1 < 8:
                out[1, c * PIECE + 36 + row, source(0, row, c + 1)] = 1
            if c - 1 >= 0:
                out[2, c * PIECE + 36 + row, source(1, row, c - 1)] = 1
    return out


def pieces_to_tile():
    main = np.zeros((288, 8 * PIECE), np.float32)
    right = np.zeros((144, 8 * PIECE), np.float32)
    left = np.zeros((144, 8 * PIECE), np.float32)
    for row in range(18):
        for q in range(16):
            main[row * 16 + q, (q // 2) * PIECE + (q % 2) * 18 + row] = 1
        right[row * 8, 36 + row] = 1
        left[row * 8 + 7, 7 * PIECE + 36 + row] = 1
    return main, right, left


def head_tables():
    spread = np.zeros((512, 64), np.float32)
    mask = np.zeros((512, C), np.float32)
    for k in range(64):
        for h in range(HEADS):
            spread[k * 8 + h, k] = 1
            mask[k * 8 + h, h * 32 : (h + 1) * 32] = 1
    return spread, spread.T.copy(), mask


def dot(a, b):
    return lax.dot_general(a, b, (((1,), (0,)), ((), ())), preferred_element_type=F32)


def dot_nt(a, b):
    return lax.dot_general(a, b, (((1,), (1,)), ((), ())), preferred_element_type=F32)


def dot_tn(a, b):
    return lax.dot_general(a, b, (((0,), (0,)), ((), ())), preferred_element_type=F32)


def norm(values):
    center = values - jnp.mean(values, axis=-1, keepdims=True)
    inverse = lax.rsqrt(jnp.mean(center * center, axis=-1, keepdims=True) + norm_eps)
    return center * inverse, inverse


def norm_back(upstream, normed, inverse, gain):
    scaled = upstream * gain
    return inverse * (
        scaled
        - jnp.mean(scaled, axis=-1, keepdims=True)
        - normed * jnp.mean(scaled * normed, axis=-1, keepdims=True)
    )


def fold_rows(values):
    return jnp.sum(values.reshape(-1, 8, values.shape[-1]), axis=0)


def over_keys(values, combine):
    out = combine(
        combine(values[:, 0:128], values[:, 128:256]),
        combine(values[:, 256:384], values[:, 384:512]),
    )
    for shift in (64, 32, 16, 8):
        out = combine(out, pltpu.roll(out, shift, axis=1))
    return jnp.concatenate([out] * 4, axis=1)


def pack_kernel(halo, x_ref, perm_ref, out_ref):
    perm = perm_ref[...]
    for block in range(4):
        tokens = x_ref[:, 16 * block : 16 * block + 16, :].reshape(256, C)
        columns = dot(perm, tokens).astype(BF16).reshape(16, 16, C)
        for i in range(16):
            q = 16 * block + i
            k, odd = divmod(q, 2)
            if not halo:
                out_ref[k, odd] = columns[i]
            elif odd:
                out_ref[k, 2] = columns[i]
                out_ref[(k + 1) % 32, 0] = columns[i]
            else:
                out_ref[k, 1] = columns[i]
                out_ref[(k - 1) % 32, 3] = columns[i]


def forward_kernel(
    place_ref, x_ref, cot_ref, perm_ref, dw_ref, gain_one_ref, w_qkv_ref, w_out_ref, gain_two_ref,
    w_up_ref, w_down_ref, spread_ref, mask_ref,
    xs_ref, in_ref, proj_ref, probs_ref, mixed_grad_ref, resid_grad_ref, keep_ref, send_ref,
    out_grad_ref, gain_grad_ref,
    cot_s, mixed_s, two_s, low_s, act_s, pre_s, sums_s,
):
    owner = place_ref[0]
    core = place_ref[1]
    first = perm_ref[jnp.where(owner == 0, 1, 0)]
    last = perm_ref[jnp.where(owner == 31, 2, 0)]
    plain = perm_ref[0]

    for r in range(4):
        for j in range(4):
            perm = first if j == 0 else (last if j == 3 else plain)
            tokens = x_ref[8 * r : 8 * r + 8, j].reshape(128, C)
            moved = dot(perm, tokens).astype(BF16).reshape(8, 16, C)
            for p in range(8):
                xs_ref[j, p + 1, 16 * r : 16 * r + 16, :] = moved[p]
    edge = jnp.zeros((8, C), F32)
    for j in range(4):
        lowest = xs_ref[j, 8].astype(F32)
        xs_ref[j, 0] = jnp.concatenate([edge, lowest[:56]], axis=0).astype(BF16)
        highest = xs_ref[j, 1].astype(F32)
        xs_ref[j, 9] = jnp.concatenate([highest[8:], edge], axis=0).astype(BF16)

    gain_one = gain_one_ref[...]

    def conv(g, carry):
        j, p = g // 8, g % 8
        total = xs_ref[j + 1, p + 1].astype(F32)
        for u in range(3):
            for v in range(3):
                total = total + dw_ref[3 * u + v : 3 * u + v + 1, :] * xs_ref[j + v, p + u].astype(F32)
        start = total.astype(BF16)
        rows = pl.ds(pl.multiple_of(g * 64, 64), 64)
        in_ref[rows, :] = start
        normed, _ = norm(start.astype(F32))
        two_s[rows, :] = (normed * gain_one).astype(BF16)
        return carry

    lax.fori_loop(0, 16, conv, 0)

    def project(i, carry):
        rows = pl.ds(pl.multiple_of(i * 256, 256), 256)
        proj_ref[rows, :] = dot(two_s[rows, :], w_qkv_ref[...]).astype(BF16)
        return carry

    lax.fori_loop(0, 4, project, 0)

    spread = spread_ref[...]
    mask = mask_ref[...]

    def attend(g, carry):
        rows = pl.ds(pl.multiple_of(g * 64, 64), 64)
        query = proj_ref[rows, 0:256]
        keys = dot(spread, proj_ref[rows, 256:512]).astype(BF16) * mask
        values = dot(spread, proj_ref[rows, 512:768]).astype(BF16) * mask
        scores = dot_nt(query, keys) * HEAD_SCALE
        expos = jnp.exp(scores - over_keys(scores, jnp.maximum))
        probs = (expos / over_keys(expos, jnp.add)).astype(BF16)
        probs_ref[rows, :] = probs
        mixed_s[rows, :] = dot(probs, values).astype(BF16)
        return carry

    lax.fori_loop(0, 16, attend, 0)

    for r in range(4):
        for j in range(2):
            tokens = cot_ref[8 * r : 8 * r + 8, j].reshape(128, C)
            moved = dot(plain, tokens).astype(BF16).reshape(8, 16, C)
            for p in range(8):
                cot_s[(j * 8 + p) * 64 + 16 * r : (j * 8 + p) * 64 + 16 * r + 16, :] = moved[p]

    gain_two = gain_two_ref[...]

    def tail(i, gain_grad):
        rows = pl.ds(pl.multiple_of(i * 128, 128), 128)
        cot = cot_s[rows, :]
        resid = in_ref[rows, :].astype(F32) + dot(mixed_s[rows, :], w_out_ref[...])
        normed, inverse = norm(resid)
        inputs = (normed * gain_two).astype(BF16)
        two_s[rows, :] = inputs
        pre = dot(inputs, w_up_ref[...])
        square = pre * pre
        tangent = jnp.tanh(gelu_coef * (pre + cubic_coef * square * pre))
        half = 0.5 * (1.0 + tangent)
        act_s[rows, :] = (pre * half).astype(BF16)
        slope = half + 0.5 * pre * (1.0 - tangent * tangent) * gelu_coef * (
            1.0 + 3.0 * cubic_coef * square
        )
        pre_grad = (dot_nt(cot, w_down_ref[...]) * slope).astype(BF16)
        pre_s[rows, :] = pre_grad
        in_grad = dot_nt(pre_grad, w_up_ref[...])
        resid_grad = cot.astype(F32) + norm_back(in_grad, normed, inverse, gain_two)
        resid_grad_ref[rows, :] = resid_grad
        low = resid_grad.astype(BF16)
        low_s[rows, :] = low
        mixed_grad_ref[rows, :] = dot_nt(low, w_out_ref[...]).astype(BF16)
        return gain_grad + fold_rows(in_grad * normed)

    gain_grad = lax.fori_loop(0, 8, tail, jnp.zeros((8, C), F32))
    gain_grad_ref[...] = gain_grad

    cot_turned = cot_s[...].T
    two_turned = two_s[...].T
    for block in range(4):
        columns = slice(256 * block, 256 * block + 256)
        down = dot(cot_turned, act_s[:, columns])
        sums_s[256 * block : 256 * block + 256, :] = down.T.astype(BF16)
        up = dot(two_turned, pre_s[:, columns])
        sums_s[1024 + 256 * block : 1280 + 256 * block, :] = up.astype(BF16)
    keep_ref[...] = sums_s[pl.ds(pl.multiple_of(core * 1024, 1024), 1024), :]
    send_ref[...] = sums_s[pl.ds(pl.multiple_of((1 - core) * 1024, 1024), 1024), :]
    out_grad_ref[...] = dot(mixed_s[...].T, low_s[...])


def backward_kernel(
    place_ref, xs_ref, in_ref, proj_ref, probs_ref, mixed_grad_ref, resid_grad_ref, out_grad_ref,
    gain_two_grad_ref, gain_one_ref, w_qkv_ref, spread_ref, gather_ref, mask_ref, perm_ref,
    pieces_ref, keep_ref, send_ref,
    proj_grad_s, inputs_s, grad_s, sums_s,
):
    owner = place_ref[0]
    core = place_ref[1]
    spread = spread_ref[...]
    gather = gather_ref[...]
    mask = mask_ref[...]

    def attend_back(g, carry):
        rows = pl.ds(pl.multiple_of(g * 64, 64), 64)
        query = proj_ref[rows, 0:256]
        keys = dot(spread, proj_ref[rows, 256:512]).astype(BF16) * mask
        values = dot(spread, proj_ref[rows, 512:768]).astype(BF16) * mask
        probs = probs_ref[rows, :]
        upstream = mixed_grad_ref[rows, :]
        wide = probs.astype(F32)
        prob_grad = dot_nt(upstream, values)
        score_grad = (
            wide * (prob_grad - over_keys(wide * prob_grad, jnp.add)) * HEAD_SCALE
        ).astype(BF16)
        proj_grad_s[rows, 0:256] = dot(score_grad, keys).astype(BF16)
        key_terms = dot_tn(score_grad, query).astype(BF16) * mask
        value_terms = dot_tn(probs, upstream).astype(BF16) * mask
        proj_grad_s[rows, 256:512] = dot(gather, key_terms).astype(BF16)
        proj_grad_s[rows, 512:768] = dot(gather, value_terms).astype(BF16)
        return carry

    lax.fori_loop(0, 16, attend_back, 0)

    gain_one = gain_one_ref[...]

    def head(i, gain_grad):
        rows = pl.ds(pl.multiple_of(i * 128, 128), 128)
        normed, inverse = norm(in_ref[rows, :].astype(F32))
        inputs_s[rows, :] = (normed * gain_one).astype(BF16)
        in_grad = dot_nt(proj_grad_s[rows, :], w_qkv_ref[...])
        grad_s[rows, :] = resid_grad_ref[rows, :] + norm_back(in_grad, normed, inverse, gain_one)
        return gain_grad + fold_rows(in_grad * normed)

    gain_grad = lax.fori_loop(0, 8, head, jnp.zeros((8, C), F32))

    which = jnp.where(owner == 0, 1.0, 0.0).astype(BF16)
    other = jnp.where(owner == 31, 1.0, 0.0).astype(BF16)
    perm = perm_ref[0] + perm_ref[1] * which + perm_ref[2] * other
    edge = jnp.zeros((8, C), F32)
    for r in range(4):
        parts = [grad_s[64 * g + 16 * r : 64 * g + 16 * r + 16, :] for g in range(16)]
        for j in range(2):
            lowest = 64 * (8 * j + 7) + 16 * r - 8
            parts.append(grad_s[lowest : lowest + 8, :] if r > 0 else edge)
        for j in range(2):
            highest = 64 * 8 * j + 16 * r + 16
            parts.append(grad_s[highest : highest + 8, :] if r < 3 else edge)
        parts.append(jnp.zeros((96, C), F32))
        tokens = jnp.concatenate(parts, axis=0).astype(BF16)
        pieces_ref[r] = dot(perm, tokens).astype(BF16)

    def taps(g, sums):
        j, p = g // 8, g % 8
        grad = grad_s[pl.ds(pl.multiple_of(g * 64, 64), 64), :]
        return tuple(
            sums[3 * u + v] + fold_rows(grad * xs_ref[j + v, p + u].astype(F32))
            for u in range(3)
            for v in range(3)
        )

    kernel_grad = lax.fori_loop(0, 16, taps, (jnp.zeros((8, C), F32),) * 9)

    inputs_turned = inputs_s[...].T
    for block in range(3):
        columns = slice(256 * block, 256 * block + 256)
        terms = dot(inputs_turned, proj_grad_s[:, columns]).astype(BF16)
        sums_s[256 * block : 256 * block + 256, 0:256] = terms
    sums_s[768:1024, 0:256] = out_grad_ref[...].astype(BF16)
    small = [jnp.sum(term, axis=0, keepdims=True) for term in kernel_grad]
    small.append(jnp.sum(gain_grad, axis=0, keepdims=True))
    small.append(jnp.sum(gain_two_grad_ref[...], axis=0, keepdims=True))
    small.append(jnp.zeros((5, C), F32))
    small = jnp.concatenate(small, axis=0).astype(BF16)
    sums_s[:, 256:384] = jnp.zeros((1024, 128), BF16)
    sums_s[0:16, 256:384] = small[:, 0:128]
    sums_s[16:32, 256:384] = small[:, 128:256]
    keep_ref[...] = sums_s[pl.ds(pl.multiple_of(core * 512, 512), 512), :]
    send_ref[...] = sums_s[pl.ds(pl.multiple_of((1 - core) * 512, 512), 512), :]


def total_kernel(factor, x_ref, out_ref):
    total = jnp.sum(x_ref[...].astype(F32), axis=0) * factor
    out_ref[...] = jnp.broadcast_to(total.astype(BF16)[None], out_ref.shape)


def tile_kernel(pieces_ref, main_ref, right_ref, left_ref, dw_ref, out_ref, wide):
    for block in range(4):
        columns = dot(main_ref[...], pieces_ref[block])
        wide[:, 8 + 16 * block : 24 + 16 * block, :] = columns.reshape(18, 16, C)
    wide[:, 72:80, :] = dot(right_ref[...], pieces_ref[0]).reshape(18, 8, C)
    wide[:, 0:8, :] = dot(left_ref[...], pieces_ref[3]).reshape(18, 8, C)

    def row(i, carry):
        rows = [wide[i + 2 - u] for u in range(3)]
        total = wide[i + 1, 8:72, :]
        for v in range(3):
            term = dw_ref[v : v + 1, :] * rows[0]
            for u in range(1, 3):
                term = term + dw_ref[3 * u + v : 3 * u + v + 1, :] * rows[u]
            total = total + term[9 - v : 73 - v, :]
        out_ref[0, i] = total
        return carry

    lax.fori_loop(0, 16, row, 0)


def outputs_kernel(
    place_ref, t_mine_ref, t_other_ref, q_mine_ref, q_other_ref,
    kernel_ref, gain_one_ref, qkv_ref, out_ref, gain_two_ref, up_ref, down_ref, halves,
):
    core = place_ref[1]

    def lower(mine, other):
        return jnp.where(core == 0, mine.astype(F32), other.astype(F32))

    def upper(mine, other):
        return jnp.where(core == 0, other.astype(F32), mine.astype(F32))

    down_ref[...] = lower(t_mine_ref[...], t_other_ref[...])
    for block in range(4):
        rows = slice(256 * block, 256 * block + 256)
        up_ref[:, rows] = upper(t_mine_ref[rows, :], t_other_ref[rows, :])
    qkv_ref[:, 0:256] = lower(q_mine_ref[0:256, 0:256], q_other_ref[0:256, 0:256])
    qkv_ref[:, 256:512] = lower(q_mine_ref[256:512, 0:256], q_other_ref[256:512, 0:256])
    qkv_ref[:, 512:768] = upper(q_mine_ref[0:256, 0:256], q_other_ref[0:256, 0:256])
    out_ref[...] = upper(q_mine_ref[256:512, 0:256], q_other_ref[256:512, 0:256])
    small = lower(q_mine_ref[0:32, 256:384], q_other_ref[0:32, 256:384])
    small = jnp.concatenate([small[0:16], small[16:32]], axis=1)
    kernel_ref[...] = small[0:9]
    gain_one_ref[...] = small[9:10]
    gain_two_ref[...] = small[10:11]


VMEM = pl.BlockSpec(memory_space=pltpu.VMEM)
SMEM = pl.BlockSpec(memory_space=pltpu.SMEM)


def call(kernel, outs, operands, scratch=(), scalars=0, flops=0, moved=0, limit=48):
    return pl.pallas_call(
        kernel,
        out_shape=tuple(jax.ShapeDtypeStruct(shape, dtype) for shape, dtype in outs),
        in_specs=[SMEM] * scalars + [VMEM] * (len(operands) - scalars),
        out_specs=tuple(VMEM for _ in outs),
        scratch_shapes=[pltpu.VMEM(shape, dtype) for shape, dtype in scratch],
        compiler_params=pltpu.CompilerParams(vmem_limit_bytes=limit * 2**20),
        cost_estimate=pl.CostEstimate(flops=flops, bytes_accessed=moved, transcendentals=0),
    )(*operands)


def local(input_map, dw_kernel, gain_one, w_qkv, w_out, gain_two, w_up, w_down, cotangent):
    tokens_axes = ("row", "col")
    sums_axes = ("yh", "row", "col")
    owner = lax.axis_index("row") * 8 + lax.axis_index("col")
    core = lax.axis_index("core")
    place = jnp.stack([owner, core]).astype(jnp.int32)
    dw_rows = dw_kernel.reshape(9, C).astype(F32)
    spread, gather, mask = (jnp.asarray(t, BF16) for t in head_tables())

    def exchange(stacked, axes):
        return lax.all_to_all(stacked, axes, split_axis=0, concat_axis=0, tiled=True)

    def swap(half):
        return lax.ppermute(half, "core", [(0, 1), (1, 0)])

    to_columns = jnp.asarray(tile_to_columns(), BF16)
    (packed,) = call(
        lambda *refs: pack_kernel(True, *refs),
        [((32, 4, 16, C), BF16)],
        [input_map[0], to_columns],
        flops=2 * 10**8,
        moved=2 * 10**6,
    )
    arrived = exchange(packed, tokens_axes)
    (packed_cot,) = call(
        lambda *refs: pack_kernel(False, *refs),
        [((32, 2, 16, C), BF16)],
        [cotangent[0], to_columns],
        flops=2 * 10**8,
        moved=2 * 10**6,
    )
    arrived_cot = exchange(packed_cot, tokens_axes)

    (
        xs, start, projected, probs, mixed_grad, resid_grad, t_keep, t_send, out_grad, gain_two_grad,
    ) = call(
        forward_kernel,
        [
            ((4, 10, 64, C), BF16),
            ((TOKENS, C), BF16),
            ((TOKENS, 3 * C), BF16),
            ((TOKENS, 512), BF16),
            ((TOKENS, C), BF16),
            ((TOKENS, C), F32),
            ((1024, C), BF16),
            ((1024, C), BF16),
            ((C, C), F32),
            ((8, C), F32),
        ],
        [
            place, arrived, arrived_cot, jnp.asarray(sources_to_groups(), BF16), dw_rows,
            gain_one.reshape(1, C), w_qkv, w_out, gain_two.reshape(1, C), w_up, w_down, spread, mask,
        ],
        [
            ((TOKENS, C), BF16),
            ((TOKENS, C), BF16),
            ((TOKENS, C), BF16),
            ((TOKENS, C), BF16),
            ((TOKENS, FF), BF16),
            ((TOKENS, FF), BF16),
            ((2048, C), BF16),
        ],
        scalars=1,
        flops=8 * 10**9,
        moved=12 * 10**6,
    )

    factor = 1.0 / math.sqrt(TOKENS * 128)

    def reduce_and_share(keep, send, rows, lanes):
        half = (keep.astype(F32) + swap(send).astype(F32)).astype(BF16)
        gathered = exchange(half.reshape(64, rows, lanes), sums_axes)
        (shared,) = call(
            lambda x_ref, out_ref: total_kernel(factor, x_ref, out_ref),
            [((64, rows, lanes), BF16)],
            [gathered],
            flops=10**6,
            moved=10**6,
        )
        mine = exchange(shared, sums_axes).reshape(64 * rows, lanes)
        return mine, swap(mine)

    t_mine, t_other = reduce_and_share(t_keep, t_send, 16, C)

    pieces, q_keep, q_send = call(
        backward_kernel,
        [((4, 8 * PIECE, C), BF16), ((512, 384), BF16), ((512, 384), BF16)],
        [
            place, xs, start, projected, probs, mixed_grad, resid_grad, out_grad, gain_two_grad,
            gain_one.reshape(1, C), w_qkv, spread, gather, mask, jnp.asarray(groups_to_pieces(), BF16),
        ],
        [
            ((TOKENS, 3 * C), BF16),
            ((TOKENS, C), BF16),
            ((TOKENS, C), F32),
            ((1024, 384), BF16),
        ],
        scalars=1,
        flops=5 * 10**9,
        moved=8 * 10**6,
    )
    q_mine, q_other = reduce_and_share(q_keep, q_send, 8, 384)

    back = exchange(pieces.reshape(32, PIECE, C), tokens_axes).reshape(4, 8 * PIECE, C)
    main, right, left = (jnp.asarray(t, BF16) for t in pieces_to_tile())
    (input_grad,) = call(
        tile_kernel,
        [((1, 16, 64, C), F32)],
        [back, main, right, left, dw_rows],
        [((18, 80, C), F32)],
        flops=10**9,
        moved=2 * 10**6,
    )
    kernel_grad, gain_one_grad, qkv_grad, out_sum, gain_two_sum, up_grad, down_grad = call(
        lambda *refs: outputs_kernel(*refs, None),
        [
            ((9, C), F32),
            ((1, C), F32),
            ((C, 3 * C), F32),
            ((C, C), F32),
            ((1, C), F32),
            ((C, FF), F32),
            ((FF, C), F32),
        ],
        [place, t_mine, t_other, q_mine, q_other],
        scalars=1,
        flops=10**6,
        moved=5 * 10**6,
    )
    return (
        input_grad,
        kernel_grad.reshape(3, 3, C),
        gain_one_grad.reshape(C),
        qkv_grad,
        out_sum,
        gain_two_sum.reshape(C),
        up_grad,
        down_grad,
    )


def solution(mesh):
    cores = Mesh(mesh.devices.reshape(2, 2, 4, 8), ("yh", "core", "row", "col"))
    split = P(("yh", "core"), "row", "col", None)
    in_specs = (split, P(), P(), P(), P(), P(), P(), P(), split)
    out_specs = (split, P(), P(), P(), P(), P(), P(), P())
    return jax.shard_map(local, mesh=cores, in_specs=in_specs, out_specs=out_specs, check_vma=False)
```

profile of v0, /device:TPU:0, one launch (start us, length us, event | category | flops | bytes accessed | tf_op | source)
XLA Modules:
  0.0 204.4 jit_solution(15857909774712868624)
XLA Ops:
  0.6 1.0 copy-done
  1.7 0.9 copy-done.2
  2.6 1.1 shard_map.234
  3.7 9.3 %all-to-all-start.1 = ((bf16[32,2,16,256]{3,2,1,0:T(8,128)(2,1)}), bf16[32,2,16,256]{3,2,1,0:T(8,128)(2,1)S(1)}, u32[]{:S(2)}, u32[]{:S(2)}) async-start(bf16[32,2,16,256]{3,2,1,0:T(8,128)(2,1)} %shard_map.234), calls=%async_computation.1 | async-start | bytes 1048576 | tf_op jit(solution)/shard_map/all_to_all | solution.py:435
  13.0 0.0 copy-start.19
  13.0 0.0 copy-start.4
  13.0 0.0 copy-start.5
  13.0 0.0 copy-start.6
  13.0 0.0 copy-start.7
  13.0 0.0 copy-start.8
  13.0 0.0 copy-start.9
  13.1 0.0 copy-start.16
  13.1 0.0 copy-start.17
  13.1 1.3 shard_map.233
  14.4 10.6 %all-to-all-done.1.cot_ref = bf16[32,2,16,256]{3,2,1,0:T(8,128)(2,1)S(1)} async-done(((bf16[32,2,16,256]{3,2,1,0:T(8,128)(2,1)}), bf16[32,2,16,256]{3,2,1,0:T(8,128)(2,1)S(1)}, u32[]{:S(2)}, u32[]{:S(2)}) %all-to-all-start.1) | async-done | bytes 524320 | tf_op jit(solution)/shard_map/all_to_all | solution.py:435
  25.0 4.7 %all-to-all-start = ((bf16[32,4,16,256]{3,2,1,0:T(8,128)(2,1)}), bf16[32,4,16,256]{3,2,1,0:T(8,128)(2,1)}, u32[]{:S(2)}, u32[]{:S(2)}) async-start(bf16[32,4,16,256]{3,2,1,0:T(8,128)(2,1)} %shard_map.233), calls=%async_computation | async-start | bytes 2097152 | tf_op jit(solution)/shard_map/all_to_all | solution.py:435
  29.7 0.1 pad_add_fusion.place_ref.refs_0_
  29.8 16.0 %all-to-all-done.x_ref = bf16[32,4,16,256]{3,2,1,0:T(8,128)(2,1)} async-done(((bf16[32,4,16,256]{3,2,1,0:T(8,128)(2,1)}), bf16[32,4,16,256]{3,2,1,0:T(8,128)(2,1)}, u32[]{:S(2)}, u32[]{:S(2)}) %all-to-all-start) | async-done | bytes 1048608 | tf_op jit(solution)/shard_map/all_to_all | solution.py:435
  45.9 0.0 copy-start.12
  45.9 0.9 copy-done.12
  46.8 36.9 %shard_map.235 = (bf16[4,10,64,256]{3,2,1,0:T(8,128)(2,1)}, bf16[1024,256]{1,0:T(8,128)(2,1)S(1)}, bf16[1024,768]{1,0:T(8,128)(2,1)}, bf16[1024,512]{1,0:T(8,128...) custom-call(s32[2]{0:T(128)S(1)} %pad_add_fusion.place_ref.refs_0_, ...), custom_call_target="tpu_custom_call" | custom-call | flops 8000000000 | bytes 12000000 | tf_op jit(solution)/shard_map/pallas_call | solution.py:414
  83.7 27.8 %shard_map.236 = (bf16[4,448,256]{2,1,0:T(8,128)(2,1)}, bf16[512,384]{1,0:T(8,128)(2,1)S(1)}, bf16[512,384]{1,0:T(8,128)(2,1)S(1)}) custom-call(s32[2]{0:T(128)S(1)} %pad_add_fusion.place_ref.refs_0_, bf16[4,10,64,256]{3,2,1,0:T(8,128)(2,1)} %get-tuple-element.28.xs_ref, bf16[1024,256]{1,0:T(8,128)(2,1)S(1)} %get-tuple-element.29.in_ref, ...), custom_call_target="tpu_custom_call" | custom-call | flops 5000000000 | bytes 8000000 | tf_op jit(solution)/shard_map/pallas_call | solution.py:414
  111.6 0.0 collective-permute-start.2
  111.6 0.5 collective-permute-start
  112.1 1.2 collective-permute-done.2
  113.3 0.8 fusion
  114.1 6.8 %all-to-all-start.5 = ((bf16[64,8,384]{2,1,0:T(8,128)(2,1)}), bf16[64,8,384]{2,1,0:T(8,128)(2,1)S(1)}, u32[]{:S(2)}, u32[]{:S(2)}) async-start(bf16[64,8,384]{2,1,0:T(8,128)(2,1)} %fusion), calls=%async_computation.5 | async-start | bytes 786432 | tf_op jit(solution)/shard_map/all_to_all | solution.py:435
  121.0 0.0 collective-permute-done
  121.0 0.9 add_convert_fusion
  121.9 10.7 %all-to-all-done.5.x_ref = bf16[64,8,384]{2,1,0:T(8,128)(2,1)S(1)} async-done(((bf16[64,8,384]{2,1,0:T(8,128)(2,1)}), bf16[64,8,384]{2,1,0:T(8,128)(2,1)S(1)}, u32[]{:S(2)}, u32[]{:S(2)}) %all-to-all-start.5) | async-done | bytes 393248 | tf_op jit(solution)/shard_map/all_to_all | solution.py:435
  132.6 5.5 %all-to-all-start.3 = ((bf16[64,16,256]{2,1,0:T(8,128)(2,1)}), bf16[64,16,256]{2,1,0:T(8,128)(2,1)S(1)}, u32[]{:S(2)}, u32[]{:S(2)}) async-start(bf16[64,16,256]{2,1,0:T(8,128)(2,1)} %bitcast.8), calls=%async_computation.3 | async-start | bytes 1048576 | tf_op jit(solution)/shard_map/all_to_all | solution.py:435
  138.1 0.8 shard_map.239
  139.0 10.6 %all-to-all-done.3.x_ref = bf16[64,16,256]{2,1,0:T(8,128)(2,1)S(1)} async-done(((bf16[64,16,256]{2,1,0:T(8,128)(2,1)}), bf16[64,16,256]{2,1,0:T(8,128)(2,1)S(1)}, u32[]{:S(2)}, u32[]{:S(2)}) %all-to-all-start.3) | async-done | bytes 524320 | tf_op jit(solution)/shard_map/all_to_all | solution.py:435
  149.6 5.6 %all-to-all-start.6 = ((bf16[64,8,384]{2,1,0:T(8,128)(2,1)}), bf16[64,8,384]{2,1,0:T(8,128)(2,1)S(1)}, u32[]{:S(2)}, u32[]{:S(2)}) async-start(bf16[64,8,384]{2,1,0:T(8,128)(2,1)} %shard_map.239), calls=%async_computation.6 | async-start | bytes 786432 | tf_op jit(solution)/shard_map/all_to_all | solution.py:435
  155.2 0.1 shard_map.238
  155.3 0.0 copy-start.11
  155.3 0.0 copy-start.14
  155.3 0.0 copy-start.15
  155.3 10.5 %all-to-all-done.6 = bf16[64,8,384]{2,1,0:T(8,128)(2,1)S(1)} async-done(((bf16[64,8,384]{2,1,0:T(8,128)(2,1)}), bf16[64,8,384]{2,1,0:T(8,128)(2,1)S(1)}, u32[]{:S(2)}, u32[]{:S(2)}) %all-to-all-start.6) | async-done | bytes 393248 | tf_op jit(solution)/shard_map/all_to_all | solution.py:435
  165.9 16.5 %all_to_all.35 = bf16[64,16,256]{2,1,0:T(8,128)(2,1)S(1)} all-to-all(bf16[64,16,256]{2,1,0:T(8,128)(2,1)S(1)} %shard_map.238), channel_id=1, replica_groups=mesh['yh'=2,'core'=2,'row'=4,'col'=8] {'yh','row','col'}, dimensions={0} | all-to-all | bytes 1048576 | tf_op jit(solution)/shard_map/all_to_all | solution.py:435
  182.4 4.0 %all-to-all-start.2 = ((bf16[32,56,256]{2,1,0:T(8,128)(2,1)}), bf16[32,56,256]{2,1,0:T(8,128)(2,1)S(1)}, u32[]{:S(2)}, u32[]{:S(2)}) async-start(bf16[32,56,256]{2,1,0:T(8,128)(2,1)} %bitcast.6), calls=%async_computation.2 | async-start | bytes 1835008 | tf_op jit(solution)/shard_map/all_to_all | solution.py:435
  186.4 0.1 collective-permute-start.1
  186.5 0.5 collective-permute-start.3
  187.0 12.0 %all-to-all-done.2 = bf16[32,56,256]{2,1,0:T(8,128)(2,1)S(1)} async-done(((bf16[32,56,256]{2,1,0:T(8,128)(2,1)}), bf16[32,56,256]{2,1,0:T(8,128)(2,1)S(1)}, u32[]{:S(2)}, u32[]{:S(2)}) %all-to-all-start.2) | async-done | bytes 917536 | tf_op jit(solution)/shard_map/all_to_all | solution.py:435
  199.0 2.4 %shard_map.237 = f32[1,16,64,256]{3,2,1,0:T(8,128)} custom-call(bf16[4,448,256]{2,1,0:T(8,128)(2,1)S(1)} %bitcast.19, bf16[288,448]{1,0:T(8,128)(2,1)S(1)} %copy-done.11, bf16[144,448]{1,0:T(8,128)(2,1)S(1)} %copy-done.15, bf16[144,448]{1,0:T(8,128)(2,1)S(1)} %copy-done.14, f32[9,256]{1,0:T(8,128)S(1)} %reshape.64.dw_ref), custom_call_target="tpu_custom_call" | custom-call | flops 1000000000 | bytes 2000000 | tf_op jit(solution)/shard_map/pallas_call | solution.py:414
  201.5 0.0 collective-permute-done.3.refs_4_
  201.5 2.3 %shard_map.240 = (f32[9,256]{1,0:T(8,128)S(1)}, f32[1,256]{1,0:T(1,128)}, f32[256,768]{1,0:T(8,128)}, f32[256,256]{1,0:T(8,128)}, f32[1,256]{1,0:T(1,128)}, /*index=5*/f32[256,1024]{1,0:T(8,128)}, f32[1024,256]{1,0:T(8,128)}) custom-call(s32[2]{0:T(128)S(1)} %pad_add_fusion.place_ref.refs_0_, bf16[1024,256]{1,0:T(8,128)(2,1)S(1)} %bitcast.16, ...), custom_call_target="tpu_custom_call" | custom-call | flops 1000000 | bytes 5000000 | tf_op jit(solution)/shard_map/pallas_call | solution.py:414
  203.7 0.6 reshape.61
  (26 shorter events, 0.1 us)
Async XLA Ops:
  0.6 1.0 copy-start
  1.7 0.9 copy-start.2
  2.6 10.4 %copy-start.1 = (bf16[1,16,64,256]{3,2,1,0:T(8,128)(2,1)S(1)}, bf16[1,16,64,256]{3,2,1,0:T(8,128)(2,1)}, u32[]{:S(2)}) copy-start(bf16[1,16,64,256]{3,2,1,0:T(8,128)(2,1)} %param.18) | copy-start | bytes 1572868
  2.6 10.4 %copy-start.3 = (bf16[256,256]{1,0:T(8,128)(2,1)S(1)}, bf16[256,256]{1,0:T(8,128)(2,1)}, u32[]{:S(2)}) copy-start(bf16[256,256]{1,0:T(8,128)(2,1)} %constant.37.clone.refs_1_) | copy-start | bytes 393220
  3.7 21.3 %all-to-all-start.1 = ((bf16[32,2,16,256]{3,2,1,0:T(8,128)(2,1)}), bf16[32,2,16,256]{3,2,1,0:T(8,128)(2,1)S(1)}, u32[]{:S(2)}, u32[]{:S(2)}) async-start(bf16[32,2,16,256]{3,2,1,0:T(8,128)(2,1)} %shard_map.234), calls=%async_computation.1 | async-start | bytes 1048576 | tf_op jit(solution)/shard_map/all_to_all | solution.py:435
  13.0 16.7 %copy-start.19 = (bf16[3,3,256]{2,1,0:T(4,128)(2,1)S(1)}, bf16[3,3,256]{2,1,0:T(4,128)(2,1)}, u32[]{:S(2)}) copy-start(bf16[3,3,256]{2,1,0:T(4,128)(2,1)} %param.19) | copy-start | bytes 13828
  13.0 32.8 %copy-start.4 = (bf16[256,1024]{1,0:T(8,128)(2,1)S(1)}, bf16[256,1024]{1,0:T(8,128)(2,1)}, u32[]{:S(2)}) copy-start(bf16[256,1024]{1,0:T(8,128)(2,1)} %w_up_ref.1) | copy-start | bytes 1572868
  13.0 32.8 %copy-start.5 = (bf16[1024,256]{1,0:T(8,128)(2,1)S(1)}, bf16[1024,256]{1,0:T(8,128)(2,1)}, u32[]{:S(2)}) copy-start(bf16[1024,256]{1,0:T(8,128)(2,1)} %w_down_ref.1) | copy-start | bytes 1572868
  13.0 32.8 %copy-start.6 = (bf16[256,768]{1,0:T(8,128)(2,1)S(1)}, bf16[256,768]{1,0:T(8,128)(2,1)}, u32[]{:S(2)}) copy-start(bf16[256,768]{1,0:T(8,128)(2,1)} %w_qkv_ref.3) | copy-start | bytes 1179652
  13.0 32.8 %copy-start.7 = (bf16[256,256]{1,0:T(8,128)(2,1)S(1)}, bf16[256,256]{1,0:T(8,128)(2,1)}, u32[]{:S(2)}) copy-start(bf16[256,256]{1,0:T(8,128)(2,1)} %w_out_ref.1) | copy-start | bytes 393220
  13.0 32.8 %copy-start.8 = (f32[256]{0:T(256)S(1)}, f32[256]{0:T(256)}, u32[]{:S(2)}) copy-start(f32[256]{0:T(256)} %param.23) | copy-start | bytes 3076
  13.0 32.8 %copy-start.9 = (f32[256]{0:T(256)S(1)}, f32[256]{0:T(256)}, u32[]{:S(2)}) copy-start(f32[256]{0:T(256)} %param.20) | copy-start | bytes 3076
  13.1 32.8 %copy-start.16 = (bf16[512,64]{1,0:T(8,128)(2,1)S(1)}, bf16[512,64]{1,0:T(8,128)(2,1)}, u32[]{:S(2)}) copy-start(bf16[512,64]{1,0:T(8,128)(2,1)} %constant.34.clone.spread_ref) | copy-start | bytes 196612
  13.1 32.8 %copy-start.17 = (bf16[3,128,128]{2,1,0:T(8,128)(2,1)S(1)}, bf16[3,128,128]{2,1,0:T(8,128)(2,1)}, u32[]{:S(2)}) copy-start(bf16[3,128,128]{2,1,0:T(8,128)(2,1)} %constant.38.clone.perm_ref) | copy-start | bytes 294916
  25.0 20.8 %all-to-all-start = ((bf16[32,4,16,256]{3,2,1,0:T(8,128)(2,1)}), bf16[32,4,16,256]{3,2,1,0:T(8,128)(2,1)}, u32[]{:S(2)}, u32[]{:S(2)}) async-start(bf16[32,4,16,256]{3,2,1,0:T(8,128)(2,1)} %shard_map.233), calls=%async_computation | async-start | bytes 2097152 | tf_op jit(solution)/shard_map/all_to_all | solution.py:435
  45.9 1.0 copy-start.12
  46.8 36.9 %copy-start.10 = (bf16[3,448,384]{2,1,0:T(8,128)(2,1)S(1)}, bf16[3,448,384]{2,1,0:T(8,128)(2,1)}, u32[]{:S(2)}) copy-start(bf16[3,448,384]{2,1,0:T(8,128)(2,1)} %constant.39.clone.perm_ref) | copy-start | bytes 3096580
  46.8 36.9 %copy-start.13 = (bf16[512,256]{1,0:T(8,128)(2,1)S(1)}, bf16[512,256]{1,0:T(8,128)(2,1)}, u32[]{:S(2)}) copy-start(bf16[512,256]{1,0:T(8,128)(2,1)} %constant.36.clone.mask_ref) | copy-start | bytes 786436
  46.8 36.9 %copy-start.18 = (bf16[64,512]{1,0:T(8,128)(2,1)S(1)}, bf16[64,512]{1,0:T(8,128)(2,1)}, u32[]{:S(2)}) copy-start(bf16[64,512]{1,0:T(8,128)(2,1)} %constant.35.clone.gather_ref) | copy-start | bytes 196612
  111.6 1.7 collective-permute-start.2
  111.6 9.4 %collective-permute-start = (bf16[1024,256]{1,0:T(8,128)(2,1)S(1)}, bf16[1024,256]{1,0:T(8,128)(2,1)S(1)}, u32[]{:S(2)}, u32[]{:S(2)}) collective-permute-start(bf16[1024,256]{1,0:T(8,128)(2,1)S(1)} %get-tuple-element.38), channel_id=1, source_target_pairs={{0,32},{32,0},{1,33},{33,1},{2,34},{34,2},{3,35},{35,3},{4,36},{36... | collective-permute-start | bytes 1572872 | tf_op jit(solution)/shard_map/ppermute | solution.py:438
  114.1 18.5 %all-to-all-start.5 = ((bf16[64,8,384]{2,1,0:T(8,128)(2,1)}), bf16[64,8,384]{2,1,0:T(8,128)(2,1)S(1)}, u32[]{:S(2)}, u32[]{:S(2)}) async-start(bf16[64,8,384]{2,1,0:T(8,128)(2,1)} %fusion), calls=%async_computation.5 | async-start | bytes 786432 | tf_op jit(solution)/shard_map/all_to_all | solution.py:435
  132.6 17.0 %all-to-all-start.3 = ((bf16[64,16,256]{2,1,0:T(8,128)(2,1)}), bf16[64,16,256]{2,1,0:T(8,128)(2,1)S(1)}, u32[]{:S(2)}, u32[]{:S(2)}) async-start(bf16[64,16,256]{2,1,0:T(8,128)(2,1)} %bitcast.8), calls=%async_computation.3 | async-start | bytes 1048576 | tf_op jit(solution)/shard_map/all_to_all | solution.py:435
  149.6 16.3 %all-to-all-start.6 = ((bf16[64,8,384]{2,1,0:T(8,128)(2,1)}), bf16[64,8,384]{2,1,0:T(8,128)(2,1)S(1)}, u32[]{:S(2)}, u32[]{:S(2)}) async-start(bf16[64,8,384]{2,1,0:T(8,128)(2,1)} %shard_map.239), calls=%async_computation.6 | async-start | bytes 786432 | tf_op jit(solution)/shard_map/all_to_all | solution.py:435
  155.3 43.7 %copy-start.11 = (bf16[288,448]{1,0:T(8,128)(2,1)S(1)}, bf16[288,448]{1,0:T(8,128)(2,1)}, u32[]{:S(2)}) copy-start(bf16[288,448]{1,0:T(8,128)(2,1)} %constant.40.clone.main_ref) | copy-start | bytes 774148
  155.3 43.7 %copy-start.14 = (bf16[144,448]{1,0:T(8,128)(2,1)S(1)}, bf16[144,448]{1,0:T(8,128)(2,1)}, u32[]{:S(2)}) copy-start(bf16[144,448]{1,0:T(8,128)(2,1)} %constant.42.clone.left_ref) | copy-start | bytes 387076
  155.3 43.7 %copy-start.15 = (bf16[144,448]{1,0:T(8,128)(2,1)S(1)}, bf16[144,448]{1,0:T(8,128)(2,1)}, u32[]{:S(2)}) copy-start(bf16[144,448]{1,0:T(8,128)(2,1)} %constant.41.clone.right_ref) | copy-start | bytes 387076
  182.4 16.6 %all-to-all-start.2 = ((bf16[32,56,256]{2,1,0:T(8,128)(2,1)}), bf16[32,56,256]{2,1,0:T(8,128)(2,1)S(1)}, u32[]{:S(2)}, u32[]{:S(2)}) async-start(bf16[32,56,256]{2,1,0:T(8,128)(2,1)} %bitcast.6), calls=%async_computation.2 | async-start | bytes 1835008 | tf_op jit(solution)/shard_map/all_to_all | solution.py:435
  186.4 15.1 %collective-permute-start.1 = (bf16[1024,256]{1,0:T(8,128)(2,1)S(1)}, bf16[1024,256]{1,0:T(8,128)(2,1)S(1)}, u32[]{:S(2)}, u32[]{:S(2)}) collective-permute-start(bf16[1024,256]{1,0:T(8,128)(2,1)S(1)} %bitcast.15), channel_id=1, source_target_pairs={{0,32},{32,0},{1,33},{33,1},{2,34},{34,2},{3,35},{35,3},{4,36},{36... | collective-permute-start | bytes 1572872 | tf_op jit(solution)/shard_map/ppermute | solution.py:438
  186.5 15.0 %collective-permute-start.3 = (bf16[512,384]{1,0:T(8,128)(2,1)S(1)}, bf16[512,384]{1,0:T(8,128)(2,1)S(1)}, u32[]{:S(2)}, u32[]{:S(2)}) collective-permute-start(bf16[512,384]{1,0:T(8,128)(2,1)S(1)} %bitcast.17), channel_id=1, source_target_pairs={{0,32},{32,0},{1,33},{33,1},{2,34},{34,2},{3,35},{35,3},{4,36},{36... | collective-permute-start | bytes 1179656 | tf_op jit(solution)/shard_map/ppermute | solution.py:438
where the time goes:
time: 205 us; the launch traced here: 204 us
  Pallas kernels  72.8 us (36%)
  waiting for transfers between devices  71.8 us (35%)
  starting transfers between devices  36.9 us (18%)
  blocking collectives  16.5 us (8%)
  local copies, waits for them, and re-layouts  3.6 us (2%)
    pallas_call x8, Pallas kernels, call(): pl.pallas_call(kernel, out_shape=tuple((jax.ShapeDtypeStruct(shape, dtype...  72.8 us
    all_to_all x6, waiting for transfers between devices, exchange(): lax.all_to_all(stacked, axes, split_axis=0, concat_axis=0, tiled=True)  70.5 us
    all_to_all x6, starting transfers between devices, exchange(): lax.all_to_all(stacked, axes, split_axis=0, concat_axis=0, tiled=True)  35.8 us
    all_to_all x1, blocking collectives, exchange(): lax.all_to_all(stacked, axes, split_axis=0, concat_axis=0, tiled=True)  16.5 us
  transfers between devices with their start and end apart: 10, of which 7 were waited for; matrix products, arithmetic and copies ran while one was open for 1% of the time, Pallas kernels for 2%

commit v1 on v0

v1 whole, which is shorter than its diff:
```python
import math

import jax
import jax.numpy as jnp
import numpy as np
from jax import lax
from jax.experimental import pallas as pl
from jax.experimental.pallas import tpu as pltpu
from jax.sharding import Mesh
from jax.sharding import PartitionSpec as P

HEADS = 8
C = 256
FF = 1024
PIECE = 56
norm_eps = 1e-05
gelu_coef = 0.7978845608028654
cubic_coef = 0.044715
HEAD_SCALE = 1.0 / math.sqrt(C // HEADS)
TOKENS = 1024
AHEAD = 4

F32 = jnp.float32
BF16 = jnp.bfloat16


def tile_to_columns():
    out = np.zeros((256, 256), np.float32)
    for col in range(16):
        for row in range(16):
            out[col * 16 + row, row * 16 + col] = 1
    return out


def sources_to_groups():
    out = np.zeros((3, 128, 128), np.float32)
    for p in range(8):
        for a in range(2):
            for e in range(8):
                for variant, shift in enumerate((0, -1, 1)):
                    if 0 <= e + shift < 8:
                        out[variant, p * 16 + a * 8 + e, (e + shift) * 16 + a * 8 + p] = 1
    return out


def groups_to_pieces():
    out = np.zeros((3, 8 * PIECE, 384), np.float32)

    def source(j, row, e):
        if row == 0:
            return 256 + j * 8 + e
        if row == 17:
            return 272 + j * 8 + e
        a, p = divmod(row - 1, 8)
        return (j * 8 + p) * 16 + a * 8 + e

    for c in range(8):
        for row in range(18):
            for slot in range(2):
                out[0, c * PIECE + slot * 18 + row, source(slot, row, c)] = 1
            if c + 1 < 8:
                out[1, c * PIECE + 36 + row, source(0, row, c + 1)] = 1
            if c - 1 >= 0:
                out[2, c * PIECE + 36 + row, source(1, row, c - 1)] = 1
    return out


def pieces_to_tile():
    main = np.zeros((288, 8 * PIECE), np.float32)
    right = np.zeros((144, 8 * PIECE), np.float32)
    left = np.zeros((144, 8 * PIECE), np.float32)
    for row in range(18):
        for q in range(16):
            main[row * 16 + q, (q // 2) * PIECE + (q % 2) * 18 + row] = 1
        right[row * 8, 36 + row] = 1
        left[row * 8 + 7, 7 * PIECE + 36 + row] = 1
    return main, right, left


def head_mask():
    mask = np.zeros((256, 128), np.float32)
    for h in range(4):
        mask[h * 64 : (h + 1) * 64, h * 32 : (h + 1) * 32] = 1
    return np.concatenate([mask, mask], axis=1)


def dot(a, b):
    return lax.dot_general(a, b, (((1,), (0,)), ((), ())), preferred_element_type=F32)


def dot_nt(a, b):
    return lax.dot_general(a, b, (((1,), (1,)), ((), ())), preferred_element_type=F32)


def dot_tn(a, b):
    return lax.dot_general(a, b, (((0,), (0,)), ((), ())), preferred_element_type=F32)


def norm(values):
    center = values - jnp.mean(values, axis=-1, keepdims=True)
    inverse = lax.rsqrt(jnp.mean(center * center, axis=-1, keepdims=True) + norm_eps)
    return center * inverse, inverse


def norm_back(upstream, normed, inverse, gain):
    scaled = upstream * gain
    return inverse * (
        scaled
        - jnp.mean(scaled, axis=-1, keepdims=True)
        - normed * jnp.mean(scaled * normed, axis=-1, keepdims=True)
    )


def fold_rows(values):
    return jnp.sum(values.reshape(-1, 8, values.shape[-1]), axis=0)


def side_by_side(rows):
    return jnp.concatenate([rows[0:64], rows[64:128]], axis=1)


def stacked(rows):
    return jnp.concatenate([rows[:, 0:128], rows[:, 128:256]], axis=0)


def block_diagonal(rows):
    zeros = jnp.zeros((64, 128), rows.dtype)
    upper = jnp.concatenate([rows[0:64], zeros], axis=1)
    return jnp.concatenate([upper, jnp.concatenate([zeros, rows[64:128]], axis=1)], axis=0)


def diagonal(blocks):
    return jnp.concatenate([blocks[0:64, 0:128], blocks[64:128, 128:256]], axis=0)


def by_head(rows, mask):
    return jnp.concatenate([side_by_side(rows)] * 4, axis=0) * mask


def attend_unit(query, key, value, mask):
    scores = dot_nt(by_head(key, mask), block_diagonal(query)).reshape(4, 64, 128) * HEAD_SCALE
    expos = jnp.exp(scores - jnp.max(scores, axis=1, keepdims=True))
    probs = expos * (1.0 / jnp.sum(expos, axis=1, keepdims=True))
    probs = probs.reshape(256, 128).astype(BF16)
    return probs, diagonal(dot_tn(probs, by_head(value, mask))).astype(BF16)


def attend_unit_back(query, key, value, probs, upstream, mask, wide_mask):
    wide = probs.astype(F32).reshape(4, 64, 128)
    upstream = block_diagonal(upstream)
    prob_grad = dot_nt(by_head(value, mask), upstream).reshape(4, 64, 128)
    centre = jnp.sum(wide * prob_grad, axis=1, keepdims=True)
    score_grad = (wide * (prob_grad - centre) * HEAD_SCALE).reshape(256, 128).astype(BF16)
    query_grad = diagonal(dot_tn(score_grad, by_head(key, mask)))
    key_grad = jnp.sum((dot(score_grad, block_diagonal(query)) * wide_mask).reshape(4, 64, 256), axis=0)
    value_grad = jnp.sum((dot(probs, upstream) * wide_mask).reshape(4, 64, 256), axis=0)
    return query_grad.astype(BF16), stacked(key_grad).astype(BF16), stacked(value_grad).astype(BF16)


def pack_kernel(x_ref, cot_ref, perm_ref, out_ref):
    perm = perm_ref[...]
    for block in range(4):
        tokens = x_ref[:, 16 * block : 16 * block + 16, :].reshape(256, C)
        columns = dot(perm, tokens).astype(BF16).reshape(16, 16, C)
        tokens = cot_ref[:, 16 * block : 16 * block + 16, :].reshape(256, C)
        cot_columns = dot(perm, tokens).astype(BF16).reshape(16, 16, C)
        for i in range(16):
            q = 16 * block + i
            k, odd = divmod(q, 2)
            out_ref[k, 4 + odd] = cot_columns[i]
            if odd:
                out_ref[k, 2] = columns[i]
                out_ref[(k + 1) % 32, 0] = columns[i]
            else:
                out_ref[k, 1] = columns[i]
                out_ref[(k - 1) % 32, 3] = columns[i]


def forward_kernel(
    place_ref, x_ref, perm_ref, dw_ref, gain_one_ref, w_qkv_ref, w_out_ref, gain_two_ref,
    w_up_ref, w_down_ref, mask_ref,
    xs_ref, in_ref, proj_ref, probs_ref, mixed_grad_ref, resid_grad_ref, sums_ref,
    out_grad_ref, gain_grad_ref,
    cot_s, mixed_s, two_s, low_s, act_s, pre_s,
):
    owner = place_ref[0]
    first = perm_ref[jnp.where(owner == 0, 1, 0)]
    last = perm_ref[jnp.where(owner == 31, 2, 0)]
    plain = perm_ref[0]

    for r in range(4):
        for j in range(4):
            perm = first if j == 0 else (last if j == 3 else plain)
            tokens = x_ref[8 * r : 8 * r + 8, j].reshape(128, C)
            moved = dot(perm, tokens).astype(BF16).reshape(8, 16, C)
            for p in range(8):
                xs_ref[j, p + 1, 16 * r : 16 * r + 16, :] = moved[p]
    edge = jnp.zeros((8, C), F32)
    for j in range(4):
        lowest = xs_ref[j, 8].astype(F32)
        xs_ref[j, 0] = jnp.concatenate([edge, lowest[:56]], axis=0).astype(BF16)
        highest = xs_ref[j, 1].astype(F32)
        xs_ref[j, 9] = jnp.concatenate([highest[8:], edge], axis=0).astype(BF16)

    gain_one = gain_one_ref[...]

    def conv(g, carry):
        j, p = g // 8, g % 8
        total = xs_ref[j + 1, p + 1].astype(F32)
        for u in range(3):
            for v in range(3):
                total = total + dw_ref[3 * u + v : 3 * u + v + 1, :] * xs_ref[j + v, p + u].astype(F32)
        start = total.astype(BF16)
        rows = pl.ds(pl.multiple_of(g * 64, 64), 64)
        in_ref[rows, :] = start
        normed, _ = norm(start.astype(F32))
        two_s[rows, :] = (normed * gain_one).astype(BF16)
        return carry

    lax.fori_loop(0, 16, conv, 0, unroll=16)

    def project(i, carry):
        rows = pl.ds(pl.multiple_of(i * 256, 256), 256)
        proj_ref[rows, :] = dot(two_s[rows, :], w_qkv_ref[...]).astype(BF16)
        return carry

    lax.fori_loop(0, 4, project, 0)

    mask = mask_ref[...]

    def attend(i, carry):
        units = []
        for n in range(AHEAD):
            pair = i * AHEAD + n
            rows = pl.ds(pl.multiple_of(pair * 128, 128), 128)
            for side in range(2):
                parts = [proj_ref[rows, 256 * m + 128 * side : 256 * m + 128 * side + 128] for m in range(3)]
                units.append((pair, rows, side, parts))
        results = [attend_unit(*parts, mask) for _, _, _, parts in units]
        for (pair, rows, side, _), (probs, mixed) in zip(units, results):
            probs_ref[2 * pair + side] = probs
            mixed_s[rows, 128 * side : 128 * side + 128] = mixed
        return carry

    lax.fori_loop(0, 8 // AHEAD, attend, 0)

    for r in range(4):
        for j in range(2):
            tokens = x_ref[8 * r : 8 * r + 8, 4 + j].reshape(128, C)
            moved = dot(plain, tokens).astype(BF16).reshape(8, 16, C)
            for p in range(8):
                cot_s[(j * 8 + p) * 64 + 16 * r : (j * 8 + p) * 64 + 16 * r + 16, :] = moved[p]

    gain_two = gain_two_ref[...]

    def tail(i, gain_grad):
        rows = pl.ds(pl.multiple_of(i * 512, 512), 512)
        cot = cot_s[rows, :]
        resid = in_ref[rows, :].astype(F32) + dot(mixed_s[rows, :], w_out_ref[...])
        normed, inverse = norm(resid)
        inputs = (normed * gain_two).astype(BF16)
        two_s[rows, :] = inputs
        pre = dot(inputs, w_up_ref[...])
        square = pre * pre
        tangent = jnp.tanh(gelu_coef * (pre + cubic_coef * square * pre))
        half = 0.5 * (1.0 + tangent)
        act_s[rows, :] = (pre * half).astype(BF16)
        slope = half + 0.5 * pre * (1.0 - tangent * tangent) * gelu_coef * (
            1.0 + 3.0 * cubic_coef * square
        )
        pre_grad = (dot_nt(cot, w_down_ref[...]) * slope).astype(BF16)
        pre_s[rows, :] = pre_grad
        in_grad = dot_nt(pre_grad, w_up_ref[...])
        resid_grad = cot.astype(F32) + norm_back(in_grad, normed, inverse, gain_two)
        resid_grad_ref[rows, :] = resid_grad
        low = resid_grad.astype(BF16)
        low_s[rows, :] = low
        mixed_grad_ref[rows, :] = dot_nt(low, w_out_ref[...]).astype(BF16)
        return gain_grad + fold_rows(in_grad * normed)

    gain_grad = lax.fori_loop(0, 2, tail, jnp.zeros((8, C), F32))
    gain_grad_ref[...] = gain_grad

    cot_turned = cot_s[...].T
    two_turned = two_s[...].T
    for block in range(4):
        columns = slice(256 * block, 256 * block + 256)
        down = dot(cot_turned, act_s[:, columns]).T.astype(BF16)
        up = dot(two_turned, pre_s[:, columns]).astype(BF16)
        for half in range(2):
            first = 2048 * half + 256 * block
            sums_ref[first : first + 256, :] = down[:, 128 * half : 128 * half + 128]
            sums_ref[first + 1024 : first + 1280, :] = up[:, 128 * half : 128 * half + 128]
    out_grad_ref[...] = dot(mixed_s[...].T, low_s[...])


def backward_kernel(
    place_ref, in_ref, proj_ref, probs_ref, mixed_grad_ref, resid_grad_ref, gain_one_ref, w_qkv_ref,
    mask_ref, perm_ref,
    pieces_ref, proj_grad_ref, inputs_ref, grad_ref, gain_grad_ref,
):
    owner = place_ref[0]
    mask = mask_ref[...]
    wide_mask = mask.astype(F32)

    def attend_back(i, carry):
        units = []
        for n in range(AHEAD):
            pair = i * AHEAD + n
            rows = pl.ds(pl.multiple_of(pair * 128, 128), 128)
            for side in range(2):
                lanes = slice(128 * side, 128 * side + 128)
                parts = [proj_ref[rows, 256 * m + 128 * side : 256 * m + 128 * side + 128] for m in range(3)]
                parts += [probs_ref[2 * pair + side], mixed_grad_ref[rows, lanes]]
                units.append((pair, rows, side, parts))
        results = [attend_unit_back(*parts, mask, wide_mask) for _, _, _, parts in units]
        for (_, rows, side, _), grads in zip(units, results):
            for m in range(3):
                proj_grad_ref[rows, 256 * m + 128 * side : 256 * m + 128 * side + 128] = grads[m]
        return carry

    lax.fori_loop(0, 8 // AHEAD, attend_back, 0)

    gain_one = gain_one_ref[...]

    def head(i, gain_grad):
        rows = pl.ds(pl.multiple_of(i * 512, 512), 512)
        normed, inverse = norm(in_ref[rows, :].astype(F32))
        inputs_ref[rows, :] = (normed * gain_one).astype(BF16)
        in_grad = dot_nt(proj_grad_ref[rows, :], w_qkv_ref[...])
        grad_ref[rows, :] = resid_grad_ref[rows, :] + norm_back(in_grad, normed, inverse, gain_one)
        return gain_grad + fold_rows(in_grad * normed)

    gain_grad_ref[...] = lax.fori_loop(0, 2, head, jnp.zeros((8, C), F32), unroll=2)

    which = jnp.where(owner == 0, 1.0, 0.0).astype(BF16)
    other = jnp.where(owner == 31, 1.0, 0.0).astype(BF16)
    perm = perm_ref[0] + perm_ref[1] * which + perm_ref[2] * other
    edge = jnp.zeros((8, C), F32)
    for r in range(4):
        parts = [grad_ref[64 * g + 16 * r : 64 * g + 16 * r + 16, :] for g in range(16)]
        for j in range(2):
            lowest = 64 * (8 * j + 7) + 16 * r - 8
            parts.append(grad_ref[lowest : lowest + 8, :] if r > 0 else edge)
        for j in range(2):
            highest = 64 * 8 * j + 16 * r + 16
            parts.append(grad_ref[highest : highest + 8, :] if r < 3 else edge)
        parts.append(jnp.zeros((96, C), F32))
        tokens = jnp.concatenate(parts, axis=0).astype(BF16)
        pieces_ref[r] = dot(perm, tokens).astype(BF16)


def sums_kernel(
    place_ref, xs_ref, inputs_ref, proj_grad_ref, grad_ref, gain_one_grad_ref, gain_two_grad_ref,
    out_grad_ref, tail_ref,
    keep_ref, send_ref,
    head_s, small_s,
):
    core = place_ref[1]

    def taps(g, sums):
        j, p = g // 8, g % 8
        grad = grad_ref[pl.ds(pl.multiple_of(g * 64, 64), 64), :]
        return tuple(
            sums[3 * u + v] + fold_rows(grad * xs_ref[j + v, p + u].astype(F32))
            for u in range(3)
            for v in range(3)
        )

    kernel_grad = lax.fori_loop(0, 16, taps, (jnp.zeros((8, C), F32),) * 9, unroll=4)

    inputs_turned = inputs_ref[...].T
    for block in range(4):
        if block < 3:
            terms = dot(inputs_turned, proj_grad_ref[:, 256 * block : 256 * block + 256])
        else:
            terms = out_grad_ref[...]
        for half in range(2):
            first = 1024 * half + 256 * block
            head_s[first : first + 256, :] = terms[:, 128 * half : 128 * half + 128].astype(BF16)
    small = [jnp.sum(term, axis=0, keepdims=True) for term in kernel_grad]
    small.append(jnp.sum(gain_one_grad_ref[...], axis=0, keepdims=True))
    small.append(jnp.sum(gain_two_grad_ref[...], axis=0, keepdims=True))
    small.append(jnp.zeros((5, C), F32))
    small = jnp.concatenate(small, axis=0)
    for half in range(2):
        small_s[16 * half : 16 * half + 16, :] = small[:, 128 * half : 128 * half + 128]
    zeros = jnp.zeros((8, 128), F32)
    for ref, half in ((keep_ref, core), (send_ref, 1 - core)):
        for k in range(64):
            parts = [
                tail_ref[pl.ds(pl.multiple_of(half * 2048 + 32 * k, 32), 32), :].astype(F32),
                head_s[pl.ds(pl.multiple_of(half * 1024 + 16 * k, 16), 16), :].astype(F32),
                small_s[pl.ds(pl.multiple_of(half * 16 + 8 * k, 8), 8), :] if k < 2 else zeros,
            ]
            ref[k] = jnp.concatenate(parts, axis=0).astype(BF16)


def total_kernel(factor, x_ref, out_ref):
    total = jnp.sum(x_ref[...].astype(F32), axis=0) * factor
    out_ref[...] = jnp.broadcast_to(total.astype(BF16)[None], out_ref.shape)


def tile_kernel(pieces_ref, main_ref, right_ref, left_ref, dw_ref, out_ref, wide):
    for block in range(4):
        columns = dot(main_ref[...], pieces_ref[block])
        wide[:, 8 + 16 * block : 24 + 16 * block, :] = columns.reshape(18, 16, C)
    wide[:, 72:80, :] = dot(right_ref[...], pieces_ref[0]).reshape(18, 8, C)
    wide[:, 0:8, :] = dot(left_ref[...], pieces_ref[3]).reshape(18, 8, C)

    def row(i, carry):
        rows = [wide[i + 2 - u] for u in range(3)]
        total = wide[i + 1, 8:72, :]
        for v in range(3):
            term = dw_ref[v : v + 1, :] * rows[0]
            for u in range(1, 3):
                term = term + dw_ref[3 * u + v : 3 * u + v + 1, :] * rows[u]
            total = total + term[9 - v : 73 - v, :]
        out_ref[0, i] = total
        return carry

    lax.fori_loop(0, 16, row, 0)


def outputs_kernel(
    place_ref, mine_ref, other_ref,
    kernel_ref, gain_one_ref, qkv_ref, out_ref, gain_two_ref, up_ref, down_ref,
):
    own = place_ref[1] == 0
    mine = mine_ref[...].astype(F32)
    other = other_ref[...].astype(F32)
    for half in range(2):
        lanes = slice(128 * half, 128 * half + 128)
        values = jnp.where(own, other, mine) if half else jnp.where(own, mine, other)
        tail = values[:, 0:32].reshape(2048, 128)
        head = values[:, 32:48].reshape(1024, 128)
        small = values[0:2, 48:56].reshape(16, 128)
        down_ref[:, lanes] = tail[0:1024]
        for block in range(4):
            first = 256 * block + 128 * half
            up_ref[:, first : first + 128] = tail[1024 + 256 * block : 1280 + 256 * block]
        for block in range(3):
            first = 256 * block + 128 * half
            qkv_ref[:, first : first + 128] = head[256 * block : 256 * block + 256]
        out_ref[:, lanes] = head[768:1024]
        for u in range(3):
            kernel_ref[u, :, lanes] = small[3 * u : 3 * u + 3]
        gain_one_ref[:, lanes] = small[9:10]
        gain_two_ref[:, lanes] = small[10:11]


VMEM = pl.BlockSpec(memory_space=pltpu.VMEM)
SMEM = pl.BlockSpec(memory_space=pltpu.SMEM)


def call(kernel, outs, operands, scratch=(), scalars=0, flops=0, moved=0, limit=24):
    return pl.pallas_call(
        kernel,
        out_shape=tuple(jax.ShapeDtypeStruct(shape, dtype) for shape, dtype in outs),
        in_specs=[SMEM] * scalars + [VMEM] * (len(operands) - scalars),
        out_specs=tuple(VMEM for _ in outs),
        scratch_shapes=[pltpu.VMEM(shape, dtype) for shape, dtype in scratch],
        compiler_params=pltpu.CompilerParams(vmem_limit_bytes=limit * 2**20),
        cost_estimate=pl.CostEstimate(flops=flops, bytes_accessed=moved, transcendentals=0),
    )(*operands)


def local(input_map, dw_kernel, gain_one, w_qkv, w_out, gain_two, w_up, w_down, cotangent):
    tokens_axes = ("row", "col")
    sums_axes = ("yh", "row", "col")
    owner = lax.axis_index("row") * 8 + lax.axis_index("col")
    core = lax.axis_index("core")
    place = jnp.stack([owner, core]).astype(jnp.int32)
    dw_rows = dw_kernel.reshape(9, C).astype(F32)
    mask = jnp.asarray(head_mask(), BF16)

    def exchange(stacked, axes):
        return lax.all_to_all(stacked, axes, split_axis=0, concat_axis=0, tiled=True)

    def swap(half):
        return lax.ppermute(half, "core", [(0, 1), (1, 0)])

    (packed,) = call(
        pack_kernel,
        [((32, 6, 16, C), BF16)],
        [input_map[0], cotangent[0], jnp.asarray(tile_to_columns(), BF16)],
        flops=4 * 10**8,
        moved=4 * 10**6,
        limit=60,
    )
    arrived = exchange(packed, tokens_axes)

    (
        xs, start, projected, probs, mixed_grad, resid_grad, tail_sums, out_grad, gain_two_grad,
    ) = call(
        forward_kernel,
        [
            ((4, 10, 64, C), BF16),
            ((TOKENS, C), BF16),
            ((TOKENS, 3 * C), BF16),
            ((16, 256, 128), BF16),
            ((TOKENS, C), BF16),
            ((TOKENS, C), F32),
            ((4096, 128), BF16),
            ((C, C), F32),
            ((8, C), F32),
        ],
        [
            place, arrived, jnp.asarray(sources_to_groups(), BF16), dw_rows,
            gain_one.reshape(1, C), w_qkv, w_out, gain_two.reshape(1, C), w_up, w_down, mask,
        ],
        [
            ((TOKENS, C), BF16),
            ((TOKENS, C), BF16),
            ((TOKENS, C), BF16),
            ((TOKENS, C), BF16),
            ((TOKENS, FF), BF16),
            ((TOKENS, FF), BF16),
        ],
        scalars=1,
        flops=8 * 10**9,
        moved=12 * 10**6,
        limit=40,
    )

    pieces, proj_grad, inputs, grad, gain_one_grad = call(
        backward_kernel,
        [
            ((4, 8 * PIECE, C), BF16),
            ((TOKENS, 3 * C), BF16),
            ((TOKENS, C), BF16),
            ((TOKENS, C), F32),
            ((8, C), F32),
        ],
        [
            place, start, projected, probs, mixed_grad, resid_grad, gain_one.reshape(1, C), w_qkv,
            mask, jnp.asarray(groups_to_pieces(), BF16),
        ],
        scalars=1,
        flops=5 * 10**9,
        moved=8 * 10**6,
        limit=32,
    )
    back = exchange(pieces.reshape(32, PIECE, C), tokens_axes).reshape(4, 8 * PIECE, C)

    keep, send = call(
        sums_kernel,
        [((64, 56, 128), BF16), ((64, 56, 128), BF16)],
        [place, xs, inputs, proj_grad, grad, gain_one_grad, gain_two_grad, out_grad, tail_sums],
        [((2048, 128), BF16), ((32, 128), F32)],
        scalars=1,
    )
    half = (keep.astype(F32) + swap(send).astype(F32)).astype(BF16)
    back, half = lax.optimization_barrier((back, half))
    main, right, left = (jnp.asarray(t, BF16) for t in pieces_to_tile())
    (input_grad,) = call(
        tile_kernel,
        [((1, 16, 64, C), F32)],
        [back, main, right, left, dw_rows],
        [((18, 80, C), F32)],
    )
    factor = 1.0 / math.sqrt(TOKENS * 128)
    (shared,) = call(
        lambda x_ref, out_ref: total_kernel(factor, x_ref, out_ref),
        [((64, 56, 128), BF16)],
        [exchange(half, sums_axes)],
        flops=10**6,
        moved=2 * 10**6,
    )
    shared, input_grad = lax.optimization_barrier((shared, input_grad))
    mine = exchange(shared, sums_axes)
    other = swap(mine)

    kernel_grad, gain_one_grad, qkv_grad, out_sum, gain_two_sum, up_grad, down_grad = call(
        outputs_kernel,
        [
            ((3, 3, C), F32),
            ((1, C), F32),
            ((C, 3 * C), F32),
            ((C, C), F32),
            ((1, C), F32),
            ((C, FF), F32),
            ((FF, C), F32),
        ],
        [place, mine, other],
        scalars=1,
        flops=10**6,
        moved=5 * 10**6,
    )
    return (
        input_grad,
        kernel_grad,
        gain_one_grad.reshape(C),
        qkv_grad,
        out_sum,
        gain_two_sum.reshape(C),
        up_grad,
        down_grad,
    )


def solution(mesh):
    cores = Mesh(mesh.devices.reshape(2, 2, 4, 8), ("yh", "core", "row", "col"))
    split = P(("yh", "core"), "row", "col", None)
    in_specs = (split, P(), P(), P(), P(), P(), P(), P(), split)
    out_specs = (split, P(), P(), P(), P(), P(), P(), P())
    return jax.shard_map(local, mesh=cores, in_specs=in_specs, out_specs=out_specs, check_vma=False)
```

time: 205 us -> 134 us (0.65)
  Pallas kernels: 72.8 us -> 34.2 us
  waiting for transfers between devices: 71.8 us -> 52.9 us
  starting transfers between devices: 36.9 us -> 21.7 us
  blocking collectives: 16.5 us -> 20.2 us
  local copies, waits for them, and re-layouts: 3.6 us -> 0.08 us
    pallas_call x8 -> x7, Pallas kernels: 72.8 us -> 34.2 us  [call(): pl.pallas_call(kernel, out_shape=tuple((jax.ShapeDtypeStruct(shape, dtype...]
    all_to_all x6 -> x3, waiting for transfers between devices: 70.5 us -> 50.4 us  [exchange(): lax.all_to_all(stacked, axes, split_axis=0, concat_axis=0, tiled=True)]
    all_to_all x6 -> x3, starting transfers between devices: 35.8 us -> 21.6 us  [exchange(): lax.all_to_all(stacked, axes, split_axis=0, concat_axis=0, tiled=True)]
    all_to_all x1, blocking collectives: 16.5 us -> 20.2 us  [exchange(): lax.all_to_all(stacked, axes, split_axis=0, concat_axis=0, tiled=True)]
    unnamed x40 -> x26, local copies, waits for them, and re-layouts: 2.98 us -> 0.07 us
  transfers between devices with their start and end apart: 10 -> 5, of which waited for: 7 -> 4; matrix products, arithmetic and copies ran while one was open for 1% -> 2% of each run, Pallas kernels for 2% -> 2%
where the time goes in v1:
time: 134 us; the launch traced here: 132 us
  waiting for transfers between devices  52.9 us (39%)
  Pallas kernels  34.2 us (26%)
  starting transfers between devices  21.7 us (16%)
  blocking collectives  20.2 us (15%)
  other arithmetic  2.42 us (2%)
    all_to_all x3, waiting for transfers between devices, exchange(): lax.all_to_all(stacked, axes, split_axis=0, concat_axis=0, tiled=True)  50.4 us
    pallas_call x7, Pallas kernels, call(): pl.pallas_call(kernel, out_shape=tuple((jax.ShapeDtypeStruct(shape, dtype...  34.2 us
    all_to_all x3, starting transfers between devices, exchange(): lax.all_to_all(stacked, axes, split_axis=0, concat_axis=0, tiled=True)  21.6 us
    all_to_all x1, blocking collectives, exchange(): lax.all_to_all(stacked, axes, split_axis=0, concat_axis=0, tiled=True)  20.2 us
  transfers between devices with their start and end apart: 5, of which 4 were waited for; matrix products, arithmetic and copies ran while one was open for 2% of the time, Pallas kernels for 2%

profile of v1, /device:TPU:0, one launch (start us, length us, event | category | flops | bytes accessed | tf_op | source)
XLA Modules:
  0.0 132.4 jit_solution(17070630965923379213)
XLA Ops:
  0.6 2.8 %shard_map.215 = bf16[32,6,16,256]{3,2,1,0:T(8,128)(2,1)} custom-call(bf16[16,64,256]{2,1,0:T(8,128)(2,1)} %bitcast.14, bf16[16,64,256]{2,1,0:T(8,128)(2,1)} %bitcast.15, bf16[256,256]{1,0:T(8,128)(2,1)} %constant.31.clone.perm_ref), custom_call_target="tpu_custom_call" | custom-call | flops 400000000 | bytes 4000000 | tf_op jit(solution)/shard_map/pallas_call | solution.py:457
  3.5 0.0 copy-start.12
  3.5 0.0 copy-start.3
  3.5 0.0 copy-start.4
  3.5 0.0 copy-start.5
  3.5 0.0 copy-start.6
  3.5 0.0 copy-start.7
  3.5 0.0 copy-start.8
  3.5 0.0 copy-start.10
  3.5 0.0 copy-start.11
  3.5 9.4 %all-to-all-start = ((bf16[32,6,16,256]{3,2,1,0:T(8,128)(2,1)}), bf16[32,6,16,256]{3,2,1,0:T(8,128)(2,1)S(1)}, u32[]{:S(2)}, u32[]{:S(2)}) async-start(bf16[32,6,16,256]{3,2,1,0:T(8,128)(2,1)} %shard_map.215), calls=%async_computation | async-start | bytes 3145728 | tf_op jit(solution)/shard_map/all_to_all | solution.py:478
  12.9 0.0 copy-done.12
  13.0 0.1 pad_add_fusion.place_ref
  13.1 22.8 %all-to-all-done.x_ref = bf16[32,6,16,256]{3,2,1,0:T(8,128)(2,1)S(1)} async-done(((bf16[32,6,16,256]{3,2,1,0:T(8,128)(2,1)}), bf16[32,6,16,256]{3,2,1,0:T(8,128)(2,1)S(1)}, u32[]{:S(2)}, u32[]{:S(2)}) %all-to-all-start) | async-done | bytes 1572896 | tf_op jit(solution)/shard_map/all_to_all | solution.py:478
  35.9 0.0 copy-done.3
  35.9 0.0 copy-done.4
  35.9 0.0 copy-done.5
  35.9 0.0 copy-done.6
  35.9 0.0 copy-done.7
  35.9 0.0 copy-done.8
  35.9 0.0 copy-done.10
  35.9 0.0 copy-done.11
  35.9 0.0 copy-start.9
  35.9 14.9 %shard_map.216 = (bf16[4,10,64,256]{3,2,1,0:T(8,128)(2,1)S(1)}, bf16[1024,256]{1,0:T(8,128)(2,1)S(1)}, bf16[1024,768]{1,0:T(8,128)(2,1)S(1)}, bf16[16,256,128]{2...) custom-call(s32[2]{0:T(128)S(1)} %pad_add_fusion.place_ref, ...), custom_call_target="tpu_custom_call" | custom-call | flops 8000000000 | bytes 12000000 | tf_op jit(solution)/shard_map/pallas_call | solution.py:457
  50.8 0.0 copy-done.9
  50.8 9.0 %shard_map.217 = (bf16[4,448,256]{2,1,0:T(8,128)(2,1)}, bf16[1024,768]{1,0:T(8,128)(2,1)S(1)}, bf16[1024,256]{1,0:T(8,128)(2,1)S(1)}, f32[1024,256]{1,0:T(8,128)S(1)}, f32[8,256]{1,0:T(8,128)S(1)}) custom-call(s32[2]{0:T(128)S(1)} %pad_add_fusion.place_ref, bf16[1024,256]{1,0:T(8,128)(2,1)S(1)} %get-tuple-element.35.in_ref, ...), custom_call_target="tpu_custom_call" | custom-call | flops 5000000000 | bytes 8000000 | tf_op jit(solution)/shard_map/pallas_call | solution.py:457
  59.8 2.6 %shard_map.218 = (bf16[64,56,128]{2,1,0:T(8,128)(2,1)S(1)}, bf16[64,56,128]{2,1,0:T(8,128)(2,1)S(1)}) custom-call(s32[2]{0:T(128)S(1)} %pad_add_fusion.place_ref, bf16[4,10,64,256]{3,2,1,0:T(8,128)(2,1)S(1)} %get-tuple-element.41.xs_ref, bf16[1024,256]{1,0:T(8,128)(2,1)S(1)} %get-tuple-element.42.inputs_ref, ...), custom_call_target="tpu_custom_call" | custom-call | tf_op jit(solution)/shard_map/pallas_call | solution.py:457
  62.3 0.1 collective-permute-start
  62.4 5.5 %all-to-all-start.1 = ((bf16[32,56,256]{2,1,0:T(8,128)(2,1)}), bf16[32,56,256]{2,1,0:T(8,128)(2,1)S(1)}, u32[]{:S(2)}, u32[]{:S(2)}) async-start(bf16[32,56,256]{2,1,0:T(8,128)(2,1)} %bitcast.6), calls=%async_computation.1 | async-start | bytes 1835008 | tf_op jit(solution)/shard_map/all_to_all | solution.py:478
  67.9 0.0 collective-permute-done
  68.0 2.3 %add_convert_fusion = bf16[64,56,128]{2,1,0:T(8,128)(2,1)} fusion(bf16[64,56,128]{2,1,0:T(8,128)(2,1)} %collective-permute-done, bf16[64,56,128]{2,1,0:T(8,128)(2,1)S(1)} %get-tuple-element.49), kind=kLoop, calls=%fused_computation | loop fusion | flops 1835008 | bytes 2752512 | tf_op jit(solution)/shard_map/convert_element_type | solution.py:553
  70.3 0.0 copy-start
  70.3 0.0 copy-start.1
  70.3 0.0 copy-start.2
  70.3 14.4 %all-to-all-done.1 = bf16[32,56,256]{2,1,0:T(8,128)(2,1)S(1)} async-done(((bf16[32,56,256]{2,1,0:T(8,128)(2,1)}), bf16[32,56,256]{2,1,0:T(8,128)(2,1)S(1)}, u32[]{:S(2)}, u32[]{:S(2)}) %all-to-all-start.1) | async-done | bytes 917536 | tf_op jit(solution)/shard_map/all_to_all | solution.py:478
  84.7 6.7 %all-to-all-start.2 = ((bf16[64,56,128]{2,1,0:T(8,128)(2,1)}), bf16[64,56,128]{2,1,0:T(8,128)(2,1)S(1)}, u32[]{:S(2)}, u32[]{:S(2)}) async-start(bf16[64,56,128]{2,1,0:T(8,128)(2,1)} %add_convert_fusion), calls=%async_computation.2 | async-start | bytes 1835008 | tf_op jit(solution)/shard_map/all_to_all | solution.py:478
  91.4 0.0 copy-done
  91.5 0.0 copy-done.1
  91.5 0.0 copy-done.2
  91.5 2.4 %shard_map.220 = f32[1,16,64,256]{3,2,1,0:T(8,128)} custom-call(bf16[4,448,256]{2,1,0:T(8,128)(2,1)S(1)} %bitcast.10, bf16[288,448]{1,0:T(8,128)(2,1)S(1)} %copy-done, bf16[144,448]{1,0:T(8,128)(2,1)S(1)} %copy-done.2, bf16[144,448]{1,0:T(8,128)(2,1)S(1)} %copy-done.1, f32[9,256]{1,0:T(8,128)S(1)} %reshape.44.dw_ref), custom_call_target="tpu_custom_call" | custom-call | tf_op jit(solution)/shard_map/pallas_call | solution.py:457
  93.9 13.2 %all-to-all-done.2.x_ref = bf16[64,56,128]{2,1,0:T(8,128)(2,1)S(1)} async-done(((bf16[64,56,128]{2,1,0:T(8,128)(2,1)}), bf16[64,56,128]{2,1,0:T(8,128)(2,1)S(1)}, u32[]{:S(2)}, u32[]{:S(2)}) %all-to-all-start.2) | async-done | bytes 917536 | tf_op jit(solution)/shard_map/all_to_all | solution.py:478
  107.1 0.2 shard_map.219
  107.3 20.2 %all_to_all.20.mine_ref = bf16[64,56,128]{2,1,0:T(8,128)(2,1)S(1)} all-to-all(bf16[64,56,128]{2,1,0:T(8,128)(2,1)S(1)} %shard_map.219), channel_id=1, replica_groups=mesh['yh'=2,'core'=2,'row'=4,'col'=8] {'yh','row','col'}, dimensions={0} | all-to-all | bytes 1835008 | tf_op jit(solution)/shard_map/all_to_all | solution.py:478
  127.6 0.0 collective-permute-start.1
  127.6 2.5 %collective-permute-done.1.other_ref = bf16[64,56,128]{2,1,0:T(8,128)(2,1)S(1)} collective-permute-done((bf16[64,56,128]{2,1,0:T(8,128)(2,1)S(1)}, bf16[64,56,128]{2,1,0:T(8,128)(2,1)S(1)}, u32[]{:S(2)}, u32[]{:S(2)}) %collective-permute-start.1) | collective-permute-done | bytes 917536 | tf_op jit(solution)/shard_map/ppermute | solution.py:481
  130.0 2.4 %shard_map.221 = (f32[3,3,256]{2,1,0:T(4,128)}, f32[1,256]{1,0:T(1,128)}, f32[256,768]{1,0:T(8,128)}, f32[256,256]{1,0:T(8,128)}, f32[1,256]{1,0:T(1,128)}, /*index=5*/f32[256,1024]{1,0:T(8,128)}, f32[1024,256]{1,0:T(8,128)}) custom-call(s32[2]{0:T(128)S(1)} %pad_add_fusion.place_ref, bf16[64,56,128]{2,1,0:T(8,128)(2,1)S(1)} %all_to_all.20.mine_ref, ...), custom_call_target="tpu_custom_call" | custom-call | flops 1000000 | bytes 5000000 | tf_op jit(solution)/shard_map/pallas_call | solution.py:457
  (1 shorter events, 0.0 us)
Async XLA Ops:
  3.5 9.5 %copy-start.12 = (bf16[3,3,256]{2,1,0:T(4,128)(2,1)S(1)}, bf16[3,3,256]{2,1,0:T(4,128)(2,1)}, u32[]{:S(2)}) copy-start(bf16[3,3,256]{2,1,0:T(4,128)(2,1)} %param.17) | copy-start | bytes 13828
  3.5 32.4 %copy-start.3 = (bf16[256,1024]{1,0:T(8,128)(2,1)S(1)}, bf16[256,1024]{1,0:T(8,128)(2,1)}, u32[]{:S(2)}) copy-start(bf16[256,1024]{1,0:T(8,128)(2,1)} %w_up_ref.1) | copy-start | bytes 1572868
  3.5 32.4 %copy-start.4 = (bf16[1024,256]{1,0:T(8,128)(2,1)S(1)}, bf16[1024,256]{1,0:T(8,128)(2,1)}, u32[]{:S(2)}) copy-start(bf16[1024,256]{1,0:T(8,128)(2,1)} %w_down_ref.1) | copy-start | bytes 1572868
  3.5 32.4 %copy-start.5 = (bf16[256,768]{1,0:T(8,128)(2,1)S(1)}, bf16[256,768]{1,0:T(8,128)(2,1)}, u32[]{:S(2)}) copy-start(bf16[256,768]{1,0:T(8,128)(2,1)} %w_qkv_ref.3) | copy-start | bytes 1179652
  3.5 32.4 %copy-start.6 = (bf16[256,256]{1,0:T(8,128)(2,1)S(1)}, bf16[256,256]{1,0:T(8,128)(2,1)}, u32[]{:S(2)}) copy-start(bf16[256,256]{1,0:T(8,128)(2,1)} %w_out_ref.1) | copy-start | bytes 393220
  3.5 32.4 %copy-start.7 = (f32[256]{0:T(256)S(1)}, f32[256]{0:T(256)}, u32[]{:S(2)}) copy-start(f32[256]{0:T(256)} %param.21) | copy-start | bytes 3076
  3.5 32.4 %copy-start.8 = (f32[256]{0:T(256)S(1)}, f32[256]{0:T(256)}, u32[]{:S(2)}) copy-start(f32[256]{0:T(256)} %param.18) | copy-start | bytes 3076
  3.5 32.4 %copy-start.10 = (bf16[256,256]{1,0:T(8,128)(2,1)S(1)}, bf16[256,256]{1,0:T(8,128)(2,1)}, u32[]{:S(2)}) copy-start(bf16[256,256]{1,0:T(8,128)(2,1)} %constant.30.clone.mask_ref) | copy-start | bytes 393220
  3.5 32.4 %copy-start.11 = (bf16[3,128,128]{2,1,0:T(8,128)(2,1)S(1)}, bf16[3,128,128]{2,1,0:T(8,128)(2,1)}, u32[]{:S(2)}) copy-start(bf16[3,128,128]{2,1,0:T(8,128)(2,1)} %constant.32.clone.perm_ref) | copy-start | bytes 294916
  3.5 32.3 %all-to-all-start = ((bf16[32,6,16,256]{3,2,1,0:T(8,128)(2,1)}), bf16[32,6,16,256]{3,2,1,0:T(8,128)(2,1)S(1)}, u32[]{:S(2)}, u32[]{:S(2)}) async-start(bf16[32,6,16,256]{3,2,1,0:T(8,128)(2,1)} %shard_map.215), calls=%async_computation | async-start | bytes 3145728 | tf_op jit(solution)/shard_map/all_to_all | solution.py:478
  35.9 14.9 %copy-start.9 = (bf16[3,448,384]{2,1,0:T(8,128)(2,1)S(1)}, bf16[3,448,384]{2,1,0:T(8,128)(2,1)}, u32[]{:S(2)}) copy-start(bf16[3,448,384]{2,1,0:T(8,128)(2,1)} %constant.33.clone.perm_ref) | copy-start | bytes 3096580
  62.3 5.6 %collective-permute-start = (bf16[64,56,128]{2,1,0:T(8,128)(2,1)S(1)}, bf16[64,56,128]{2,1,0:T(8,128)(2,1)}, u32[]{:S(2)}, u32[]{:S(2)}) collective-permute-start(bf16[64,56,128]{2,1,0:T(8,128)(2,1)S(1)} %get-tuple-element.50), channel_id=1, source_target_pairs={{0,32},{32,0},{1,33},{33,1},{2,34},{34,2},{3,35},{35,3},{4,36},{36... | collective-permute-start | bytes 2752520 | tf_op jit(solution)/shard_map/ppermute | solution.py:481
  62.4 22.3 %all-to-all-start.1 = ((bf16[32,56,256]{2,1,0:T(8,128)(2,1)}), bf16[32,56,256]{2,1,0:T(8,128)(2,1)S(1)}, u32[]{:S(2)}, u32[]{:S(2)}) async-start(bf16[32,56,256]{2,1,0:T(8,128)(2,1)} %bitcast.6), calls=%async_computation.1 | async-start | bytes 1835008 | tf_op jit(solution)/shard_map/all_to_all | solution.py:478
  70.3 21.1 %copy-start = (bf16[288,448]{1,0:T(8,128)(2,1)S(1)}, bf16[288,448]{1,0:T(8,128)(2,1)}, u32[]{:S(2)}) copy-start(bf16[288,448]{1,0:T(8,128)(2,1)} %constant.34.clone.main_ref) | copy-start | bytes 774148
  70.3 21.2 %copy-start.1 = (bf16[144,448]{1,0:T(8,128)(2,1)S(1)}, bf16[144,448]{1,0:T(8,128)(2,1)}, u32[]{:S(2)}) copy-start(bf16[144,448]{1,0:T(8,128)(2,1)} %constant.36.clone.left_ref) | copy-start | bytes 387076
  70.3 21.2 %copy-start.2 = (bf16[144,448]{1,0:T(8,128)(2,1)S(1)}, bf16[144,448]{1,0:T(8,128)(2,1)}, u32[]{:S(2)}) copy-start(bf16[144,448]{1,0:T(8,128)(2,1)} %constant.35.clone.right_ref) | copy-start | bytes 387076
  84.7 22.4 %all-to-all-start.2 = ((bf16[64,56,128]{2,1,0:T(8,128)(2,1)}), bf16[64,56,128]{2,1,0:T(8,128)(2,1)S(1)}, u32[]{:S(2)}, u32[]{:S(2)}) async-start(bf16[64,56,128]{2,1,0:T(8,128)(2,1)} %add_convert_fusion), calls=%async_computation.2 | async-start | bytes 1835008 | tf_op jit(solution)/shard_map/all_to_all | solution.py:478
  127.6 2.5 %collective-permute-start.1 = (bf16[64,56,128]{2,1,0:T(8,128)(2,1)S(1)}, bf16[64,56,128]{2,1,0:T(8,128)(2,1)S(1)}, u32[]{:S(2)}, u32[]{:S(2)}) collective-permute-start(bf16[64,56,128]{2,1,0:T(8,128)(2,1)S(1)} %all_to_all.20.mine_ref), channel_id=1, source_target_pairs={{0,32},{32,0},{1,33},{33,1},{2,34},{34,2},{3,35},{35,3},{4,36},{36... | collective-permute-start | bytes 2752520 | tf_op jit(solution)/shard_map/ppermute | solution.py:481

commit v2 on v1

--- a/solution.py
+++ b/solution.py
@@ -12,7 +12,10 @@
 HEADS = 8
 C = 256
 FF = 1024
-PIECE = 56
+PIECE = 40
+SUMS = 48
+JOINED = PIECE + SUMS
+SHARE = SUMS + 8
 norm_eps = 1e-05
 gelu_coef = 0.7978845608028654
 cubic_coef = 0.044715
@@ -44,37 +47,27 @@
 
 
 def groups_to_pieces():
-    out = np.zeros((3, 8 * PIECE, 384), np.float32)
-
-    def source(j, row, e):
-        if row == 0:
-            return 256 + j * 8 + e
-        if row == 17:
-            return 272 + j * 8 + e
-        a, p = divmod(row - 1, 8)
-        return (j * 8 + p) * 16 + a * 8 + e
-
+    out = np.zeros((8 * PIECE, 384), np.float32)
     for c in range(8):
-        for row in range(18):
-            for slot in range(2):
-                out[0, c * PIECE + slot * 18 + row, source(slot, row, c)] = 1
-            if c + 1 < 8:
-                out[1, c * PIECE + 36 + row, source(0, row, c + 1)] = 1
-            if c - 1 >= 0:
-                out[2, c * PIECE + 36 + row, source(1, row, c - 1)] = 1
+        for j in range(2):
+            out[c * PIECE + 18 * j, 256 + 8 * j + c] = 1
+            out[c * PIECE + 18 * j + 17, 272 + 8 * j + c] = 1
+            for row in range(16):
+                a, p = divmod(row, 8)
+                out[c * PIECE + 18 * j + 1 + row, (j * 8 + p) * 16 + a * 8 + c] = 1
+        out[c * PIECE + 36, 288 + c] = 1
     return out
 
 
 def pieces_to_tile():
     main = np.zeros((288, 8 * PIECE), np.float32)
-    right = np.zeros((144, 8 * PIECE), np.float32)
-    left = np.zeros((144, 8 * PIECE), np.float32)
+    edges = np.zeros((2, 32, 8 * PIECE), np.float32)
     for row in range(18):
         for q in range(16):
             main[row * 16 + q, (q // 2) * PIECE + (q % 2) * 18 + row] = 1
-        right[row * 8, 36 + row] = 1
-        left[row * 8 + 7, 7 * PIECE + 36 + row] = 1
-    return main, right, left
+        edges[0, row, row] = 1
+        edges[1, row, 7 * PIECE + 18 + row] = 1
+    return main, edges
 
 
 def head_mask():
@@ -287,19 +280,15 @@
         columns = slice(256 * block, 256 * block + 256)
         down = dot(cot_turned, act_s[:, columns]).T.astype(BF16)
         up = dot(two_turned, pre_s[:, columns]).astype(BF16)
-        for half in range(2):
-            first = 2048 * half + 256 * block
-            sums_ref[first : first + 256, :] = down[:, 128 * half : 128 * half + 128]
-            sums_ref[first + 1024 : first + 1280, :] = up[:, 128 * half : 128 * half + 128]
+        sums_ref[256 * block : 256 * block + 256, :] = down
+        sums_ref[1024 + 256 * block : 1280 + 256 * block, :] = up
     out_grad_ref[...] = dot(mixed_s[...].T, low_s[...])
 
 
 def backward_kernel(
-    place_ref, in_ref, proj_ref, probs_ref, mixed_grad_ref, resid_grad_ref, gain_one_ref, w_qkv_ref,
-    mask_ref, perm_ref,
-    pieces_ref, proj_grad_ref, inputs_ref, grad_ref, gain_grad_ref,
+    in_ref, proj_ref, probs_ref, mixed_grad_ref, resid_grad_ref, gain_one_ref, w_qkv_ref, mask_ref,
+    proj_grad_ref, inputs_ref, grad_ref, gain_grad_ref,
 ):
-    owner = place_ref[0]
     mask = mask_ref[...]
     wide_mask = mask.astype(F32)
 
@@ -333,10 +322,51 @@
 
     gain_grad_ref[...] = lax.fori_loop(0, 2, head, jnp.zeros((8, C), F32), unroll=2)
 
-    which = jnp.where(owner == 0, 1.0, 0.0).astype(BF16)
-    other = jnp.where(owner == 31, 1.0, 0.0).astype(BF16)
-    perm = perm_ref[0] + perm_ref[1] * which + perm_ref[2] * other
+
+def sums_kernel(
+    place_ref, xs_ref, inputs_ref, proj_grad_ref, grad_ref, gain_one_grad_ref, gain_two_grad_ref,
+    out_grad_ref, tail_ref,
+    keep_ref, send_ref,
+    head_s, small_s,
+):
+    core = place_ref[1]
+
+    def taps(g, sums):
+        j, p = g // 8, g % 8
+        grad = grad_ref[pl.ds(pl.multiple_of(g * 64, 64), 64), :]
+        return tuple(
+            sums[3 * u + v] + fold_rows(grad * xs_ref[j + v, p + u].astype(F32))
+            for u in range(3)
+            for v in range(3)
+        )
+
+    kernel_grad = lax.fori_loop(0, 16, taps, (jnp.zeros((8, C), F32),) * 9, unroll=4)
+
+    inputs_turned = inputs_ref[...].T
+    for block in range(3):
+        terms = dot(inputs_turned, proj_grad_ref[:, 256 * block : 256 * block + 256])
+        head_s[256 * block : 256 * block + 256, :] = terms.astype(BF16)
+    head_s[768:1024, :] = out_grad_ref[...].astype(BF16)
+    small = [jnp.sum(term, axis=0, keepdims=True) for term in kernel_grad]
+    small.append(jnp.sum(gain_one_grad_ref[...], axis=0, keepdims=True))
+    small.append(jnp.sum(gain_two_grad_ref[...], axis=0, keepdims=True))
+    small.append(jnp.zeros((5, C), F32))
+    small_s[...] = jnp.concatenate(small, axis=0)
+    for ref, half in ((keep_ref, core), (send_ref, 1 - core)):
+        for k in range(32):
+            tail = pl.ds(pl.multiple_of(half * 1024 + 32 * k, 32), 32)
+            head = pl.ds(pl.multiple_of(half * 512 + 16 * k, 16), 16)
+            ref[k, 0:32, :] = tail_ref[tail, :]
+            ref[k, 32:48, :] = head_s[head, :]
+        rows = small_s[pl.ds(pl.multiple_of(half * 8, 8), 8), :]
+        ref[32, 0:16, :] = jnp.concatenate([rows, rows], axis=0).astype(BF16)
+        ref[32, 16:48, :] = jnp.zeros((32, C), BF16)
+
+
+def pieces_kernel(grad_ref, keep_ref, swapped_ref, perm_ref, out_ref):
+    perm = perm_ref[...]
     edge = jnp.zeros((8, C), F32)
+    small = keep_ref[32, 0:16, :].astype(F32) + swapped_ref[32, 0:16, :].astype(F32)
     for r in range(4):
         parts = [grad_ref[64 * g + 16 * r : 64 * g + 16 * r + 16, :] for g in range(16)]
         for j in range(2):
@@ -345,68 +375,50 @@
         for j in range(2):
             highest = 64 * 8 * j + 16 * r + 16
             parts.append(grad_ref[highest : highest + 8, :] if r < 3 else edge)
-        parts.append(jnp.zeros((96, C), F32))
+        parts.append(small[0:8] if r == 0 else edge)
+        parts.append(jnp.zeros((88, C), F32))
         tokens = jnp.concatenate(parts, axis=0).astype(BF16)
-        pieces_ref[r] = dot(perm, tokens).astype(BF16)
-
-
-def sums_kernel(
-    place_ref, xs_ref, inputs_ref, proj_grad_ref, grad_ref, gain_one_grad_ref, gain_two_grad_ref,
-    out_grad_ref, tail_ref,
-    keep_ref, send_ref,
-    head_s, small_s,
-):
-    core = place_ref[1]
-
-    def taps(g, sums):
-        j, p = g // 8, g % 8
-        grad = grad_ref[pl.ds(pl.multiple_of(g * 64, 64), 64), :]
-        return tuple(
-            sums[3 * u + v] + fold_rows(grad * xs_ref[j + v, p + u].astype(F32))
-            for u in range(3)
-            for v in range(3)
-        )
-
-    kernel_grad = lax.fori_loop(0, 16, taps, (jnp.zeros((8, C), F32),) * 9, unroll=4)
-
-    inputs_turned = inputs_ref[...].T
+        moved = dot(perm, tokens).reshape(8, PIECE, C)
+        pieces = slice(8 * r, 8 * r + 8)
+        sums = keep_ref[pieces].astype(F32) + swapped_ref[pieces].astype(F32)
+        joined = jnp.concatenate([moved, sums], axis=1)
+        out_ref[r] = joined.reshape(8 * JOINED, C).astype(BF16)
+
+
+def partial_kernel(factor, x_ref, out_ref):
+    total = jnp.zeros((SHARE, C), F32)
+    for r in range(4):
+        pieces = jnp.sum(x_ref[r].astype(F32).reshape(8, JOINED, C), axis=0)
+        total = total + jnp.concatenate([pieces[PIECE:], pieces[32:40]], axis=0)
+    out_ref[...] = total * factor
+
+
+def total_kernel(mine_ref, other_ref, out_ref):
+    total = mine_ref[...] + other_ref[...]
+    rows = jnp.concatenate([total] * 8, axis=0).astype(BF16)
+    for r in range(4):
+        out_ref[r] = rows
+
+
+def unpack_kernel(pieces_ref, main_ref, edges_ref, tile_ref, first_ref, last_ref):
     for block in range(4):
-        if block < 3:
-            terms = dot(inputs_turned, proj_grad_ref[:, 256 * block : 256 * block + 256])
-        else:
-            terms = out_grad_ref[...]
-        for half in range(2):
-            first = 1024 * half + 256 * block
-            head_s[first : first + 256, :] = terms[:, 128 * half : 128 * half + 128].astype(BF16)
-    small = [jnp.sum(term, axis=0, keepdims=True) for term in kernel_grad]
-    small.append(jnp.sum(gain_one_grad_ref[...], axis=0, keepdims=True))
-    small.append(jnp.sum(gain_two_grad_ref[...], axis=0, keepdims=True))
-    small.append(jnp.zeros((5, C), F32))
-    small = jnp.concatenate(small, axis=0)
-    for half in range(2):
-        small_s[16 * half : 16 * half + 16, :] = small[:, 128 * half : 128 * half + 128]
-    zeros = jnp.zeros((8, 128), F32)
-    for ref, half in ((keep_ref, core), (send_ref, 1 - core)):
-        for k in range(64):
-            parts = [
-                tail_ref[pl.ds(pl.multiple_of(half * 2048 + 32 * k, 32), 32), :].astype(F32),
-                head_s[pl.ds(pl.multiple_of(half * 1024 + 16 * k, 16), 16), :].astype(F32),
-                small_s[pl.ds(pl.multiple_of(half * 16 + 8 * k, 8), 8), :] if k < 2 else zeros,
-            ]
-            ref[k] = jnp.concatenate(parts, axis=0).astype(BF16)
-
-
-def total_kernel(factor, x_ref, out_ref):
-    total = jnp.sum(x_ref[...].astype(F32), axis=0) * factor
-    out_ref[...] = jnp.broadcast_to(total.astype(BF16)[None], out_ref.shape)
-
-
-def tile_kernel(pieces_ref, main_ref, right_ref, left_ref, dw_ref, out_ref, wide):
-    for block in range(4):
-        columns = dot(main_ref[...], pieces_ref[block])
-        wide[:, 8 + 16 * block : 24 + 16 * block, :] = columns.reshape(18, 16, C)
-    wide[:, 72:80, :] = dot(right_ref[...], pieces_ref[0]).reshape(18, 8, C)
-    wide[:, 0:8, :] = dot(left_ref[...], pieces_ref[3]).reshape(18, 8, C)
+        pieces = pieces_ref[block].astype(F32).reshape(8, JOINED, C)
+        pieces = pieces[:, :PIECE].reshape(8 * PIECE, C).astype(BF16)
+        columns = dot(main_ref[...], pieces).astype(BF16)
+        tile_ref[:, 16 * block : 16 * block + 16, :] = columns.reshape(18, 16, C)
+        if block == 0:
+            first_ref[...] = dot(edges_ref[0], pieces).astype(BF16)
+        if block == 3:
+            last_ref[...] = dot(edges_ref[1], pieces).astype(BF16)
+
+
+def tile_kernel(tile_ref, left_ref, right_ref, dw_ref, out_ref, wide):
+    wide[:, 8:72, :] = tile_ref[...].astype(F32)
+    left = left_ref[...].astype(F32)
+    right = right_ref[...].astype(F32)
+    for i in range(18):
+        wide[i, 7:8, :] = left[i : i + 1]
+        wide[i, 72:73, :] = right[i : i + 1]
 
     def row(i, carry):
         rows = [wide[i + 2 - u] for u in range(3)]
@@ -427,26 +439,27 @@
     kernel_ref, gain_one_ref, qkv_ref, out_ref, gain_two_ref, up_ref, down_ref,
 ):
     own = place_ref[1] == 0
-    mine = mine_ref[...].astype(F32)
-    other = other_ref[...].astype(F32)
-    for half in range(2):
-        lanes = slice(128 * half, 128 * half + 128)
-        values = jnp.where(own, other, mine) if half else jnp.where(own, mine, other)
-        tail = values[:, 0:32].reshape(2048, 128)
-        head = values[:, 32:48].reshape(1024, 128)
-        small = values[0:2, 48:56].reshape(16, 128)
-        down_ref[:, lanes] = tail[0:1024]
-        for block in range(4):
-            first = 256 * block + 128 * half
-            up_ref[:, first : first + 128] = tail[1024 + 256 * block : 1280 + 256 * block]
-        for block in range(3):
-            first = 256 * block + 128 * half
-            qkv_ref[:, first : first + 128] = head[256 * block : 256 * block + 256]
-        out_ref[:, lanes] = head[768:1024]
-        for u in range(3):
-            kernel_ref[u, :, lanes] = small[3 * u : 3 * u + 3]
-        gain_one_ref[:, lanes] = small[9:10]
-        gain_two_ref[:, lanes] = small[10:11]
+    for r in range(4):
+        mine = mine_ref[r].astype(F32).reshape(8, SHARE, C)
+        other = other_ref[r].astype(F32).reshape(8, SHARE, C)
+        lower = jnp.where(own, mine, other)
+        upper = jnp.where(own, other, mine)
+        down_ref[256 * r : 256 * r + 256, :] = lower[:, 0:32].reshape(256, C)
+        up_ref[:, 256 * r : 256 * r + 256] = upper[:, 0:32].reshape(256, C)
+        rows = slice(128 * (r % 2), 128 * (r % 2) + 128)
+        block = r // 2
+        qkv_ref[rows, 256 * block : 256 * block + 256] = lower[:, 32:48].reshape(128, C)
+        if r < 2:
+            qkv_ref[rows, 512:768] = upper[:, 32:48].reshape(128, C)
+        else:
+            out_ref[rows, :] = upper[:, 32:48].reshape(128, C)
+        if r == 0:
+            small = [side[c, 52:53] for side in (lower, upper) for c in range(8)]
+            small = jnp.concatenate(small, axis=0)
+            for u in range(3):
+                kernel_ref[u] = small[3 * u : 3 * u + 3]
+            gain_one_ref[...] = small[9:10]
+            gain_two_ref[...] = small[10:11]
 
 
 VMEM = pl.BlockSpec(memory_space=pltpu.VMEM)
@@ -466,19 +479,22 @@
 
 
 def local(input_map, dw_kernel, gain_one, w_qkv, w_out, gain_two, w_up, w_down, cotangent):
-    tokens_axes = ("row", "col")
-    sums_axes = ("yh", "row", "col")
     owner = lax.axis_index("row") * 8 + lax.axis_index("col")
     core = lax.axis_index("core")
     place = jnp.stack([owner, core]).astype(jnp.int32)
     dw_rows = dw_kernel.reshape(9, C).astype(F32)
     mask = jnp.asarray(head_mask(), BF16)
 
-    def exchange(stacked, axes):
-        return lax.all_to_all(stacked, axes, split_axis=0, concat_axis=0, tiled=True)
-
-    def swap(half):
-        return lax.ppermute(half, "core", [(0, 1), (1, 0)])
+    def exchange(stacked):
+        return lax.all_to_all(stacked, ("row", "col"), split_axis=0, concat_axis=0, tiled=True)
+
+    def swap(values, axis):
+        return lax.ppermute(values, axis, [(0, 1), (1, 0)])
+
+    def shift(values, axis, step):
+        size = lax.axis_size(axis)
+        pairs = [(i, i + step) for i in range(size) if 0 <= i + step < size]
+        return lax.ppermute(values, axis, pairs)
 
     (packed,) = call(
         pack_kernel,
@@ -488,7 +504,7 @@
         moved=4 * 10**6,
         limit=60,
     )
-    arrived = exchange(packed, tokens_axes)
+    arrived = exchange(packed)
 
     (
         xs, start, projected, probs, mixed_grad, resid_grad, tail_sums, out_grad, gain_two_grad,
@@ -501,7 +517,7 @@
             ((16, 256, 128), BF16),
             ((TOKENS, C), BF16),
             ((TOKENS, C), F32),
-            ((4096, 128), BF16),
+            ((2048, C), BF16),
             ((C, C), F32),
             ((8, C), F32),
         ],
@@ -523,54 +539,54 @@
         limit=40,
     )
 
-    pieces, proj_grad, inputs, grad, gain_one_grad = call(
+    proj_grad, inputs, grad, gain_one_grad = call(
         backward_kernel,
-        [
-            ((4, 8 * PIECE, C), BF16),
-            ((TOKENS, 3 * C), BF16),
-            ((TOKENS, C), BF16),
-            ((TOKENS, C), F32),
-            ((8, C), F32),
-        ],
-        [
-            place, start, projected, probs, mixed_grad, resid_grad, gain_one.reshape(1, C), w_qkv,
-            mask, jnp.asarray(groups_to_pieces(), BF16),
-        ],
-        scalars=1,
+        [((TOKENS, 3 * C), BF16), ((TOKENS, C), BF16), ((TOKENS, C), F32), ((8, C), F32)],
+        [start, projected, probs, mixed_grad, resid_grad, gain_one.reshape(1, C), w_qkv, mask],
         flops=5 * 10**9,
         moved=8 * 10**6,
         limit=32,
     )
-    back = exchange(pieces.reshape(32, PIECE, C), tokens_axes).reshape(4, 8 * PIECE, C)
-
     keep, send = call(
         sums_kernel,
-        [((64, 56, 128), BF16), ((64, 56, 128), BF16)],
+        [((33, SUMS, C), BF16), ((33, SUMS, C), BF16)],
         [place, xs, inputs, proj_grad, grad, gain_one_grad, gain_two_grad, out_grad, tail_sums],
-        [((2048, 128), BF16), ((32, 128), F32)],
+        [((1024, C), BF16), ((16, C), F32)],
         scalars=1,
     )
-    half = (keep.astype(F32) + swap(send).astype(F32)).astype(BF16)
-    back, half = lax.optimization_barrier((back, half))
-    main, right, left = (jnp.asarray(t, BF16) for t in pieces_to_tile())
+    (pieces,) = call(
+        pieces_kernel,
+        [((4, 8 * JOINED, C), BF16)],
+        [grad, keep, swap(send, "core"), jnp.asarray(groups_to_pieces(), BF16)],
+    )
+    back = exchange(pieces.reshape(32, JOINED, C)).reshape(4, 8 * JOINED, C)
+    factor = 1.0 / math.sqrt(TOKENS * 128)
+    (partial,) = call(
+        lambda x_ref, out_ref: partial_kernel(factor, x_ref, out_ref),
+        [((SHARE, C), F32)],
+        [back],
+    )
+    main, edges = (jnp.asarray(t, BF16) for t in pieces_to_tile())
+    tile, first, last = call(
+        unpack_kernel,
+        [((18, 64, C), BF16), ((32, C), BF16), ((32, C), BF16)],
+        [back, main, edges],
+    )
+    left, right = shift(last, "col", 1), shift(first, "col", -1)
+    (shared,) = call(
+        total_kernel,
+        [((4, 8 * SHARE, C), BF16)],
+        [partial, swap(partial, "yh")],
+    )
+    mine = exchange(shared.reshape(32, SHARE, C)).reshape(4, 8 * SHARE, C)
     (input_grad,) = call(
         tile_kernel,
         [((1, 16, 64, C), F32)],
-        [back, main, right, left, dw_rows],
+        [tile, left, right, dw_rows],
         [((18, 80, C), F32)],
     )
-    factor = 1.0 / math.sqrt(TOKENS * 128)
-    (shared,) = call(
-        lambda x_ref, out_ref: total_kernel(factor, x_ref, out_ref),
-        [((64, 56, 128), BF16)],
-        [exchange(half, sums_axes)],
-        flops=10**6,
-        moved=2 * 10**6,
-    )
-    shared, input_grad = lax.optimization_barrier((shared, input_grad))
-    mine = exchange(shared, sums_axes)
-    other = swap(mine)
-
+    mine, input_grad = lax.optimization_barrier((mine, input_grad))
+    other = swap(mine, "core")
     kernel_grad, gain_one_grad, qkv_grad, out_sum, gain_two_sum, up_grad, down_grad = call(
         outputs_kernel,
         [

time: 134 us -> 123 us (0.918)
  waiting for transfers between devices: 52.9 us -> 37.5 us
  blocking collectives: 20.2 us -> 27.5 us
  other arithmetic: 2.42 us -> 0.08 us
    all_to_all x3 -> x2, waiting for transfers between devices: 50.4 us -> 24 us  [exchange(): lax.all_to_all(stacked, ('row', 'col'), split_axis=0, concat_axis=0, tile...]
    ppermute x2 -> x5, waiting for transfers between devices: 2.47 us -> 13.4 us  [the longest x3 7.56 us: swap(): return lax.ppermute(values, axis, [(0, 1), (1, 0)])]
    all_to_all x3 -> x2, starting transfers between devices: 21.6 us -> 13.3 us  [exchange(): lax.all_to_all(stacked, ('row', 'col'), split_axis=0, concat_axis=0, tile...]
    ppermute x2 -> x5, starting transfers between devices: 0.09 us -> 8.2 us  [the longest x2 4.95 us: shift(): return lax.ppermute(values, axis, pairs)]
    all_to_all x1, blocking collectives: 20.2 us -> 27.5 us  [exchange(): lax.all_to_all(stacked, ('row', 'col'), split_axis=0, concat_axis=0, tile...]
    convert_element_type x1 -> x0, other arithmetic: 2.34 us -> none  [local(): half = (keep.astype(F32) + swap(send).astype(F32)).astype(BF16)]
    pallas_call x7 -> x10, Pallas kernels: 34.2 us -> 33.6 us  [call(): pl.pallas_call(kernel, out_shape=tuple((jax.ShapeDtypeStruct(shape, dtype...]
  transfers between devices with their start and end apart: 5 -> 7, of which waited for: 4 -> 7; matrix products, arithmetic and copies ran while one was open for 2% -> 0% of each run, Pallas kernels for 2% -> 2%
where the time goes in v2:
time: 123 us; the launch traced here: 121 us
  waiting for transfers between devices  37.5 us (30%)
  Pallas kernels  33.6 us (27%)
  blocking collectives  27.5 us (22%)
  starting transfers between devices  21.5 us (17%)
    pallas_call x10, Pallas kernels, call(): pl.pallas_call(kernel, out_shape=tuple((jax.ShapeDtypeStruct(shape, dtype...  33.6 us
    all_to_all x1, blocking collectives, exchange(): lax.all_to_all(stacked, ('row', 'col'), split_axis=0, concat_axis=0, tile...  27.5 us
    all_to_all x2, waiting for transfers between devices, exchange(): lax.all_to_all(stacked, ('row', 'col'), split_axis=0, concat_axis=0, tile...  24 us
    all_to_all x2, starting transfers between devices, exchange(): lax.all_to_all(stacked, ('row', 'col'), split_axis=0, concat_axis=0, tile...  13.3 us
    ppermute x3, waiting for transfers between devices, swap(): return lax.ppermute(values, axis, [(0, 1), (1, 0)])  7.56 us
    ppermute x2, waiting for transfers between devices, shift(): return lax.ppermute(values, axis, pairs)  5.86 us
    ppermute x2, starting transfers between devices, shift(): return lax.ppermute(values, axis, pairs)  4.95 us
    ppermute x3, starting transfers between devices, swap(): return lax.ppermute(values, axis, [(0, 1), (1, 0)])  3.25 us
  transfers between devices with their start and end apart: 7, of which 7 were waited for; matrix products, arithmetic and copies ran while one was open for 0% of the time, Pallas kernels for 2%

profile of v2, /device:TPU:0, one launch (start us, length us, event | category | flops | bytes accessed | tf_op | source)
XLA Modules:
  0.0 121.1 jit_solution(12944803707921415261)
XLA Ops:
  0.6 2.8 %shard_map.206 = bf16[32,6,16,256]{3,2,1,0:T(8,128)(2,1)} custom-call(bf16[16,64,256]{2,1,0:T(8,128)(2,1)} %bitcast.20, bf16[16,64,256]{2,1,0:T(8,128)(2,1)} %bitcast.21, bf16[256,256]{1,0:T(8,128)(2,1)} %constant.29.clone.perm_ref), custom_call_target="tpu_custom_call" | custom-call | flops 400000000 | bytes 4000000 | tf_op jit(solution)/shard_map/pallas_call | solution.py:470
  3.5 0.0 copy-start.11
  3.5 0.0 copy-start.3
  3.5 0.0 copy-start.6
  3.5 0.0 copy-start.7
  3.5 0.0 copy-start.8
  3.5 0.0 copy-start.9
  3.5 0.0 copy-start.10
  3.5 9.4 %all-to-all-start = ((bf16[32,6,16,256]{3,2,1,0:T(8,128)(2,1)}), bf16[32,6,16,256]{3,2,1,0:T(8,128)(2,1)S(1)}, u32[]{:S(2)}, u32[]{:S(2)}) async-start(bf16[32,6,16,256]{3,2,1,0:T(8,128)(2,1)} %shard_map.206), calls=%async_computation | async-start | bytes 3145728 | tf_op jit(solution)/shard_map/all_to_all | solution.py:489
  13.0 0.0 copy-done.11
  13.0 0.1 pad_add_fusion.place_ref
  13.1 22.8 %all-to-all-done.x_ref = bf16[32,6,16,256]{3,2,1,0:T(8,128)(2,1)S(1)} async-done(((bf16[32,6,16,256]{3,2,1,0:T(8,128)(2,1)}), bf16[32,6,16,256]{3,2,1,0:T(8,128)(2,1)S(1)}, u32[]{:S(2)}, u32[]{:S(2)}) %all-to-all-start) | async-done | bytes 1572896 | tf_op jit(solution)/shard_map/all_to_all | solution.py:489
  35.9 0.0 copy-done.3
  35.9 0.0 copy-done.4
  35.9 0.0 copy-done.5
  35.9 0.0 copy-done.6
  35.9 0.0 copy-done.7
  35.9 0.0 copy-done.8
  35.9 0.0 copy-done.9
  35.9 0.0 copy-done.10
  35.9 14.9 %shard_map.207 = (bf16[4,10,64,256]{3,2,1,0:T(8,128)(2,1)S(1)}, bf16[1024,256]{1,0:T(8,128)(2,1)S(1)}, bf16[1024,768]{1,0:T(8,128)(2,1)S(1)}, bf16[16,256,128]{2...) custom-call(s32[2]{0:T(128)S(1)} %pad_add_fusion.place_ref, ...), custom_call_target="tpu_custom_call" | custom-call | flops 8000000000 | bytes 12000000 | tf_op jit(solution)/shard_map/pallas_call | solution.py:470
  50.8 6.8 %shard_map.208 = (bf16[1024,768]{1,0:T(8,128)(2,1)S(1)}, bf16[1024,256]{1,0:T(8,128)(2,1)S(1)}, f32[1024,256]{1,0:T(8,128)S(1)}, f32[8,256]{1,0:T(8,128)S(1)}) custom-call(bf16[1024,256]{1,0:T(8,128)(2,1)S(1)} %get-tuple-element.35.in_ref, bf16[1024,768]{1,0:T(8,128)(2,1)S(1)} %get-tuple-element.36.proj_ref, ...), custom_call_target="tpu_custom_call" | custom-call | flops 5000000000 | bytes 8000000 | tf_op jit(solution)/shard_map/pallas_call | solution.py:470
  57.6 0.0 copy-start
  57.6 2.3 %shard_map.209 = (bf16[33,48,256]{2,1,0:T(8,128)(2,1)S(1)}, bf16[33,48,256]{2,1,0:T(8,128)(2,1)S(1)}) custom-call(s32[2]{0:T(128)S(1)} %pad_add_fusion.place_ref, bf16[4,10,64,256]{3,2,1,0:T(8,128)(2,1)S(1)} %get-tuple-element.41.xs_ref, bf16[1024,256]{1,0:T(8,128)(2,1)S(1)} %get-tuple-element.42.inputs_ref, ...), custom_call_target="tpu_custom_call" | custom-call | tf_op jit(solution)/shard_map/pallas_call | solution.py:470
  59.9 0.3 collective-permute-start
  60.2 2.3 %collective-permute-done.swapped_ref = bf16[33,48,256]{2,1,0:T(8,128)(2,1)S(1)} collective-permute-done((bf16[33,48,256]{2,1,0:T(8,128)(2,1)S(1)}, bf16[33,48,256]{2,1,0:T(8,128)(2,1)S(1)}, u32[]{:S(2)}, u32[]{:S(2)}) %collective-permute-start) | collective-permute-done | bytes 811040 | tf_op jit(solution)/shard_map/ppermute | solution.py:492
  62.5 0.0 copy-done
  62.5 0.8 shard_map.210
  63.3 27.5 %all_to_all.15 = bf16[32,88,256]{2,1,0:T(8,128)(2,1)S(1)} all-to-all(bf16[32,88,256]{2,1,0:T(8,128)(2,1)S(1)} %bitcast.14), channel_id=1, replica_groups=mesh['yh'=2,'core'=2,'row'=4,'col'=8] {'row','col'}, dimensions={0} | all-to-all | bytes 2883584 | tf_op jit(solution)/shard_map/all_to_all | solution.py:489
  90.8 0.1 shard_map.211.mine_ref
  90.9 0.0 copy-start.1
  90.9 0.0 copy-start.2
  90.9 3.0 %collective-permute-start.1 = (f32[56,256]{1,0:T(8,128)S(1)}, f32[56,256]{1,0:T(8,128)S(1)}, u32[]{:S(2)}, u32[]{:S(2)}) collective-permute-start(f32[56,256]{1,0:T(8,128)S(1)} %shard_map.211.mine_ref), channel_id=1, source_target_pairs={{0,64},{64,0},{1,65},{65,1},{2,66},{66,2},{3,67},{67,3},{4,68},{68... | collective-permute-start | bytes 172040 | tf_op jit(solution)/shard_map/ppermute | solution.py:492
  93.9 2.8 %collective-permute-done.1.other_ref = f32[56,256]{1,0:T(8,128)S(1)} collective-permute-done((f32[56,256]{1,0:T(8,128)S(1)}, f32[56,256]{1,0:T(8,128)S(1)}, u32[]{:S(2)}, u32[]{:S(2)}) %collective-permute-start.1) | collective-permute-done | bytes 57376 | tf_op jit(solution)/shard_map/ppermute | solution.py:492
  96.7 1.0 shard_map.212
  97.7 3.9 %all-to-all-start.2 = ((bf16[32,56,256]{2,1,0:T(8,128)(2,1)}), bf16[32,56,256]{2,1,0:T(8,128)(2,1)S(1)}, u32[]{:S(2)}, u32[]{:S(2)}) async-start(bf16[32,56,256]{2,1,0:T(8,128)(2,1)} %bitcast.8), calls=%async_computation.2 | async-start | bytes 1835008 | tf_op jit(solution)/shard_map/all_to_all | solution.py:489
  101.6 0.0 copy-done.1
  101.6 0.0 copy-done.2
  101.6 0.5 shard_map.213
  102.1 3.7 %collective-permute-start.2 = (bf16[32,256]{1,0:T(8,128)(2,1)S(1)}, bf16[32,256]{1,0:T(8,128)(2,1)S(1)}, u32[]{:S(2)}, u32[]{:S(2)}) collective-permute-start(bf16[32,256]{1,0:T(8,128)(2,1)S(1)} %get-tuple-element.51), channel_id=1, source_target_pairs={{0,1},{1,2},{2,3},{3,4},{4,5},{5,6},{6,7},{8,9},{9,10},{10,11},{11... | collective-permute-start | bytes 49160 | tf_op jit(solution)/shard_map/ppermute | solution.py:497
  105.8 1.3 %collective-permute-start.3 = (bf16[32,256]{1,0:T(8,128)(2,1)S(1)}, bf16[32,256]{1,0:T(8,128)(2,1)S(1)}, u32[]{:S(2)}, u32[]{:S(2)}) collective-permute-start(bf16[32,256]{1,0:T(8,128)(2,1)S(1)} %get-tuple-element.52), channel_id=1, source_target_pairs={{1,0},{2,1},{3,2},{4,3},{5,4},{6,5},{7,6},{9,8},{10,9},{11,10},{12... | collective-permute-start | bytes 49160 | tf_op jit(solution)/shard_map/ppermute | solution.py:497
  107.1 1.2 collective-permute-done.2.left_ref
  108.3 4.7 %collective-permute-done.3.right_ref = bf16[32,256]{1,0:T(8,128)(2,1)S(1)} collective-permute-done((bf16[32,256]{1,0:T(8,128)(2,1)S(1)}, bf16[32,256]{1,0:T(8,128)(2,1)S(1)}, u32[]{:S(2)}, u32[]{:S(2)}) %collective-permute-start.3) | collective-permute-done | bytes 16416 | tf_op jit(solution)/shard_map/ppermute | solution.py:497
  113.0 2.0 %shard_map.214 = f32[1,16,64,256]{3,2,1,0:T(8,128)} custom-call(bf16[18,64,256]{2,1,0:T(8,128)(2,1)S(1)} %get-tuple-element.50.tile_ref, bf16[32,256]{1,0:T(8,128)(2,1)S(1)} %collective-permute-done.2.left_ref, bf16[32,256]{1,0:T(8,128)(2,1)S(1)} %collective-permute-done.3.right_ref, f32[9,256]{1,0:T(8,128)S(1)} %reshape.52.dw_ref), custom_call_target="tpu_custom_call" | custom-call | tf_op jit(solution)/shard_map/pallas_call | solution.py:470
  114.9 1.2 %all-to-all-done.2 = bf16[32,56,256]{2,1,0:T(8,128)(2,1)S(1)} async-done(((bf16[32,56,256]{2,1,0:T(8,128)(2,1)}), bf16[32,56,256]{2,1,0:T(8,128)(2,1)S(1)}, u32[]{:S(2)}, u32[]{:S(2)}) %all-to-all-start.2) | async-done | bytes 917536 | tf_op jit(solution)/shard_map/all_to_all | solution.py:489
  116.2 0.0 collective-permute-start.4
  116.2 2.5 %collective-permute-done.4.other_ref = bf16[4,448,256]{2,1,0:T(8,128)(2,1)S(1)} collective-permute-done((bf16[4,448,256]{2,1,0:T(8,128)(2,1)S(1)}, bf16[4,448,256]{2,1,0:T(8,128)(2,1)S(1)}, u32[]{:S(2)}, u32[]{:S(2)}) %collective-permute-start.4) | collective-permute-done | bytes 917536 | tf_op jit(solution)/shard_map/ppermute | solution.py:492
  118.6 2.4 %shard_map.215 = (f32[3,3,256]{2,1,0:T(4,128)}, f32[1,256]{1,0:T(1,128)}, f32[256,768]{1,0:T(8,128)}, f32[256,256]{1,0:T(8,128)}, f32[1,256]{1,0:T(1,128)}, /*index=5*/f32[256,1024]{1,0:T(8,128)}, f32[1024,256]{1,0:T(8,128)}) custom-call(s32[2]{0:T(128)S(1)} %pad_add_fusion.place_ref, bf16[4,448,256]{2,1,0:T(8,128)(2,1)S(1)} %bitcast.16, ...), custom_call_target="tpu_custom_call" | custom-call | flops 1000000 | bytes 5000000 | tf_op jit(solution)/shard_map/pallas_call | solution.py:470
  (3 shorter events, 0.0 us)
Async XLA Ops:
  3.5 9.5 %copy-start.11 = (bf16[3,3,256]{2,1,0:T(4,128)(2,1)S(1)}, bf16[3,3,256]{2,1,0:T(4,128)(2,1)}, u32[]{:S(2)}) copy-start(bf16[3,3,256]{2,1,0:T(4,128)(2,1)} %param.16) | copy-start | bytes 13828
  3.5 32.4 %copy-start.3 = (bf16[256,1024]{1,0:T(8,128)(2,1)S(1)}, bf16[256,1024]{1,0:T(8,128)(2,1)}, u32[]{:S(2)}) copy-start(bf16[256,1024]{1,0:T(8,128)(2,1)} %w_up_ref.1) | copy-start | bytes 1572868
  3.5 32.4 %copy-start.4 = (bf16[1024,256]{1,0:T(8,128)(2,1)S(1)}, bf16[1024,256]{1,0:T(8,128)(2,1)}, u32[]{:S(2)}) copy-start(bf16[1024,256]{1,0:T(8,128)(2,1)} %w_down_ref.1) | copy-start | bytes 1572868
  3.5 32.4 %copy-start.5 = (bf16[256,768]{1,0:T(8,128)(2,1)S(1)}, bf16[256,768]{1,0:T(8,128)(2,1)}, u32[]{:S(2)}) copy-start(bf16[256,768]{1,0:T(8,128)(2,1)} %w_qkv_ref.3) | copy-start | bytes 1179652
  3.5 32.4 %copy-start.6 = (bf16[256,256]{1,0:T(8,128)(2,1)S(1)}, bf16[256,256]{1,0:T(8,128)(2,1)}, u32[]{:S(2)}) copy-start(bf16[256,256]{1,0:T(8,128)(2,1)} %w_out_ref.1) | copy-start | bytes 393220
  3.5 32.4 %copy-start.7 = (f32[256]{0:T(256)S(1)}, f32[256]{0:T(256)}, u32[]{:S(2)}) copy-start(f32[256]{0:T(256)} %param.20) | copy-start | bytes 3076
  3.5 32.4 %copy-start.8 = (f32[256]{0:T(256)S(1)}, f32[256]{0:T(256)}, u32[]{:S(2)}) copy-start(f32[256]{0:T(256)} %param.17) | copy-start | bytes 3076
  3.5 32.4 %copy-start.9 = (bf16[256,256]{1,0:T(8,128)(2,1)S(1)}, bf16[256,256]{1,0:T(8,128)(2,1)}, u32[]{:S(2)}) copy-start(bf16[256,256]{1,0:T(8,128)(2,1)} %constant.28.clone.mask_ref) | copy-start | bytes 393220
  3.5 32.4 %copy-start.10 = (bf16[3,128,128]{2,1,0:T(8,128)(2,1)S(1)}, bf16[3,128,128]{2,1,0:T(8,128)(2,1)}, u32[]{:S(2)}) copy-start(bf16[3,128,128]{2,1,0:T(8,128)(2,1)} %constant.30.clone.perm_ref) | copy-start | bytes 294916
  3.5 32.3 %all-to-all-start = ((bf16[32,6,16,256]{3,2,1,0:T(8,128)(2,1)}), bf16[32,6,16,256]{3,2,1,0:T(8,128)(2,1)S(1)}, u32[]{:S(2)}, u32[]{:S(2)}) async-start(bf16[32,6,16,256]{3,2,1,0:T(8,128)(2,1)} %shard_map.206), calls=%async_computation | async-start | bytes 3145728 | tf_op jit(solution)/shard_map/all_to_all | solution.py:489
  57.6 4.9 %copy-start = (bf16[320,384]{1,0:T(8,128)(2,1)S(1)}, bf16[320,384]{1,0:T(8,128)(2,1)}, u32[]{:S(2)}) copy-start(bf16[320,384]{1,0:T(8,128)(2,1)} %constant.31.clone.perm_ref) | copy-start | bytes 737284
  59.9 2.6 %collective-permute-start = (bf16[33,48,256]{2,1,0:T(8,128)(2,1)S(1)}, bf16[33,48,256]{2,1,0:T(8,128)(2,1)S(1)}, u32[]{:S(2)}, u32[]{:S(2)}) collective-permute-start(bf16[33,48,256]{2,1,0:T(8,128)(2,1)S(1)} %get-tuple-element.49), channel_id=1, source_target_pairs={{0,32},{32,0},{1,33},{33,1},{2,34},{34,2},{3,35},{35,3},{4,36},{36... | collective-permute-start | bytes 2433032 | tf_op jit(solution)/shard_map/ppermute | solution.py:492
  90.9 10.7 %copy-start.1 = (bf16[288,320]{1,0:T(8,128)(2,1)S(1)}, bf16[288,320]{1,0:T(8,128)(2,1)}, u32[]{:S(2)}) copy-start(bf16[288,320]{1,0:T(8,128)(2,1)} %constant.32.clone.main_ref) | copy-start | bytes 552964
  90.9 10.7 %copy-start.2 = (bf16[2,32,320]{2,1,0:T(8,128)(2,1)S(1)}, bf16[2,32,320]{2,1,0:T(8,128)(2,1)}, u32[]{:S(2)}) copy-start(bf16[2,32,320]{2,1,0:T(8,128)(2,1)} %constant.33.clone.edges_ref) | copy-start | bytes 122884
  90.9 5.8 %collective-permute-start.1 = (f32[56,256]{1,0:T(8,128)S(1)}, f32[56,256]{1,0:T(8,128)S(1)}, u32[]{:S(2)}, u32[]{:S(2)}) collective-permute-start(f32[56,256]{1,0:T(8,128)S(1)} %shard_map.211.mine_ref), channel_id=1, source_target_pairs={{0,64},{64,0},{1,65},{65,1},{2,66},{66,2},{3,67},{67,3},{4,68},{68... | collective-permute-start | bytes 172040 | tf_op jit(solution)/shard_map/ppermute | solution.py:492
  97.7 18.5 %all-to-all-start.2 = ((bf16[32,56,256]{2,1,0:T(8,128)(2,1)}), bf16[32,56,256]{2,1,0:T(8,128)(2,1)S(1)}, u32[]{:S(2)}, u32[]{:S(2)}) async-start(bf16[32,56,256]{2,1,0:T(8,128)(2,1)} %bitcast.8), calls=%async_computation.2 | async-start | bytes 1835008 | tf_op jit(solution)/shard_map/all_to_all | solution.py:489
  102.1 6.2 %collective-permute-start.2 = (bf16[32,256]{1,0:T(8,128)(2,1)S(1)}, bf16[32,256]{1,0:T(8,128)(2,1)S(1)}, u32[]{:S(2)}, u32[]{:S(2)}) collective-permute-start(bf16[32,256]{1,0:T(8,128)(2,1)S(1)} %get-tuple-element.51), channel_id=1, source_target_pairs={{0,1},{1,2},{2,3},{3,4},{4,5},{5,6},{6,7},{8,9},{9,10},{10,11},{11... | collective-permute-start | bytes 49160 | tf_op jit(solution)/shard_map/ppermute | solution.py:497
  105.8 7.2 %collective-permute-start.3 = (bf16[32,256]{1,0:T(8,128)(2,1)S(1)}, bf16[32,256]{1,0:T(8,128)(2,1)S(1)}, u32[]{:S(2)}, u32[]{:S(2)}) collective-permute-start(bf16[32,256]{1,0:T(8,128)(2,1)S(1)} %get-tuple-element.52), channel_id=1, source_target_pairs={{1,0},{2,1},{3,2},{4,3},{5,4},{6,5},{7,6},{9,8},{10,9},{11,10},{12... | collective-permute-start | bytes 49160 | tf_op jit(solution)/shard_map/ppermute | solution.py:497
  116.2 2.5 %collective-permute-start.4 = (bf16[4,448,256]{2,1,0:T(8,128)(2,1)S(1)}, bf16[4,448,256]{2,1,0:T(8,128)(2,1)S(1)}, u32[]{:S(2)}, u32[]{:S(2)}) collective-permute-start(bf16[4,448,256]{2,1,0:T(8,128)(2,1)S(1)} %bitcast.15), channel_id=1, source_target_pairs={{0,32},{32,0},{1,33},{33,1},{2,34},{34,2},{3,35},{35,3},{4,36},{36... | collective-permute-start | bytes 2752520 | tf_op jit(solution)/shard_map/ppermute | solution.py:492

commit v3 on v2

--- a/solution.py
+++ b/solution.py
@@ -21,29 +21,42 @@
 cubic_coef = 0.044715
 HEAD_SCALE = 1.0 / math.sqrt(C // HEADS)
 TOKENS = 1024
-AHEAD = 4
+AHEAD = 8
+CHUNK = 1024
+ROWS = 64
+SPAN = 16
 
 F32 = jnp.float32
 BF16 = jnp.bfloat16
 
 
+def positions(size):
+    return tuple(lax.broadcasted_iota(jnp.int32, (size, size), axis) for axis in range(2))
+
+
+def as_matrix(chosen):
+    return jnp.where(chosen, 1.0, 0.0).astype(BF16)
+
+
 def tile_to_columns():
-    out = np.zeros((256, 256), np.float32)
-    for col in range(16):
-        for row in range(16):
-            out[col * 16 + row, row * 16 + col] = 1
-    return out
-
-
-def sources_to_groups():
-    out = np.zeros((3, 128, 128), np.float32)
-    for p in range(8):
-        for a in range(2):
-            for e in range(8):
-                for variant, shift in enumerate((0, -1, 1)):
-                    if 0 <= e + shift < 8:
-                        out[variant, p * 16 + a * 8 + e, (e + shift) * 16 + a * 8 + p] = 1
-    return out
+    to, of = positions(256)
+    return as_matrix(((to >> 4) == (of & 15)) & ((to & 15) == (of >> 4)))
+
+
+def sources_to_groups(shift):
+    to, of = positions(128)
+    same = ((to >> 4) == (of & 7)) & (((to >> 3) & 1) == ((of >> 3) & 1))
+    return as_matrix(same & ((of >> 4) == (to & 7) + shift))
+
+
+def head_mask():
+    row, lane = positions(256)
+    return as_matrix((row >> 6) == ((lane >> 5) & 3))
+
+
+def turned_head_mask():
+    lane, row = (lax.broadcasted_iota(jnp.int32, (128, 256), axis) for axis in range(2))
+    return as_matrix((row >> 6) == (lane >> 5))
 
 
 def groups_to_pieces():
@@ -70,13 +83,6 @@
     return main, edges
 
 
-def head_mask():
-    mask = np.zeros((256, 128), np.float32)
-    for h in range(4):
-        mask[h * 64 : (h + 1) * 64, h * 32 : (h + 1) * 32] = 1
-    return np.concatenate([mask, mask], axis=1)
-
-
 def dot(a, b):
     return lax.dot_general(a, b, (((1,), (0,)), ((), ())), preferred_element_type=F32)
 
@@ -122,36 +128,57 @@
     return jnp.concatenate([upper, jnp.concatenate([zeros, rows[64:128]], axis=1)], axis=0)
 
 
-def diagonal(blocks):
-    return jnp.concatenate([blocks[0:64, 0:128], blocks[64:128, 128:256]], axis=0)
-
-
 def by_head(rows, mask):
     return jnp.concatenate([side_by_side(rows)] * 4, axis=0) * mask
 
 
-def attend_unit(query, key, value, mask):
-    scores = dot_nt(by_head(key, mask), block_diagonal(query)).reshape(4, 64, 128) * HEAD_SCALE
+def by_lane_half(columns, lower):
+    return jnp.concatenate([columns * lower, columns * (1 - lower)], axis=0)
+
+
+def by_head_turned(columns, lower, turned_mask):
+    swapped = jnp.concatenate([columns[:, 64:128], columns[:, 0:64]], axis=1)
+    parts = []
+    for first, second in ((columns, swapped), (swapped, columns)):
+        part = first * lower + second * (1 - lower)
+        parts.append(jnp.concatenate([part, part], axis=1) * turned_mask)
+    return jnp.concatenate(parts, axis=0)
+
+
+def own_half(blocks, lower):
+    return jnp.where(lower, blocks[0:128], blocks[128:256]).astype(BF16)
+
+
+def lane_half():
+    return lax.broadcasted_iota(jnp.int32, (1, 128), 1) < 64
+
+
+def attend_unit(query_turned, key, value_turned, lower, mask, turned_mask):
+    low = lower.astype(F32).astype(BF16)
+    scores = dot(by_head(key, mask), by_lane_half(query_turned, low)).reshape(4, 64, 128) * HEAD_SCALE
     expos = jnp.exp(scores - jnp.max(scores, axis=1, keepdims=True))
     probs = expos * (1.0 / jnp.sum(expos, axis=1, keepdims=True))
     probs = probs.reshape(256, 128).astype(BF16)
-    return probs, diagonal(dot_tn(probs, by_head(value, mask))).astype(BF16)
-
-
-def attend_unit_back(query, key, value, probs, upstream, mask, wide_mask):
+    mixed = dot(by_head_turned(value_turned, low, turned_mask), probs)
+    return probs, own_half(mixed, lower)
+
+
+def attend_unit_back(
+    query, key_turned, value, probs, upstream, upstream_turned, lower, mask, turned_mask, wide_mask
+):
+    low = lower.astype(F32).astype(BF16)
     wide = probs.astype(F32).reshape(4, 64, 128)
-    upstream = block_diagonal(upstream)
-    prob_grad = dot_nt(by_head(value, mask), upstream).reshape(4, 64, 128)
+    prob_grad = dot(by_head(value, mask), by_lane_half(upstream_turned, low)).reshape(4, 64, 128)
     centre = jnp.sum(wide * prob_grad, axis=1, keepdims=True)
     score_grad = (wide * (prob_grad - centre) * HEAD_SCALE).reshape(256, 128).astype(BF16)
-    query_grad = diagonal(dot_tn(score_grad, by_head(key, mask)))
+    query_grad = own_half(dot(by_head_turned(key_turned, low, turned_mask), score_grad), lower)
     key_grad = jnp.sum((dot(score_grad, block_diagonal(query)) * wide_mask).reshape(4, 64, 256), axis=0)
-    value_grad = jnp.sum((dot(probs, upstream) * wide_mask).reshape(4, 64, 256), axis=0)
-    return query_grad.astype(BF16), stacked(key_grad).astype(BF16), stacked(value_grad).astype(BF16)
-
-
-def pack_kernel(x_ref, cot_ref, perm_ref, out_ref):
-    perm = perm_ref[...]
+    value_grad = jnp.sum((dot(probs, block_diagonal(upstream)) * wide_mask).reshape(4, 64, 256), axis=0)
+    return query_grad, stacked(key_grad).astype(BF16), stacked(value_grad).astype(BF16)
+
+
+def pack_kernel(x_ref, cot_ref, out_ref):
+    perm = tile_to_columns()
     for block in range(4):
         tokens = x_ref[:, 16 * block : 16 * block + 16, :].reshape(256, C)
         columns = dot(perm, tokens).astype(BF16).reshape(16, 16, C)
@@ -169,17 +196,24 @@
                 out_ref[(k - 1) % 32, 3] = columns[i]
 
 
+def store_halves(core, lower, upper, keep_ref, send_ref, rows):
+    keep_ref[rows, :] = jnp.where(core == 0, lower, upper).astype(BF16)
+    send_ref[rows, :] = jnp.where(core == 0, upper, lower).astype(BF16)
+
+
 def forward_kernel(
-    place_ref, x_ref, perm_ref, dw_ref, gain_one_ref, w_qkv_ref, w_out_ref, gain_two_ref,
-    w_up_ref, w_down_ref, mask_ref,
-    xs_ref, in_ref, proj_ref, probs_ref, mixed_grad_ref, resid_grad_ref, sums_ref,
+    place_ref, x_ref, dw_ref, gain_one_ref, w_qkv_ref, w_out_ref, gain_two_ref,
+    w_up_ref, w_down_ref,
+    xs_ref, in_ref, proj_ref, key_turned_ref, probs_ref, mixed_grad_ref, resid_grad_ref, keep_ref, send_ref,
     out_grad_ref, gain_grad_ref,
-    cot_s, mixed_s, two_s, low_s, act_s, pre_s,
+    cot_s, mixed_s, two_s, low_s, act_s, pre_s, turned_s, mixed_turned_s,
+    narrow_s, normed_s, wide_s, cot_wide_s,
 ):
     owner = place_ref[0]
-    first = perm_ref[jnp.where(owner == 0, 1, 0)]
-    last = perm_ref[jnp.where(owner == 31, 2, 0)]
-    plain = perm_ref[0]
+    core = place_ref[1]
+    first = sources_to_groups(jnp.where(owner == 0, -1, 0))
+    last = sources_to_groups(jnp.where(owner == 31, 1, 0))
+    plain = sources_to_groups(0)
 
     for r in range(4):
         for j in range(4):
@@ -219,7 +253,12 @@
 
     lax.fori_loop(0, 4, project, 0)
 
-    mask = mask_ref[...]
+    turned_s[0:256, :] = proj_ref[:, 0:256].T
+    turned_s[256:512, :] = proj_ref[:, 512:768].T
+    key_turned_ref[...] = proj_ref[:, 256:512].T
+    mask = head_mask()
+    turned_mask = turned_head_mask()
+    lower = lane_half()
 
     def attend(i, carry):
         units = []
@@ -227,15 +266,19 @@
             pair = i * AHEAD + n
             rows = pl.ds(pl.multiple_of(pair * 128, 128), 128)
             for side in range(2):
-                parts = [proj_ref[rows, 256 * m + 128 * side : 256 * m + 128 * side + 128] for m in range(3)]
-                units.append((pair, rows, side, parts))
-        results = [attend_unit(*parts, mask) for _, _, _, parts in units]
-        for (pair, rows, side, _), (probs, mixed) in zip(units, results):
-            probs_ref[2 * pair + side] = probs
-            mixed_s[rows, 128 * side : 128 * side + 128] = mixed
+                lanes = slice(128 * side, 128 * side + 128)
+                query = turned_s[lanes, rows]
+                key = proj_ref[rows, 256 + 128 * side : 384 + 128 * side]
+                value = turned_s[256 + 128 * side : 384 + 128 * side, rows]
+                units.append((2 * pair + side, lanes, rows, (query, key, value)))
+        results = [attend_unit(*parts, lower, mask, turned_mask) for _, _, _, parts in units]
+        for (unit, lanes, rows, _), (probs, mixed) in zip(units, results):
+            probs_ref[unit] = probs
+            mixed_turned_s[lanes, rows] = mixed
         return carry
 
     lax.fori_loop(0, 8 // AHEAD, attend, 0)
+    mixed_s[...] = mixed_turned_s[...].T
 
     for r in range(4):
         for j in range(2):
@@ -247,50 +290,71 @@
     gain_two = gain_two_ref[...]
 
     def tail(i, gain_grad):
-        rows = pl.ds(pl.multiple_of(i * 512, 512), 512)
-        cot = cot_s[rows, :]
-        resid = in_ref[rows, :].astype(F32) + dot(mixed_s[rows, :], w_out_ref[...])
-        normed, inverse = norm(resid)
-        inputs = (normed * gain_two).astype(BF16)
-        two_s[rows, :] = inputs
-        pre = dot(inputs, w_up_ref[...])
-        square = pre * pre
-        tangent = jnp.tanh(gelu_coef * (pre + cubic_coef * square * pre))
-        half = 0.5 * (1.0 + tangent)
-        act_s[rows, :] = (pre * half).astype(BF16)
-        slope = half + 0.5 * pre * (1.0 - tangent * tangent) * gelu_coef * (
-            1.0 + 3.0 * cubic_coef * square
-        )
-        pre_grad = (dot_nt(cot, w_down_ref[...]) * slope).astype(BF16)
-        pre_s[rows, :] = pre_grad
-        in_grad = dot_nt(pre_grad, w_up_ref[...])
-        resid_grad = cot.astype(F32) + norm_back(in_grad, normed, inverse, gain_two)
-        resid_grad_ref[rows, :] = resid_grad
-        low = resid_grad.astype(BF16)
-        low_s[rows, :] = low
-        mixed_grad_ref[rows, :] = dot_nt(low, w_out_ref[...]).astype(BF16)
-        return gain_grad + fold_rows(in_grad * normed)
-
-    gain_grad = lax.fori_loop(0, 2, tail, jnp.zeros((8, C), F32))
+        rows = pl.ds(pl.multiple_of(i * CHUNK, CHUNK), CHUNK)
+        narrow_s[...] = dot(mixed_s[rows, :], w_out_ref[...])
+        inverses = []
+        for n in range(CHUNK // ROWS):
+            part = slice(ROWS * n, ROWS * n + ROWS)
+            own = pl.ds(pl.multiple_of(i * CHUNK + ROWS * n, ROWS), ROWS)
+            normed, inverse = norm(in_ref[own, :].astype(F32) + narrow_s[part, :])
+            inverses.append(inverse)
+            normed_s[part, :] = normed
+            two_s[own, :] = (normed * gain_two).astype(BF16)
+        wide_s[...] = dot(two_s[rows, :], w_up_ref[...])
+        cot_wide_s[...] = dot_nt(cot_s[rows, :], w_down_ref[...])
+        for n in range(CHUNK // SPAN):
+            part = slice(SPAN * n, SPAN * n + SPAN)
+            own = pl.ds(pl.multiple_of(i * CHUNK + SPAN * n, SPAN), SPAN)
+            for block in range(4):
+                columns = slice(256 * block, 256 * block + 256)
+                pre = wide_s[part, columns]
+                square = pre * pre
+                tangent = jnp.tanh(pre * (gelu_coef + (gelu_coef * cubic_coef) * square))
+                half = 0.5 + 0.5 * tangent
+                act = pre * half
+                act_s[own, columns] = act.astype(BF16)
+                slope = half + (act - act * half) * (
+                    2.0 * gelu_coef + (6.0 * gelu_coef * cubic_coef) * square
+                )
+                pre_s[own, columns] = (cot_wide_s[part, columns] * slope).astype(BF16)
+        narrow_s[...] = dot_nt(pre_s[rows, :], w_up_ref[...])
+        for n in range(CHUNK // ROWS):
+            part = slice(ROWS * n, ROWS * n + ROWS)
+            own = pl.ds(pl.multiple_of(i * CHUNK + ROWS * n, ROWS), ROWS)
+            in_grad = narrow_s[part, :]
+            normed = normed_s[part, :]
+            back = norm_back(in_grad, normed, inverses[n], gain_two)
+            resid_grad = cot_s[own, :].astype(F32) + back
+            resid_grad_ref[own, :] = resid_grad
+            low_s[own, :] = resid_grad.astype(BF16)
+            gain_grad = gain_grad + fold_rows(in_grad * normed)
+        mixed_grad_ref[rows, :] = dot_nt(low_s[rows, :], w_out_ref[...]).astype(BF16)
+        return gain_grad
+
+    gain_grad = lax.fori_loop(0, TOKENS // CHUNK, tail, jnp.zeros((8, C), F32))
     gain_grad_ref[...] = gain_grad
 
     cot_turned = cot_s[...].T
     two_turned = two_s[...].T
     for block in range(4):
         columns = slice(256 * block, 256 * block + 256)
-        down = dot(cot_turned, act_s[:, columns]).T.astype(BF16)
-        up = dot(two_turned, pre_s[:, columns]).astype(BF16)
-        sums_ref[256 * block : 256 * block + 256, :] = down
-        sums_ref[1024 + 256 * block : 1280 + 256 * block, :] = up
-    out_grad_ref[...] = dot(mixed_s[...].T, low_s[...])
+        down = dot(cot_turned, act_s[:, columns]).T
+        up = dot(two_turned, pre_s[:, columns])
+        store_halves(core, down, up, keep_ref, send_ref, slice(256 * block, 256 * block + 256))
+    out_grad_ref[...] = dot(mixed_turned_s[...], low_s[...])
 
 
 def backward_kernel(
-    in_ref, proj_ref, probs_ref, mixed_grad_ref, resid_grad_ref, gain_one_ref, w_qkv_ref, mask_ref,
+    in_ref, proj_ref, key_turned_ref, probs_ref, mixed_grad_ref, resid_grad_ref, gain_one_ref,
+    w_qkv_ref,
     proj_grad_ref, inputs_ref, grad_ref, gain_grad_ref,
+    upstream_s, query_grad_s,
 ):
-    mask = mask_ref[...]
+    upstream_s[...] = mixed_grad_ref[...].T
+    mask = head_mask()
     wide_mask = mask.astype(F32)
+    turned_mask = turned_head_mask()
+    lower = lane_half()
 
     def attend_back(i, carry):
         units = []
@@ -299,16 +363,26 @@
             rows = pl.ds(pl.multiple_of(pair * 128, 128), 128)
             for side in range(2):
                 lanes = slice(128 * side, 128 * side + 128)
-                parts = [proj_ref[rows, 256 * m + 128 * side : 256 * m + 128 * side + 128] for m in range(3)]
-                parts += [probs_ref[2 * pair + side], mixed_grad_ref[rows, lanes]]
-                units.append((pair, rows, side, parts))
-        results = [attend_unit_back(*parts, mask, wide_mask) for _, _, _, parts in units]
-        for (_, rows, side, _), grads in zip(units, results):
-            for m in range(3):
-                proj_grad_ref[rows, 256 * m + 128 * side : 256 * m + 128 * side + 128] = grads[m]
+                parts = (
+                    proj_ref[rows, lanes],
+                    key_turned_ref[lanes, rows],
+                    proj_ref[rows, 512 + 128 * side : 640 + 128 * side],
+                    probs_ref[2 * pair + side],
+                    mixed_grad_ref[rows, lanes],
+                    upstream_s[lanes, rows],
+                )
+                units.append((side, lanes, rows, parts))
+        results = [
+            attend_unit_back(*parts, lower, mask, turned_mask, wide_mask) for _, _, _, parts in units
+        ]
+        for (side, lanes, rows, _), grads in zip(units, results):
+            query_grad_s[lanes, rows] = grads[0]
+            proj_grad_ref[rows, 256 + 128 * side : 384 + 128 * side] = grads[1]
+            proj_grad_ref[rows, 512 + 128 * side : 640 + 128 * side] = grads[2]
         return carry
 
     lax.fori_loop(0, 8 // AHEAD, attend_back, 0)
+    proj_grad_ref[:, 0:256] = query_grad_s[...].T
 
     gain_one = gain_one_ref[...]
 
@@ -325,9 +399,8 @@
 
 def sums_kernel(
     place_ref, xs_ref, inputs_ref, proj_grad_ref, grad_ref, gain_one_grad_ref, gain_two_grad_ref,
-    out_grad_ref, tail_ref,
+    out_grad_ref,
     keep_ref, send_ref,
-    head_s, small_s,
 ):
     core = place_ref[1]
 
@@ -343,30 +416,29 @@
     kernel_grad = lax.fori_loop(0, 16, taps, (jnp.zeros((8, C), F32),) * 9, unroll=4)
 
     inputs_turned = inputs_ref[...].T
-    for block in range(3):
-        terms = dot(inputs_turned, proj_grad_ref[:, 256 * block : 256 * block + 256])
-        head_s[256 * block : 256 * block + 256, :] = terms.astype(BF16)
-    head_s[768:1024, :] = out_grad_ref[...].astype(BF16)
+    terms = [
+        dot(inputs_turned, proj_grad_ref[:, 256 * block : 256 * block + 256])
+        for block in range(3)
+    ]
+    terms.append(out_grad_ref[...])
+    for block in range(2):
+        rows = slice(256 * block, 256 * block + 256)
+        store_halves(core, terms[block], terms[2 + block], keep_ref, send_ref, rows)
     small = [jnp.sum(term, axis=0, keepdims=True) for term in kernel_grad]
     small.append(jnp.sum(gain_one_grad_ref[...], axis=0, keepdims=True))
     small.append(jnp.sum(gain_two_grad_ref[...], axis=0, keepdims=True))
     small.append(jnp.zeros((5, C), F32))
-    small_s[...] = jnp.concatenate(small, axis=0)
-    for ref, half in ((keep_ref, core), (send_ref, 1 - core)):
-        for k in range(32):
-            tail = pl.ds(pl.multiple_of(half * 1024 + 32 * k, 32), 32)
-            head = pl.ds(pl.multiple_of(half * 512 + 16 * k, 16), 16)
-            ref[k, 0:32, :] = tail_ref[tail, :]
-            ref[k, 32:48, :] = head_s[head, :]
-        rows = small_s[pl.ds(pl.multiple_of(half * 8, 8), 8), :]
-        ref[32, 0:16, :] = jnp.concatenate([rows, rows], axis=0).astype(BF16)
-        ref[32, 16:48, :] = jnp.zeros((32, C), BF16)
-
-
-def pieces_kernel(grad_ref, keep_ref, swapped_ref, perm_ref, out_ref):
+    lower, upper = jnp.concatenate(small[0:8], axis=0), jnp.concatenate(small[8:], axis=0)
+    lower, upper = (jnp.concatenate([rows, rows], axis=0) for rows in (lower, upper))
+    store_halves(core, lower, upper, keep_ref, send_ref, slice(512, 528))
+
+
+def pieces_kernel(
+    grad_ref, tail_ref, other_tail_ref, head_ref, other_head_ref, perm_ref, out_ref
+):
     perm = perm_ref[...]
     edge = jnp.zeros((8, C), F32)
-    small = keep_ref[32, 0:16, :].astype(F32) + swapped_ref[32, 0:16, :].astype(F32)
+    small = head_ref[512:528, :].astype(F32) + other_head_ref[512:528, :].astype(F32)
     for r in range(4):
         parts = [grad_ref[64 * g + 16 * r : 64 * g + 16 * r + 16, :] for g in range(16)]
         for j in range(2):
@@ -379,9 +451,12 @@
         parts.append(jnp.zeros((88, C), F32))
         tokens = jnp.concatenate(parts, axis=0).astype(BF16)
         moved = dot(perm, tokens).reshape(8, PIECE, C)
-        pieces = slice(8 * r, 8 * r + 8)
-        sums = keep_ref[pieces].astype(F32) + swapped_ref[pieces].astype(F32)
-        joined = jnp.concatenate([moved, sums], axis=1)
+        rows = slice(256 * r, 256 * r + 256)
+        tail = tail_ref[rows, :].astype(F32) + other_tail_ref[rows, :].astype(F32)
+        rows = slice(128 * r, 128 * r + 128)
+        head = head_ref[rows, :].astype(F32) + other_head_ref[rows, :].astype(F32)
+        joined = [moved, tail.reshape(8, 32, C), head.reshape(8, 16, C)]
+        joined = jnp.concatenate(joined, axis=1)
         out_ref[r] = joined.reshape(8 * JOINED, C).astype(BF16)
 
 
@@ -483,7 +558,6 @@
     core = lax.axis_index("core")
     place = jnp.stack([owner, core]).astype(jnp.int32)
     dw_rows = dw_kernel.reshape(9, C).astype(F32)
-    mask = jnp.asarray(head_mask(), BF16)
 
     def exchange(stacked):
         return lax.all_to_all(stacked, ("row", "col"), split_axis=0, concat_axis=0, tiled=True)
@@ -499,7 +573,7 @@
     (packed,) = call(
         pack_kernel,
         [((32, 6, 16, C), BF16)],
-        [input_map[0], cotangent[0], jnp.asarray(tile_to_columns(), BF16)],
+        [input_map[0], cotangent[0]],
         flops=4 * 10**8,
         moved=4 * 10**6,
         limit=60,
@@ -507,23 +581,26 @@
     arrived = exchange(packed)
 
     (
-        xs, start, projected, probs, mixed_grad, resid_grad, tail_sums, out_grad, gain_two_grad,
+        xs, start, projected, key_turned, probs, mixed_grad, resid_grad, tail_keep, tail_send,
+        out_grad, gain_two_grad,
     ) = call(
         forward_kernel,
         [
             ((4, 10, 64, C), BF16),
             ((TOKENS, C), BF16),
             ((TOKENS, 3 * C), BF16),
+            ((C, TOKENS), BF16),
             ((16, 256, 128), BF16),
             ((TOKENS, C), BF16),
             ((TOKENS, C), F32),
-            ((2048, C), BF16),
+            ((1024, C), BF16),
+            ((1024, C), BF16),
             ((C, C), F32),
             ((8, C), F32),
         ],
         [
-            place, arrived, jnp.asarray(sources_to_groups(), BF16), dw_rows,
-            gain_one.reshape(1, C), w_qkv, w_out, gain_two.reshape(1, C), w_up, w_down, mask,
+            place, arrived, dw_rows,
+            gain_one.reshape(1, C), w_qkv, w_out, gain_two.reshape(1, C), w_up, w_down,
         ],
         [
             ((TOKENS, C), BF16),
@@ -532,32 +609,43 @@
             ((TOKENS, C), BF16),
             ((TOKENS, FF), BF16),
             ((TOKENS, FF), BF16),
+            ((2 * C, TOKENS), BF16),
+            ((C, TOKENS), BF16),
+            ((CHUNK, C), F32),
+            ((CHUNK, C), F32),
+            ((CHUNK, FF), F32),
+            ((CHUNK, FF), F32),
         ],
         scalars=1,
         flops=8 * 10**9,
         moved=12 * 10**6,
-        limit=40,
+        limit=36,
     )
 
     proj_grad, inputs, grad, gain_one_grad = call(
         backward_kernel,
         [((TOKENS, 3 * C), BF16), ((TOKENS, C), BF16), ((TOKENS, C), F32), ((8, C), F32)],
-        [start, projected, probs, mixed_grad, resid_grad, gain_one.reshape(1, C), w_qkv, mask],
+        [
+            start, projected, key_turned, probs, mixed_grad, resid_grad, gain_one.reshape(1, C), w_qkv,
+        ],
+        [((C, TOKENS), BF16), ((C, TOKENS), BF16)],
         flops=5 * 10**9,
         moved=8 * 10**6,
         limit=32,
     )
     keep, send = call(
         sums_kernel,
-        [((33, SUMS, C), BF16), ((33, SUMS, C), BF16)],
-        [place, xs, inputs, proj_grad, grad, gain_one_grad, gain_two_grad, out_grad, tail_sums],
-        [((1024, C), BF16), ((16, C), F32)],
+        [((528, C), BF16), ((528, C), BF16)],
+        [place, xs, inputs, proj_grad, grad, gain_one_grad, gain_two_grad, out_grad],
         scalars=1,
     )
     (pieces,) = call(
         pieces_kernel,
         [((4, 8 * JOINED, C), BF16)],
-        [grad, keep, swap(send, "core"), jnp.asarray(groups_to_pieces(), BF16)],
+        [
+            grad, tail_keep, swap(tail_send, "core"), keep, swap(send, "core"),
+            jnp.asarray(groups_to_pieces(), BF16),
+        ],
     )
     back = exchange(pieces.reshape(32, JOINED, C)).reshape(4, 8 * JOINED, C)
     factor = 1.0 / math.sqrt(TOKENS * 128)

time: 123 us -> 116 us (0.943)
  Pallas kernels: 33.6 us -> 27.3 us
    pallas_call x10, Pallas kernels: 33.6 us -> 27.3 us  [call(): pl.pallas_call(kernel, out_shape=tuple((jax.ShapeDtypeStruct(shape, dtype...]
    ppermute x3 -> x4, waiting for transfers between devices: 7.56 us -> 6.43 us  [swap(): return lax.ppermute(values, axis, [(0, 1), (1, 0)])]
    ppermute x3 -> x4, starting transfers between devices: 3.25 us -> 3.81 us  [swap(): return lax.ppermute(values, axis, [(0, 1), (1, 0)])]
  transfers between devices with their start and end apart: 7 -> 8, of which waited for: 7 -> 7; matrix products, arithmetic and copies ran while one was open for 0% -> 0% of each run, Pallas kernels for 2% -> 8%
where the time goes in v3:
time: 116 us; the launch traced here: 115 us
  waiting for transfers between devices  36.3 us (31%)
  blocking collectives  27.7 us (24%)
  Pallas kernels  27.3 us (24%)
  starting transfers between devices  22.4 us (19%)
    all_to_all x1, blocking collectives, exchange(): lax.all_to_all(stacked, ('row', 'col'), split_axis=0, concat_axis=0, tile...  27.7 us
    pallas_call x10, Pallas kernels, call(): pl.pallas_call(kernel, out_shape=tuple((jax.ShapeDtypeStruct(shape, dtype...  27.3 us
    all_to_all x2, waiting for transfers between devices, exchange(): lax.all_to_all(stacked, ('row', 'col'), split_axis=0, concat_axis=0, tile...  24 us
    all_to_all x2, starting transfers between devices, exchange(): lax.all_to_all(stacked, ('row', 'col'), split_axis=0, concat_axis=0, tile...  13.6 us
    ppermute x4, waiting for transfers between devices, swap(): return lax.ppermute(values, axis, [(0, 1), (1, 0)])  6.43 us
    ppermute x2, waiting for transfers between devices, shift(): return lax.ppermute(values, axis, pairs)  5.81 us
    ppermute x2, starting transfers between devices, shift(): return lax.ppermute(values, axis, pairs)  4.99 us
    ppermute x4, starting transfers between devices, swap(): return lax.ppermute(values, axis, [(0, 1), (1, 0)])  3.81 us
  transfers between devices with their start and end apart: 8, of which 7 were waited for; matrix products, arithmetic and copies ran while one was open for 0% of the time, Pallas kernels for 8%

profile of v3, /device:TPU:0, one launch (start us, length us, event | category | flops | bytes accessed | tf_op | source)
XLA Modules:
  0.0 114.6 jit_solution(13486448691641640157)
XLA Ops:
  0.6 2.8 %shard_map.179 = bf16[32,6,16,256]{3,2,1,0:T(8,128)(2,1)} custom-call(bf16[16,64,256]{2,1,0:T(8,128)(2,1)} %bitcast.20, bf16[16,64,256]{2,1,0:T(8,128)(2,1)} %bitcast.21), custom_call_target="tpu_custom_call" | custom-call | flops 400000000 | bytes 4000000 | tf_op jit(solution)/shard_map/pallas_call | solution.py:545
  3.4 0.0 copy-start.9
  3.4 0.0 copy-start.3
  3.4 0.0 copy-start.4
  3.4 0.0 copy-start.5
  3.4 0.0 copy-start.6
  3.5 0.0 copy-start.7
  3.5 0.0 copy-start.8
  3.5 9.4 %all-to-all-start = ((bf16[32,6,16,256]{3,2,1,0:T(8,128)(2,1)}), bf16[32,6,16,256]{3,2,1,0:T(8,128)(2,1)S(1)}, u32[]{:S(2)}, u32[]{:S(2)}) async-start(bf16[32,6,16,256]{3,2,1,0:T(8,128)(2,1)} %shard_map.179), calls=%async_computation | async-start | bytes 3145728 | tf_op jit(solution)/shard_map/all_to_all | solution.py:563
  12.9 0.0 copy-done.9
  12.9 0.1 pad_add_fusion.place_ref
  13.0 22.8 %all-to-all-done.x_ref = bf16[32,6,16,256]{3,2,1,0:T(8,128)(2,1)S(1)} async-done(((bf16[32,6,16,256]{3,2,1,0:T(8,128)(2,1)}), bf16[32,6,16,256]{3,2,1,0:T(8,128)(2,1)S(1)}, u32[]{:S(2)}, u32[]{:S(2)}) %all-to-all-start) | async-done | bytes 1572896 | tf_op jit(solution)/shard_map/all_to_all | solution.py:563
  35.8 0.0 copy-done.3
  35.8 0.0 copy-done.4
  35.8 0.0 copy-done.5
  35.8 0.0 copy-done.6
  35.8 0.0 copy-done.7
  35.9 0.0 copy-done.8
  35.9 11.0 %shard_map.180 = (bf16[4,10,64,256]{3,2,1,0:T(8,128)(2,1)S(1)}, bf16[1024,256]{1,0:T(8,128)(2,1)S(1)}, bf16[1024,768]{1,0:T(8,128)(2,1)S(1)}, bf16[256,1024]{1,0...) custom-call(s32[2]{0:T(128)S(1)} %pad_add_fusion.place_ref, ...), custom_call_target="tpu_custom_call" | custom-call | flops 8000000000 | bytes 12000000 | tf_op jit(solution)/shard_map/pallas_call | solution.py:545
  46.9 0.3 collective-permute-start
  47.2 4.7 %shard_map.181 = (bf16[1024,768]{1,0:T(8,128)(2,1)S(1)}, bf16[1024,256]{1,0:T(8,128)(2,1)S(1)}, f32[1024,256]{1,0:T(8,128)S(1)}, f32[8,256]{1,0:T(8,128)S(1)}) custom-call(bf16[1024,256]{1,0:T(8,128)(2,1)S(1)} %get-tuple-element.37.in_ref, bf16[1024,768]{1,0:T(8,128)(2,1)S(1)} %get-tuple-element.38.proj_ref, ...), custom_call_target="tpu_custom_call" | custom-call | flops 5000000000 | bytes 8000000 | tf_op jit(solution)/shard_map/pallas_call | solution.py:545
  51.9 0.0 copy-start
  51.9 2.1 %shard_map.182 = (bf16[528,256]{1,0:T(8,128)(2,1)S(1)}, bf16[528,256]{1,0:T(8,128)(2,1)S(1)}) custom-call(s32[2]{0:T(128)S(1)} %pad_add_fusion.place_ref, bf16[4,10,64,256]{3,2,1,0:T(8,128)(2,1)S(1)} %get-tuple-element.46.xs_ref, bf16[1024,256]{1,0:T(8,128)(2,1)S(1)} %get-tuple-element.47.inputs_ref, bf16[1024,768]{1,0:T(8,128)(2,1)S(1)} %get-tuple-element.48.proj_grad_ref, ...), custom_call_target="tpu_custom_call" | custom-call | tf_op jit(solution)/shard_map/pallas_call | solution.py:545
  54.0 0.6 collective-permute-start.1
  54.6 1.2 %collective-permute-done.1.other_head_ref = bf16[528,256]{1,0:T(8,128)(2,1)S(1)} collective-permute-done((bf16[528,256]{1,0:T(8,128)(2,1)S(1)}, bf16[528,256]{1,0:T(8,128)(2,1)S(1)}, u32[]{:S(2)}, u32[]{:S(2)}) %collective-permute-start.1) | collective-permute-done | bytes 270368 | tf_op jit(solution)/shard_map/ppermute | solution.py:566
  55.8 0.0 collective-permute-done.other_tail_ref
  55.8 0.0 copy-done
  55.8 0.6 shard_map.183
  56.4 27.7 %all_to_all.15 = bf16[32,88,256]{2,1,0:T(8,128)(2,1)S(1)} all-to-all(bf16[32,88,256]{2,1,0:T(8,128)(2,1)S(1)} %bitcast.14), channel_id=1, replica_groups=mesh['yh'=2,'core'=2,'row'=4,'col'=8] {'row','col'}, dimensions={0} | all-to-all | bytes 2883584 | tf_op jit(solution)/shard_map/all_to_all | solution.py:563
  84.2 0.1 shard_map.184.mine_ref
  84.3 0.0 copy-start.1
  84.3 0.0 copy-start.2
  84.3 3.0 %collective-permute-start.2 = (f32[56,256]{1,0:T(8,128)S(1)}, f32[56,256]{1,0:T(8,128)S(1)}, u32[]{:S(2)}, u32[]{:S(2)}) collective-permute-start(f32[56,256]{1,0:T(8,128)S(1)} %shard_map.184.mine_ref), channel_id=1, source_target_pairs={{0,64},{64,0},{1,65},{65,1},{2,66},{66,2},{3,67},{67,3},{4,68},{68... | collective-permute-start | bytes 172040 | tf_op jit(solution)/shard_map/ppermute | solution.py:566
  87.3 2.8 %collective-permute-done.2.other_ref = f32[56,256]{1,0:T(8,128)S(1)} collective-permute-done((f32[56,256]{1,0:T(8,128)S(1)}, f32[56,256]{1,0:T(8,128)S(1)}, u32[]{:S(2)}, u32[]{:S(2)}) %collective-permute-start.2) | collective-permute-done | bytes 57376 | tf_op jit(solution)/shard_map/ppermute | solution.py:566
  90.1 1.0 shard_map.185
  91.1 4.2 %all-to-all-start.2 = ((bf16[32,56,256]{2,1,0:T(8,128)(2,1)}), bf16[32,56,256]{2,1,0:T(8,128)(2,1)S(1)}, u32[]{:S(2)}, u32[]{:S(2)}) async-start(bf16[32,56,256]{2,1,0:T(8,128)(2,1)} %bitcast.8), calls=%async_computation.2 | async-start | bytes 1835008 | tf_op jit(solution)/shard_map/all_to_all | solution.py:563
  95.2 0.0 copy-done.1
  95.2 0.0 copy-done.2
  95.2 0.5 shard_map.186
  95.8 3.7 %collective-permute-start.3 = (bf16[32,256]{1,0:T(8,128)(2,1)S(1)}, bf16[32,256]{1,0:T(8,128)(2,1)S(1)}, u32[]{:S(2)}, u32[]{:S(2)}) collective-permute-start(bf16[32,256]{1,0:T(8,128)(2,1)S(1)} %get-tuple-element.55), channel_id=1, source_target_pairs={{0,1},{1,2},{2,3},{3,4},{4,5},{5,6},{6,7},{8,9},{9,10},{10,11},{11... | collective-permute-start | bytes 49160 | tf_op jit(solution)/shard_map/ppermute | solution.py:571
  99.5 1.3 %collective-permute-start.4 = (bf16[32,256]{1,0:T(8,128)(2,1)S(1)}, bf16[32,256]{1,0:T(8,128)(2,1)S(1)}, u32[]{:S(2)}, u32[]{:S(2)}) collective-permute-start(bf16[32,256]{1,0:T(8,128)(2,1)S(1)} %get-tuple-element.56), channel_id=1, source_target_pairs={{1,0},{2,1},{3,2},{4,3},{5,4},{6,5},{7,6},{9,8},{10,9},{11,10},{12... | collective-permute-start | bytes 49160 | tf_op jit(solution)/shard_map/ppermute | solution.py:571
  100.8 1.8 %collective-permute-done.3.left_ref = bf16[32,256]{1,0:T(8,128)(2,1)S(1)} collective-permute-done((bf16[32,256]{1,0:T(8,128)(2,1)S(1)}, bf16[32,256]{1,0:T(8,128)(2,1)S(1)}, u32[]{:S(2)}, u32[]{:S(2)}) %collective-permute-start.3) | collective-permute-done | bytes 16416 | tf_op jit(solution)/shard_map/ppermute | solution.py:571
  102.6 4.0 %collective-permute-done.4.right_ref = bf16[32,256]{1,0:T(8,128)(2,1)S(1)} collective-permute-done((bf16[32,256]{1,0:T(8,128)(2,1)S(1)}, bf16[32,256]{1,0:T(8,128)(2,1)S(1)}, u32[]{:S(2)}, u32[]{:S(2)}) %collective-permute-start.4) | collective-permute-done | bytes 16416 | tf_op jit(solution)/shard_map/ppermute | solution.py:571
  106.6 2.0 %shard_map.187 = f32[1,16,64,256]{3,2,1,0:T(8,128)} custom-call(bf16[18,64,256]{2,1,0:T(8,128)(2,1)S(1)} %get-tuple-element.54.tile_ref, bf16[32,256]{1,0:T(8,128)(2,1)S(1)} %collective-permute-done.3.left_ref, bf16[32,256]{1,0:T(8,128)(2,1)S(1)} %collective-permute-done.4.right_ref, f32[9,256]{1,0:T(8,128)S(1)} %reshape.52.dw_ref), custom_call_target="tpu_custom_call" | custom-call | tf_op jit(solution)/shard_map/pallas_call | solution.py:545
  108.6 1.2 %all-to-all-done.2 = bf16[32,56,256]{2,1,0:T(8,128)(2,1)S(1)} async-done(((bf16[32,56,256]{2,1,0:T(8,128)(2,1)}), bf16[32,56,256]{2,1,0:T(8,128)(2,1)S(1)}, u32[]{:S(2)}, u32[]{:S(2)}) %all-to-all-start.2) | async-done | bytes 917536 | tf_op jit(solution)/shard_map/all_to_all | solution.py:563
  109.7 0.0 collective-permute-start.5
  109.8 2.5 %collective-permute-done.5.other_ref = bf16[4,448,256]{2,1,0:T(8,128)(2,1)S(1)} collective-permute-done((bf16[4,448,256]{2,1,0:T(8,128)(2,1)S(1)}, bf16[4,448,256]{2,1,0:T(8,128)(2,1)S(1)}, u32[]{:S(2)}, u32[]{:S(2)}) %collective-permute-start.5) | collective-permute-done | bytes 917536 | tf_op jit(solution)/shard_map/ppermute | solution.py:566
  112.2 2.4 %shard_map.188 = (f32[3,3,256]{2,1,0:T(4,128)}, f32[1,256]{1,0:T(1,128)}, f32[256,768]{1,0:T(8,128)}, f32[256,256]{1,0:T(8,128)}, f32[1,256]{1,0:T(1,128)}, /*index=5*/f32[256,1024]{1,0:T(8,128)}, f32[1024,256]{1,0:T(8,128)}) custom-call(s32[2]{0:T(128)S(1)} %pad_add_fusion.place_ref, bf16[4,448,256]{2,1,0:T(8,128)(2,1)S(1)} %bitcast.16, ...), custom_call_target="tpu_custom_call" | custom-call | flops 1000000 | bytes 5000000 | tf_op jit(solution)/shard_map/pallas_call | solution.py:545
  (1 shorter events, 0.0 us)
Async XLA Ops:
  3.4 9.5 %copy-start.9 = (bf16[3,3,256]{2,1,0:T(4,128)(2,1)S(1)}, bf16[3,3,256]{2,1,0:T(4,128)(2,1)}, u32[]{:S(2)}) copy-start(bf16[3,3,256]{2,1,0:T(4,128)(2,1)} %param.13) | copy-start | bytes 13828
  3.4 32.4 %copy-start.3 = (bf16[256,1024]{1,0:T(8,128)(2,1)S(1)}, bf16[256,1024]{1,0:T(8,128)(2,1)}, u32[]{:S(2)}) copy-start(bf16[256,1024]{1,0:T(8,128)(2,1)} %w_up_ref.1) | copy-start | bytes 1572868
  3.4 32.4 %copy-start.4 = (bf16[1024,256]{1,0:T(8,128)(2,1)S(1)}, bf16[1024,256]{1,0:T(8,128)(2,1)}, u32[]{:S(2)}) copy-start(bf16[1024,256]{1,0:T(8,128)(2,1)} %w_down_ref.1) | copy-start | bytes 1572868
  3.4 32.4 %copy-start.5 = (bf16[256,768]{1,0:T(8,128)(2,1)S(1)}, bf16[256,768]{1,0:T(8,128)(2,1)}, u32[]{:S(2)}) copy-start(bf16[256,768]{1,0:T(8,128)(2,1)} %w_qkv_ref.3) | copy-start | bytes 1179652
  3.4 32.4 %copy-start.6 = (bf16[256,256]{1,0:T(8,128)(2,1)S(1)}, bf16[256,256]{1,0:T(8,128)(2,1)}, u32[]{:S(2)}) copy-start(bf16[256,256]{1,0:T(8,128)(2,1)} %w_out_ref.1) | copy-start | bytes 393220
  3.5 32.4 %copy-start.7 = (f32[256]{0:T(256)S(1)}, f32[256]{0:T(256)}, u32[]{:S(2)}) copy-start(f32[256]{0:T(256)} %param.17) | copy-start | bytes 3076
  3.5 32.4 %copy-start.8 = (f32[256]{0:T(256)S(1)}, f32[256]{0:T(256)}, u32[]{:S(2)}) copy-start(f32[256]{0:T(256)} %param.14) | copy-start | bytes 3076
  3.5 32.3 %all-to-all-start = ((bf16[32,6,16,256]{3,2,1,0:T(8,128)(2,1)}), bf16[32,6,16,256]{3,2,1,0:T(8,128)(2,1)S(1)}, u32[]{:S(2)}, u32[]{:S(2)}) async-start(bf16[32,6,16,256]{3,2,1,0:T(8,128)(2,1)} %shard_map.179), calls=%async_computation | async-start | bytes 3145728 | tf_op jit(solution)/shard_map/all_to_all | solution.py:563
  46.9 8.9 %collective-permute-start = (bf16[1024,256]{1,0:T(8,128)(2,1)S(1)}, bf16[1024,256]{1,0:T(8,128)(2,1)S(1)}, u32[]{:S(2)}, u32[]{:S(2)}) collective-permute-start(bf16[1024,256]{1,0:T(8,128)(2,1)S(1)} %get-tuple-element.45), channel_id=1, source_target_pairs={{0,32},{32,0},{1,33},{33,1},{2,34},{34,2},{3,35},{35,3},{4,36},{36... | collective-permute-start | bytes 1572872 | tf_op jit(solution)/shard_map/ppermute | solution.py:566
  51.9 3.9 %copy-start = (bf16[320,384]{1,0:T(8,128)(2,1)S(1)}, bf16[320,384]{1,0:T(8,128)(2,1)}, u32[]{:S(2)}) copy-start(bf16[320,384]{1,0:T(8,128)(2,1)} %constant.22.clone.perm_ref) | copy-start | bytes 737284
  54.0 1.7 %collective-permute-start.1 = (bf16[528,256]{1,0:T(8,128)(2,1)S(1)}, bf16[528,256]{1,0:T(8,128)(2,1)S(1)}, u32[]{:S(2)}, u32[]{:S(2)}) collective-permute-start(bf16[528,256]{1,0:T(8,128)(2,1)S(1)} %get-tuple-element.53), channel_id=1, source_target_pairs={{0,32},{32,0},{1,33},{33,1},{2,34},{34,2},{3,35},{35,3},{4,36},{36... | collective-permute-start | bytes 811016 | tf_op jit(solution)/shard_map/ppermute | solution.py:566
  84.3 10.9 %copy-start.1 = (bf16[288,320]{1,0:T(8,128)(2,1)S(1)}, bf16[288,320]{1,0:T(8,128)(2,1)}, u32[]{:S(2)}) copy-start(bf16[288,320]{1,0:T(8,128)(2,1)} %constant.23.clone.main_ref) | copy-start | bytes 552964
  84.3 10.9 %copy-start.2 = (bf16[2,32,320]{2,1,0:T(8,128)(2,1)S(1)}, bf16[2,32,320]{2,1,0:T(8,128)(2,1)}, u32[]{:S(2)}) copy-start(bf16[2,32,320]{2,1,0:T(8,128)(2,1)} %constant.24.clone.edges_ref) | copy-start | bytes 122884
  84.3 5.8 %collective-permute-start.2 = (f32[56,256]{1,0:T(8,128)S(1)}, f32[56,256]{1,0:T(8,128)S(1)}, u32[]{:S(2)}, u32[]{:S(2)}) collective-permute-start(f32[56,256]{1,0:T(8,128)S(1)} %shard_map.184.mine_ref), channel_id=1, source_target_pairs={{0,64},{64,0},{1,65},{65,1},{2,66},{66,2},{3,67},{67,3},{4,68},{68... | collective-permute-start | bytes 172040 | tf_op jit(solution)/shard_map/ppermute | solution.py:566
  91.1 18.7 %all-to-all-start.2 = ((bf16[32,56,256]{2,1,0:T(8,128)(2,1)}), bf16[32,56,256]{2,1,0:T(8,128)(2,1)S(1)}, u32[]{:S(2)}, u32[]{:S(2)}) async-start(bf16[32,56,256]{2,1,0:T(8,128)(2,1)} %bitcast.8), calls=%async_computation.2 | async-start | bytes 1835008 | tf_op jit(solution)/shard_map/all_to_all | solution.py:563
  95.8 6.8 %collective-permute-start.3 = (bf16[32,256]{1,0:T(8,128)(2,1)S(1)}, bf16[32,256]{1,0:T(8,128)(2,1)S(1)}, u32[]{:S(2)}, u32[]{:S(2)}) collective-permute-start(bf16[32,256]{1,0:T(8,128)(2,1)S(1)} %get-tuple-element.55), channel_id=1, source_target_pairs={{0,1},{1,2},{2,3},{3,4},{4,5},{5,6},{6,7},{8,9},{9,10},{10,11},{11... | collective-permute-start | bytes 49160 | tf_op jit(solution)/shard_map/ppermute | solution.py:571
  99.5 7.1 %collective-permute-start.4 = (bf16[32,256]{1,0:T(8,128)(2,1)S(1)}, bf16[32,256]{1,0:T(8,128)(2,1)S(1)}, u32[]{:S(2)}, u32[]{:S(2)}) collective-permute-start(bf16[32,256]{1,0:T(8,128)(2,1)S(1)} %get-tuple-element.56), channel_id=1, source_target_pairs={{1,0},{2,1},{3,2},{4,3},{5,4},{6,5},{7,6},{9,8},{10,9},{11,10},{12... | collective-permute-start | bytes 49160 | tf_op jit(solution)/shard_map/ppermute | solution.py:571
  109.7 2.5 %collective-permute-start.5 = (bf16[4,448,256]{2,1,0:T(8,128)(2,1)S(1)}, bf16[4,448,256]{2,1,0:T(8,128)(2,1)S(1)}, u32[]{:S(2)}, u32[]{:S(2)}) collective-permute-start(bf16[4,448,256]{2,1,0:T(8,128)(2,1)S(1)} %bitcast.15), channel_id=1, source_target_pairs={{0,32},{32,0},{1,33},{33,1},{2,34},{34,2},{3,35},{35,3},{4,36},{36... | collective-permute-start | bytes 2752520 | tf_op jit(solution)/shard_map/ppermute | solution.py:566

commit v4 on v3

--- a/solution.py
+++ b/solution.py
@@ -204,7 +204,7 @@
 def forward_kernel(
     place_ref, x_ref, dw_ref, gain_one_ref, w_qkv_ref, w_out_ref, gain_two_ref,
     w_up_ref, w_down_ref,
-    xs_ref, in_ref, proj_ref, key_turned_ref, probs_ref, mixed_grad_ref, resid_grad_ref, keep_ref, send_ref,
+    xs_ref, in_ref, inputs_ref, proj_ref, key_turned_ref, probs_ref, mixed_grad_ref, resid_grad_ref, keep_ref, send_ref,
     out_grad_ref, gain_grad_ref,
     cot_s, mixed_s, two_s, low_s, act_s, pre_s, turned_s, mixed_turned_s,
     narrow_s, normed_s, wide_s, cot_wide_s,
@@ -231,27 +231,24 @@
 
     gain_one = gain_one_ref[...]
 
-    def conv(g, carry):
+    def conv(g):
         j, p = g // 8, g % 8
         total = xs_ref[j + 1, p + 1].astype(F32)
         for u in range(3):
             for v in range(3):
                 total = total + dw_ref[3 * u + v : 3 * u + v + 1, :] * xs_ref[j + v, p + u].astype(F32)
         start = total.astype(BF16)
-        rows = pl.ds(pl.multiple_of(g * 64, 64), 64)
+        rows = slice(64 * g, 64 * g + 64)
         in_ref[rows, :] = start
         normed, _ = norm(start.astype(F32))
-        two_s[rows, :] = (normed * gain_one).astype(BF16)
-        return carry
-
-    lax.fori_loop(0, 16, conv, 0, unroll=16)
-
-    def project(i, carry):
-        rows = pl.ds(pl.multiple_of(i * 256, 256), 256)
-        proj_ref[rows, :] = dot(two_s[rows, :], w_qkv_ref[...]).astype(BF16)
-        return carry
-
-    lax.fori_loop(0, 4, project, 0)
+        inputs_ref[rows, :] = (normed * gain_one).astype(BF16)
+
+
+    for start in range(2):
+        for g in range(8 * start, 8 * start + 8):
+            conv(g)
+        rows = slice(512 * start, 512 * start + 512)
+        proj_ref[rows, :] = dot(inputs_ref[rows, :], w_qkv_ref[...]).astype(BF16)
 
     turned_s[0:256, :] = proj_ref[:, 0:256].T
     turned_s[256:512, :] = proj_ref[:, 512:768].T
@@ -345,11 +342,11 @@
 
 
 def backward_kernel(
-    in_ref, proj_ref, key_turned_ref, probs_ref, mixed_grad_ref, resid_grad_ref, gain_one_ref,
-    w_qkv_ref,
-    proj_grad_ref, inputs_ref, grad_ref, gain_grad_ref,
+    place_ref, inputs_ref, proj_ref, key_turned_ref, probs_ref, mixed_grad_ref, out_grad_ref,
+    proj_grad_ref, keep_ref, send_ref,
     upstream_s, query_grad_s,
 ):
+    core = place_ref[1]
     upstream_s[...] = mixed_grad_ref[...].T
     mask = head_mask()
     wide_mask = mask.astype(F32)
@@ -384,37 +381,6 @@
     lax.fori_loop(0, 8 // AHEAD, attend_back, 0)
     proj_grad_ref[:, 0:256] = query_grad_s[...].T
 
-    gain_one = gain_one_ref[...]
-
-    def head(i, gain_grad):
-        rows = pl.ds(pl.multiple_of(i * 512, 512), 512)
-        normed, inverse = norm(in_ref[rows, :].astype(F32))
-        inputs_ref[rows, :] = (normed * gain_one).astype(BF16)
-        in_grad = dot_nt(proj_grad_ref[rows, :], w_qkv_ref[...])
-        grad_ref[rows, :] = resid_grad_ref[rows, :] + norm_back(in_grad, normed, inverse, gain_one)
-        return gain_grad + fold_rows(in_grad * normed)
-
-    gain_grad_ref[...] = lax.fori_loop(0, 2, head, jnp.zeros((8, C), F32), unroll=2)
-
-
-def sums_kernel(
-    place_ref, xs_ref, inputs_ref, proj_grad_ref, grad_ref, gain_one_grad_ref, gain_two_grad_ref,
-    out_grad_ref,
-    keep_ref, send_ref,
-):
-    core = place_ref[1]
-
-    def taps(g, sums):
-        j, p = g // 8, g % 8
-        grad = grad_ref[pl.ds(pl.multiple_of(g * 64, 64), 64), :]
-        return tuple(
-            sums[3 * u + v] + fold_rows(grad * xs_ref[j + v, p + u].astype(F32))
-            for u in range(3)
-            for v in range(3)
-        )
-
-    kernel_grad = lax.fori_loop(0, 16, taps, (jnp.zeros((8, C), F32),) * 9, unroll=4)
-
     inputs_turned = inputs_ref[...].T
     terms = [
         dot(inputs_turned, proj_grad_ref[:, 256 * block : 256 * block + 256])
@@ -424,21 +390,45 @@
     for block in range(2):
         rows = slice(256 * block, 256 * block + 256)
         store_halves(core, terms[block], terms[2 + block], keep_ref, send_ref, rows)
+
+
+def head_kernel(
+    xs_ref, in_ref, proj_grad_ref, resid_grad_ref, gain_two_grad_ref, gain_one_ref, w_qkv_ref,
+    grad_ref, small_ref,
+):
+    gain_one = gain_one_ref[...]
+
+    def head(i, gain_grad):
+        rows = pl.ds(pl.multiple_of(i * 512, 512), 512)
+        normed, inverse = norm(in_ref[rows, :].astype(F32))
+        in_grad = dot_nt(proj_grad_ref[rows, :], w_qkv_ref[...])
+        grad_ref[rows, :] = resid_grad_ref[rows, :] + norm_back(in_grad, normed, inverse, gain_one)
+        return gain_grad + fold_rows(in_grad * normed)
+
+    gain_grad = lax.fori_loop(0, 2, head, jnp.zeros((8, C), F32), unroll=2)
+
+    def taps(g, sums):
+        j, p = g // 8, g % 8
+        grad = grad_ref[pl.ds(pl.multiple_of(g * 64, 64), 64), :]
+        return tuple(
+            sums[3 * u + v] + fold_rows(grad * xs_ref[j + v, p + u].astype(F32))
+            for u in range(3)
+            for v in range(3)
+        )
+
+    kernel_grad = lax.fori_loop(0, 16, taps, (jnp.zeros((8, C), F32),) * 9, unroll=4)
     small = [jnp.sum(term, axis=0, keepdims=True) for term in kernel_grad]
-    small.append(jnp.sum(gain_one_grad_ref[...], axis=0, keepdims=True))
+    small.append(jnp.sum(gain_grad, axis=0, keepdims=True))
     small.append(jnp.sum(gain_two_grad_ref[...], axis=0, keepdims=True))
     small.append(jnp.zeros((5, C), F32))
-    lower, upper = jnp.concatenate(small[0:8], axis=0), jnp.concatenate(small[8:], axis=0)
-    lower, upper = (jnp.concatenate([rows, rows], axis=0) for rows in (lower, upper))
-    store_halves(core, lower, upper, keep_ref, send_ref, slice(512, 528))
+    small_ref[...] = jnp.concatenate(small, axis=0)
 
 
 def pieces_kernel(
-    grad_ref, tail_ref, other_tail_ref, head_ref, other_head_ref, perm_ref, out_ref
+    grad_ref, small_ref, tail_ref, other_tail_ref, head_ref, other_head_ref, perm_ref, out_ref
 ):
     perm = perm_ref[...]
     edge = jnp.zeros((8, C), F32)
-    small = head_ref[512:528, :].astype(F32) + other_head_ref[512:528, :].astype(F32)
     for r in range(4):
         parts = [grad_ref[64 * g + 16 * r : 64 * g + 16 * r + 16, :] for g in range(16)]
         for j in range(2):
@@ -447,7 +437,7 @@
         for j in range(2):
             highest = 64 * 8 * j + 16 * r + 16
             parts.append(grad_ref[highest : highest + 8, :] if r < 3 else edge)
-        parts.append(small[0:8] if r == 0 else edge)
+        parts.append(small_ref[8 * r : 8 * r + 8, :] if r < 2 else edge)
         parts.append(jnp.zeros((88, C), F32))
         tokens = jnp.concatenate(parts, axis=0).astype(BF16)
         moved = dot(perm, tokens).reshape(8, PIECE, C)
@@ -514,6 +504,7 @@
     kernel_ref, gain_one_ref, qkv_ref, out_ref, gain_two_ref, up_ref, down_ref,
 ):
     own = place_ref[1] == 0
+    small = []
     for r in range(4):
         mine = mine_ref[r].astype(F32).reshape(8, SHARE, C)
         other = other_ref[r].astype(F32).reshape(8, SHARE, C)
@@ -528,13 +519,13 @@
             qkv_ref[rows, 512:768] = upper[:, 32:48].reshape(128, C)
         else:
             out_ref[rows, :] = upper[:, 32:48].reshape(128, C)
-        if r == 0:
-            small = [side[c, 52:53] for side in (lower, upper) for c in range(8)]
-            small = jnp.concatenate(small, axis=0)
-            for u in range(3):
-                kernel_ref[u] = small[3 * u : 3 * u + 3]
-            gain_one_ref[...] = small[9:10]
-            gain_two_ref[...] = small[10:11]
+        if r < 2:
+            small.append((mine + other)[:, 48:56])
+    small = jnp.concatenate([part[c, 4:5] for part in small for c in range(8)], axis=0)
+    for u in range(3):
+        kernel_ref[u] = small[3 * u : 3 * u + 3]
+    gain_one_ref[...] = small[9:10]
+    gain_two_ref[...] = small[10:11]
 
 
 VMEM = pl.BlockSpec(memory_space=pltpu.VMEM)
@@ -581,12 +572,13 @@
     arrived = exchange(packed)
 
     (
-        xs, start, projected, key_turned, probs, mixed_grad, resid_grad, tail_keep, tail_send,
+        xs, start, inputs, projected, key_turned, probs, mixed_grad, resid_grad, tail_keep, tail_send,
         out_grad, gain_two_grad,
     ) = call(
         forward_kernel,
         [
             ((4, 10, 64, C), BF16),
+            ((TOKENS, C), BF16),
             ((TOKENS, C), BF16),
             ((TOKENS, 3 * C), BF16),
             ((C, TOKENS), BF16),
@@ -622,28 +614,26 @@
         limit=36,
     )
 
-    proj_grad, inputs, grad, gain_one_grad = call(
+    proj_grad, keep, send = call(
         backward_kernel,
-        [((TOKENS, 3 * C), BF16), ((TOKENS, C), BF16), ((TOKENS, C), F32), ((8, C), F32)],
-        [
-            start, projected, key_turned, probs, mixed_grad, resid_grad, gain_one.reshape(1, C), w_qkv,
-        ],
+        [((TOKENS, 3 * C), BF16), ((512, C), BF16), ((512, C), BF16)],
+        [place, inputs, projected, key_turned, probs, mixed_grad, out_grad],
         [((C, TOKENS), BF16), ((C, TOKENS), BF16)],
+        scalars=1,
         flops=5 * 10**9,
         moved=8 * 10**6,
         limit=32,
     )
-    keep, send = call(
-        sums_kernel,
-        [((528, C), BF16), ((528, C), BF16)],
-        [place, xs, inputs, proj_grad, grad, gain_one_grad, gain_two_grad, out_grad],
-        scalars=1,
+    grad, small = call(
+        head_kernel,
+        [((TOKENS, C), F32), ((16, C), F32)],
+        [xs, start, proj_grad, resid_grad, gain_two_grad, gain_one.reshape(1, C), w_qkv],
     )
     (pieces,) = call(
         pieces_kernel,
         [((4, 8 * JOINED, C), BF16)],
         [
-            grad, tail_keep, swap(tail_send, "core"), keep, swap(send, "core"),
+            grad, small, tail_keep, swap(tail_send, "core"), keep, swap(send, "core"),
             jnp.asarray(groups_to_pieces(), BF16),
         ],
     )

time: 116 us -> 113 us (0.974)
    ppermute x4, waiting for transfers between devices: 6.43 us -> 5.26 us  [swap(): return lax.ppermute(values, axis, [(0, 1), (1, 0)])]
  transfers between devices with their start and end apart: 8 -> 8, of which waited for: 7 -> 6; matrix products, arithmetic and copies ran while one was open for 0% -> 0% of each run, Pallas kernels for 8% -> 8%
where the time goes in v4:
time: 113 us; the launch traced here: 112 us
  waiting for transfers between devices  35.2 us (31%)
  blocking collectives  27.1 us (24%)
  Pallas kernels  26.5 us (23%)
  starting transfers between devices  22.3 us (20%)
    all_to_all x1, blocking collectives, exchange(): lax.all_to_all(stacked, ('row', 'col'), split_axis=0, concat_axis=0, tile...  27.1 us
    pallas_call x10, Pallas kernels, call(): pl.pallas_call(kernel, out_shape=tuple((jax.ShapeDtypeStruct(shape, dtype...  26.5 us
    all_to_all x2, waiting for transfers between devices, exchange(): lax.all_to_all(stacked, ('row', 'col'), split_axis=0, concat_axis=0, tile...  24 us
    all_to_all x2, starting transfers between devices, exchange(): lax.all_to_all(stacked, ('row', 'col'), split_axis=0, concat_axis=0, tile...  13.5 us
    ppermute x2, waiting for transfers between devices, shift(): return lax.ppermute(values, axis, pairs)  5.86 us
    ppermute x4, waiting for transfers between devices, swap(): return lax.ppermute(values, axis, [(0, 1), (1, 0)])  5.26 us
    ppermute x2, starting transfers between devices, shift(): return lax.ppermute(values, axis, pairs)  4.99 us
    ppermute x4, starting transfers between devices, swap(): return lax.ppermute(values, axis, [(0, 1), (1, 0)])  3.81 us
  transfers between devices with their start and end apart: 8, of which 6 were waited for; matrix products, arithmetic and copies ran while one was open for 0% of the time, Pallas kernels for 8%

profile of v4, /device:TPU:0, one launch (start us, length us, event | category | flops | bytes accessed | tf_op | source)
XLA Modules:
  0.0 112.0 jit_solution(11277057192004702185)
XLA Ops:
  0.6 2.8 %shard_map.179 = bf16[32,6,16,256]{3,2,1,0:T(8,128)(2,1)} custom-call(bf16[16,64,256]{2,1,0:T(8,128)(2,1)} %bitcast.20, bf16[16,64,256]{2,1,0:T(8,128)(2,1)} %bitcast.21), custom_call_target="tpu_custom_call" | custom-call | flops 400000000 | bytes 4000000 | tf_op jit(solution)/shard_map/pallas_call | solution.py:536
  3.4 0.0 copy-start.9
  3.4 0.0 copy-start
  3.4 0.0 copy-start.4
  3.4 0.0 copy-start.5
  3.4 0.0 copy-start.6
  3.5 0.0 copy-start.7
  3.5 0.0 copy-start.8
  3.5 9.4 %all-to-all-start = ((bf16[32,6,16,256]{3,2,1,0:T(8,128)(2,1)}), bf16[32,6,16,256]{3,2,1,0:T(8,128)(2,1)S(1)}, u32[]{:S(2)}, u32[]{:S(2)}) async-start(bf16[32,6,16,256]{3,2,1,0:T(8,128)(2,1)} %shard_map.179), calls=%async_computation | async-start | bytes 3145728 | tf_op jit(solution)/shard_map/all_to_all | solution.py:554
  12.9 0.0 copy-done.9
  12.9 0.1 pad_add_fusion.place_ref
  13.0 22.8 %all-to-all-done.x_ref = bf16[32,6,16,256]{3,2,1,0:T(8,128)(2,1)S(1)} async-done(((bf16[32,6,16,256]{3,2,1,0:T(8,128)(2,1)}), bf16[32,6,16,256]{3,2,1,0:T(8,128)(2,1)S(1)}, u32[]{:S(2)}, u32[]{:S(2)}) %all-to-all-start) | async-done | bytes 1572896 | tf_op jit(solution)/shard_map/all_to_all | solution.py:554
  35.8 0.0 copy-done
  35.8 0.0 copy-done.4
  35.8 0.0 copy-done.5
  35.8 0.0 copy-done.6
  35.8 0.0 copy-done.7
  35.9 0.0 copy-done.8
  35.9 10.2 %shard_map.180 = (bf16[4,10,64,256]{3,2,1,0:T(8,128)(2,1)S(1)}, bf16[1024,256]{1,0:T(8,128)(2,1)S(1)}, bf16[1024,256]{1,0:T(8,128)(2,1)S(1)}, bf16[1024,768]{1,0...) custom-call(s32[2]{0:T(128)S(1)} %pad_add_fusion.place_ref, ...), custom_call_target="tpu_custom_call" | custom-call | flops 8000000000 | bytes 12000000 | tf_op jit(solution)/shard_map/pallas_call | solution.py:536
  46.1 0.3 collective-permute-start
  46.3 4.8 %shard_map.181 = (bf16[1024,768]{1,0:T(8,128)(2,1)S(1)}, bf16[512,256]{1,0:T(8,128)(2,1)S(1)}, bf16[512,256]{1,0:T(8,128)(2,1)S(1)}) custom-call(s32[2]{0:T(128)S(1)} %pad_add_fusion.place_ref, bf16[1024,256]{1,0:T(8,128)(2,1)S(1)} %get-tuple-element.39.inputs_ref, bf16[1024,768]{1,0:T(8,128)(2,1)S(1)} %get-tuple-element.40.proj_ref, ...), custom_call_target="tpu_custom_call" | custom-call | flops 5000000000 | bytes 8000000 | tf_op jit(solution)/shard_map/pallas_call | solution.py:536
  51.1 0.6 collective-permute-start.1
  51.7 0.0 copy-start.1
  51.7 2.0 %shard_map.182 = (f32[1024,256]{1,0:T(8,128)S(1)}, f32[16,256]{1,0:T(8,128)S(1)}) custom-call(bf16[4,10,64,256]{3,2,1,0:T(8,128)(2,1)S(1)} %get-tuple-element.37.xs_ref, bf16[1024,256]{1,0:T(8,128)(2,1)S(1)} %get-tuple-element.38.in_ref, bf16[1024,768]{1,0:T(8,128)(2,1)S(1)} %get-tuple-element.45.proj_grad_ref, ...), custom_call_target="tpu_custom_call" | custom-call | tf_op jit(solution)/shard_map/pallas_call | solution.py:536
  53.7 0.0 collective-permute-done.1.other_head_ref
  53.7 0.0 collective-permute-done.other_tail_ref
  53.7 0.0 copy-done.1
  53.7 0.7 shard_map.183
  54.4 27.1 %all_to_all.15 = bf16[32,88,256]{2,1,0:T(8,128)(2,1)S(1)} all-to-all(bf16[32,88,256]{2,1,0:T(8,128)(2,1)S(1)} %bitcast.14), channel_id=1, replica_groups=mesh['yh'=2,'core'=2,'row'=4,'col'=8] {'row','col'}, dimensions={0} | all-to-all | bytes 2883584 | tf_op jit(solution)/shard_map/all_to_all | solution.py:554
  81.5 0.1 shard_map.184.mine_ref
  81.7 0.0 copy-start.2
  81.7 0.0 copy-start.3
  81.7 3.0 %collective-permute-start.2 = (f32[56,256]{1,0:T(8,128)S(1)}, f32[56,256]{1,0:T(8,128)S(1)}, u32[]{:S(2)}, u32[]{:S(2)}) collective-permute-start(f32[56,256]{1,0:T(8,128)S(1)} %shard_map.184.mine_ref), channel_id=1, source_target_pairs={{0,64},{64,0},{1,65},{65,1},{2,66},{66,2},{3,67},{67,3},{4,68},{68... | collective-permute-start | bytes 172040 | tf_op jit(solution)/shard_map/ppermute | solution.py:557
  84.7 2.8 %collective-permute-done.2.other_ref = f32[56,256]{1,0:T(8,128)S(1)} collective-permute-done((f32[56,256]{1,0:T(8,128)S(1)}, f32[56,256]{1,0:T(8,128)S(1)}, u32[]{:S(2)}, u32[]{:S(2)}) %collective-permute-start.2) | collective-permute-done | bytes 57376 | tf_op jit(solution)/shard_map/ppermute | solution.py:557
  87.4 1.0 shard_map.185
  88.4 4.1 %all-to-all-start.2 = ((bf16[32,56,256]{2,1,0:T(8,128)(2,1)}), bf16[32,56,256]{2,1,0:T(8,128)(2,1)S(1)}, u32[]{:S(2)}, u32[]{:S(2)}) async-start(bf16[32,56,256]{2,1,0:T(8,128)(2,1)} %bitcast.8), calls=%async_computation.2 | async-start | bytes 1835008 | tf_op jit(solution)/shard_map/all_to_all | solution.py:554
  92.5 0.0 copy-done.2
  92.5 0.0 copy-done.3
  92.5 0.5 shard_map.186
  93.0 3.7 %collective-permute-start.3 = (bf16[32,256]{1,0:T(8,128)(2,1)S(1)}, bf16[32,256]{1,0:T(8,128)(2,1)S(1)}, u32[]{:S(2)}, u32[]{:S(2)}) collective-permute-start(bf16[32,256]{1,0:T(8,128)(2,1)S(1)} %get-tuple-element.55), channel_id=1, source_target_pairs={{0,1},{1,2},{2,3},{3,4},{4,5},{5,6},{6,7},{8,9},{9,10},{10,11},{11... | collective-permute-start | bytes 49160 | tf_op jit(solution)/shard_map/ppermute | solution.py:562
  96.7 1.3 %collective-permute-start.4 = (bf16[32,256]{1,0:T(8,128)(2,1)S(1)}, bf16[32,256]{1,0:T(8,128)(2,1)S(1)}, u32[]{:S(2)}, u32[]{:S(2)}) collective-permute-start(bf16[32,256]{1,0:T(8,128)(2,1)S(1)} %get-tuple-element.56), channel_id=1, source_target_pairs={{1,0},{2,1},{3,2},{4,3},{5,4},{6,5},{7,6},{9,8},{10,9},{11,10},{12... | collective-permute-start | bytes 49160 | tf_op jit(solution)/shard_map/ppermute | solution.py:562
  98.0 1.2 %collective-permute-done.3.left_ref = bf16[32,256]{1,0:T(8,128)(2,1)S(1)} collective-permute-done((bf16[32,256]{1,0:T(8,128)(2,1)S(1)}, bf16[32,256]{1,0:T(8,128)(2,1)S(1)}, u32[]{:S(2)}, u32[]{:S(2)}) %collective-permute-start.3) | collective-permute-done | bytes 16416 | tf_op jit(solution)/shard_map/ppermute | solution.py:562
  99.2 4.7 %collective-permute-done.4.right_ref = bf16[32,256]{1,0:T(8,128)(2,1)S(1)} collective-permute-done((bf16[32,256]{1,0:T(8,128)(2,1)S(1)}, bf16[32,256]{1,0:T(8,128)(2,1)S(1)}, u32[]{:S(2)}, u32[]{:S(2)}) %collective-permute-start.4) | collective-permute-done | bytes 16416 | tf_op jit(solution)/shard_map/ppermute | solution.py:562
  103.9 2.0 %shard_map.187 = f32[1,16,64,256]{3,2,1,0:T(8,128)} custom-call(bf16[18,64,256]{2,1,0:T(8,128)(2,1)S(1)} %get-tuple-element.54.tile_ref, bf16[32,256]{1,0:T(8,128)(2,1)S(1)} %collective-permute-done.3.left_ref, bf16[32,256]{1,0:T(8,128)(2,1)S(1)} %collective-permute-done.4.right_ref, f32[9,256]{1,0:T(8,128)S(1)} %reshape.52.dw_ref), custom_call_target="tpu_custom_call" | custom-call | tf_op jit(solution)/shard_map/pallas_call | solution.py:536
  105.9 1.2 %all-to-all-done.2 = bf16[32,56,256]{2,1,0:T(8,128)(2,1)S(1)} async-done(((bf16[32,56,256]{2,1,0:T(8,128)(2,1)}), bf16[32,56,256]{2,1,0:T(8,128)(2,1)S(1)}, u32[]{:S(2)}, u32[]{:S(2)}) %all-to-all-start.2) | async-done | bytes 917536 | tf_op jit(solution)/shard_map/all_to_all | solution.py:554
  107.1 0.0 collective-permute-start.5
  107.1 2.5 %collective-permute-done.5.other_ref = bf16[4,448,256]{2,1,0:T(8,128)(2,1)S(1)} collective-permute-done((bf16[4,448,256]{2,1,0:T(8,128)(2,1)S(1)}, bf16[4,448,256]{2,1,0:T(8,128)(2,1)S(1)}, u32[]{:S(2)}, u32[]{:S(2)}) %collective-permute-start.5) | collective-permute-done | bytes 917536 | tf_op jit(solution)/shard_map/ppermute | solution.py:557
  109.6 2.4 %shard_map.188 = (f32[3,3,256]{2,1,0:T(4,128)}, f32[1,256]{1,0:T(1,128)}, f32[256,768]{1,0:T(8,128)}, f32[256,256]{1,0:T(8,128)}, f32[1,256]{1,0:T(1,128)}, /*index=5*/f32[256,1024]{1,0:T(8,128)}, f32[1024,256]{1,0:T(8,128)}) custom-call(s32[2]{0:T(128)S(1)} %pad_add_fusion.place_ref, bf16[4,448,256]{2,1,0:T(8,128)(2,1)S(1)} %bitcast.16, ...), custom_call_target="tpu_custom_call" | custom-call | flops 1000000 | bytes 5000000 | tf_op jit(solution)/shard_map/pallas_call | solution.py:536
  (1 shorter events, 0.0 us)
Async XLA Ops:
  3.4 9.5 %copy-start.9 = (bf16[3,3,256]{2,1,0:T(4,128)(2,1)S(1)}, bf16[3,3,256]{2,1,0:T(4,128)(2,1)}, u32[]{:S(2)}) copy-start(bf16[3,3,256]{2,1,0:T(4,128)(2,1)} %param.13) | copy-start | bytes 13828
  3.4 32.4 %copy-start = (bf16[256,768]{1,0:T(8,128)(2,1)S(1)}, bf16[256,768]{1,0:T(8,128)(2,1)}, u32[]{:S(2)}) copy-start(bf16[256,768]{1,0:T(8,128)(2,1)} %w_qkv_ref.3) | copy-start | bytes 1179652
  3.4 32.4 %copy-start.4 = (f32[256]{0:T(256)S(1)}, f32[256]{0:T(256)}, u32[]{:S(2)}) copy-start(f32[256]{0:T(256)} %param.14) | copy-start | bytes 3076
  3.4 32.4 %copy-start.5 = (bf16[256,1024]{1,0:T(8,128)(2,1)S(1)}, bf16[256,1024]{1,0:T(8,128)(2,1)}, u32[]{:S(2)}) copy-start(bf16[256,1024]{1,0:T(8,128)(2,1)} %w_up_ref.1) | copy-start | bytes 1572868
  3.4 32.4 %copy-start.6 = (bf16[1024,256]{1,0:T(8,128)(2,1)S(1)}, bf16[1024,256]{1,0:T(8,128)(2,1)}, u32[]{:S(2)}) copy-start(bf16[1024,256]{1,0:T(8,128)(2,1)} %w_down_ref.1) | copy-start | bytes 1572868
  3.5 32.4 %copy-start.7 = (bf16[256,256]{1,0:T(8,128)(2,1)S(1)}, bf16[256,256]{1,0:T(8,128)(2,1)}, u32[]{:S(2)}) copy-start(bf16[256,256]{1,0:T(8,128)(2,1)} %w_out_ref.1) | copy-start | bytes 393220
  3.5 32.4 %copy-start.8 = (f32[256]{0:T(256)S(1)}, f32[256]{0:T(256)}, u32[]{:S(2)}) copy-start(f32[256]{0:T(256)} %param.17) | copy-start | bytes 3076
  3.5 32.3 %all-to-all-start = ((bf16[32,6,16,256]{3,2,1,0:T(8,128)(2,1)}), bf16[32,6,16,256]{3,2,1,0:T(8,128)(2,1)S(1)}, u32[]{:S(2)}, u32[]{:S(2)}) async-start(bf16[32,6,16,256]{3,2,1,0:T(8,128)(2,1)} %shard_map.179), calls=%async_computation | async-start | bytes 3145728 | tf_op jit(solution)/shard_map/all_to_all | solution.py:554
  46.1 7.6 %collective-permute-start = (bf16[1024,256]{1,0:T(8,128)(2,1)S(1)}, bf16[1024,256]{1,0:T(8,128)(2,1)S(1)}, u32[]{:S(2)}, u32[]{:S(2)}) collective-permute-start(bf16[1024,256]{1,0:T(8,128)(2,1)S(1)} %get-tuple-element.51), channel_id=1, source_target_pairs={{0,32},{32,0},{1,33},{33,1},{2,34},{34,2},{3,35},{35,3},{4,36},{36... | collective-permute-start | bytes 1572872 | tf_op jit(solution)/shard_map/ppermute | solution.py:557
  51.1 2.6 %collective-permute-start.1 = (bf16[512,256]{1,0:T(8,128)(2,1)S(1)}, bf16[512,256]{1,0:T(8,128)(2,1)S(1)}, u32[]{:S(2)}, u32[]{:S(2)}) collective-permute-start(bf16[512,256]{1,0:T(8,128)(2,1)S(1)} %get-tuple-element.53), channel_id=1, source_target_pairs={{0,32},{32,0},{1,33},{33,1},{2,34},{34,2},{3,35},{35,3},{4,36},{36... | collective-permute-start | bytes 786440 | tf_op jit(solution)/shard_map/ppermute | solution.py:557
  51.7 2.0 %copy-start.1 = (bf16[320,384]{1,0:T(8,128)(2,1)S(1)}, bf16[320,384]{1,0:T(8,128)(2,1)}, u32[]{:S(2)}) copy-start(bf16[320,384]{1,0:T(8,128)(2,1)} %constant.22.clone.perm_ref) | copy-start | bytes 737284
  81.7 10.8 %copy-start.2 = (bf16[288,320]{1,0:T(8,128)(2,1)S(1)}, bf16[288,320]{1,0:T(8,128)(2,1)}, u32[]{:S(2)}) copy-start(bf16[288,320]{1,0:T(8,128)(2,1)} %constant.23.clone.main_ref) | copy-start | bytes 552964
  81.7 10.8 %copy-start.3 = (bf16[2,32,320]{2,1,0:T(8,128)(2,1)S(1)}, bf16[2,32,320]{2,1,0:T(8,128)(2,1)}, u32[]{:S(2)}) copy-start(bf16[2,32,320]{2,1,0:T(8,128)(2,1)} %constant.24.clone.edges_ref) | copy-start | bytes 122884
  81.7 5.8 %collective-permute-start.2 = (f32[56,256]{1,0:T(8,128)S(1)}, f32[56,256]{1,0:T(8,128)S(1)}, u32[]{:S(2)}, u32[]{:S(2)}) collective-permute-start(f32[56,256]{1,0:T(8,128)S(1)} %shard_map.184.mine_ref), channel_id=1, source_target_pairs={{0,64},{64,0},{1,65},{65,1},{2,66},{66,2},{3,67},{67,3},{4,68},{68... | collective-permute-start | bytes 172040 | tf_op jit(solution)/shard_map/ppermute | solution.py:557
  88.4 18.7 %all-to-all-start.2 = ((bf16[32,56,256]{2,1,0:T(8,128)(2,1)}), bf16[32,56,256]{2,1,0:T(8,128)(2,1)S(1)}, u32[]{:S(2)}, u32[]{:S(2)}) async-start(bf16[32,56,256]{2,1,0:T(8,128)(2,1)} %bitcast.8), calls=%async_computation.2 | async-start | bytes 1835008 | tf_op jit(solution)/shard_map/all_to_all | solution.py:554
  93.0 6.2 %collective-permute-start.3 = (bf16[32,256]{1,0:T(8,128)(2,1)S(1)}, bf16[32,256]{1,0:T(8,128)(2,1)S(1)}, u32[]{:S(2)}, u32[]{:S(2)}) collective-permute-start(bf16[32,256]{1,0:T(8,128)(2,1)S(1)} %get-tuple-element.55), channel_id=1, source_target_pairs={{0,1},{1,2},{2,3},{3,4},{4,5},{5,6},{6,7},{8,9},{9,10},{10,11},{11... | collective-permute-start | bytes 49160 | tf_op jit(solution)/shard_map/ppermute | solution.py:562
  96.7 7.2 %collective-permute-start.4 = (bf16[32,256]{1,0:T(8,128)(2,1)S(1)}, bf16[32,256]{1,0:T(8,128)(2,1)S(1)}, u32[]{:S(2)}, u32[]{:S(2)}) collective-permute-start(bf16[32,256]{1,0:T(8,128)(2,1)S(1)} %get-tuple-element.56), channel_id=1, source_target_pairs={{1,0},{2,1},{3,2},{4,3},{5,4},{6,5},{7,6},{9,8},{10,9},{11,10},{12... | collective-permute-start | bytes 49160 | tf_op jit(solution)/shard_map/ppermute | solution.py:562
  107.1 2.5 %collective-permute-start.5 = (bf16[4,448,256]{2,1,0:T(8,128)(2,1)S(1)}, bf16[4,448,256]{2,1,0:T(8,128)(2,1)S(1)}, u32[]{:S(2)}, u32[]{:S(2)}) collective-permute-start(bf16[4,448,256]{2,1,0:T(8,128)(2,1)S(1)} %bitcast.15), channel_id=1, source_target_pairs={{0,32},{32,0},{1,33},{33,1},{2,34},{34,2},{3,35},{35,3},{4,36},{36... | collective-permute-start | bytes 2752520 | tf_op jit(solution)/shard_map/ppermute | solution.py:557

commit v5 on v4

--- a/solution.py
+++ b/solution.py
@@ -416,7 +416,7 @@
             for v in range(3)
         )
 
-    kernel_grad = lax.fori_loop(0, 16, taps, (jnp.zeros((8, C), F32),) * 9, unroll=4)
+    kernel_grad = lax.fori_loop(0, 16, taps, (jnp.zeros((8, C), F32),) * 9, unroll=16)
     small = [jnp.sum(term, axis=0, keepdims=True) for term in kernel_grad]
     small.append(jnp.sum(gain_grad, axis=0, keepdims=True))
     small.append(jnp.sum(gain_two_grad_ref[...], axis=0, keepdims=True))
@@ -455,11 +455,11 @@
     for r in range(4):
         pieces = jnp.sum(x_ref[r].astype(F32).reshape(8, JOINED, C), axis=0)
         total = total + jnp.concatenate([pieces[PIECE:], pieces[32:40]], axis=0)
-    out_ref[...] = total * factor
+    out_ref[...] = (total * factor).astype(BF16)
 
 
 def total_kernel(mine_ref, other_ref, out_ref):
-    total = mine_ref[...] + other_ref[...]
+    total = mine_ref[...].astype(F32) + other_ref[...].astype(F32)
     rows = jnp.concatenate([total] * 8, axis=0).astype(BF16)
     for r in range(4):
         out_ref[r] = rows
@@ -499,37 +499,65 @@
     lax.fori_loop(0, 16, row, 0)
 
 
+def write_half(half, rows, qkv_ref, out_ref, up_ref, down_ref, tall, wide, sems):
+    values = rows[...].astype(F32)
+    tail = values[:, 0:32].reshape(1024, C)
+    head = values[:, 32:48].reshape(512, C)
+
+    def run(pairs):
+        copies = [pltpu.make_async_copy(*pair, sems.at[i]) for i, pair in enumerate(pairs)]
+        for copy in copies:
+            copy.start()
+        for copy in copies:
+            copy.wait()
+
+    @pl.when(half == 0)
+    def _():
+        tall[...] = tail
+        wide[:, 0:256] = head[0:256]
+        wide[:, 256:512] = head[256:512]
+        run([(tall, down_ref), (wide.at[:, 0:512], qkv_ref.at[:, 0:512])])
+
+    @pl.when(half == 1)
+    def _():
+        for block in range(4):
+            wide[:, 256 * block : 256 * block + 256] = tail[256 * block : 256 * block + 256]
+        tall[0:512, :] = head
+        run([
+            (wide, up_ref),
+            (tall.at[0:256, :], qkv_ref.at[:, 512:768]),
+            (tall.at[256:512, :], out_ref),
+        ])
+
+
+def first_outputs_kernel(place_ref, mine_ref, *refs):
+    write_half(place_ref[1], mine_ref, *refs)
+
+
 def outputs_kernel(
-    place_ref, mine_ref, other_ref,
-    kernel_ref, gain_one_ref, qkv_ref, out_ref, gain_two_ref, up_ref, down_ref,
+    place_ref, mine_ref, other_ref, qkv_in, out_in, up_in, down_in,
+    kernel_ref, gain_one_ref, gain_two_ref, qkv_ref, out_ref, up_ref, down_ref,
+    tall, wide, sems, kernel_s, gain_one_s, gain_two_s, small_sems,
 ):
-    own = place_ref[1] == 0
-    small = []
-    for r in range(4):
-        mine = mine_ref[r].astype(F32).reshape(8, SHARE, C)
-        other = other_ref[r].astype(F32).reshape(8, SHARE, C)
-        lower = jnp.where(own, mine, other)
-        upper = jnp.where(own, other, mine)
-        down_ref[256 * r : 256 * r + 256, :] = lower[:, 0:32].reshape(256, C)
-        up_ref[:, 256 * r : 256 * r + 256] = upper[:, 0:32].reshape(256, C)
-        rows = slice(128 * (r % 2), 128 * (r % 2) + 128)
-        block = r // 2
-        qkv_ref[rows, 256 * block : 256 * block + 256] = lower[:, 32:48].reshape(128, C)
-        if r < 2:
-            qkv_ref[rows, 512:768] = upper[:, 32:48].reshape(128, C)
-        else:
-            out_ref[rows, :] = upper[:, 32:48].reshape(128, C)
-        if r < 2:
-            small.append((mine + other)[:, 48:56])
-    small = jnp.concatenate([part[c, 4:5] for part in small for c in range(8)], axis=0)
+    small = mine_ref[0:16].astype(F32) + other_ref[0:16].astype(F32)
+    small = jnp.concatenate([small[k, 52:53] for k in range(16)], axis=0)
     for u in range(3):
-        kernel_ref[u] = small[3 * u : 3 * u + 3]
-    gain_one_ref[...] = small[9:10]
-    gain_two_ref[...] = small[10:11]
+        kernel_s[u] = small[3 * u : 3 * u + 3]
+    gain_one_s[...] = small[9:10]
+    gain_two_s[...] = small[10:11]
+    pairs = ((kernel_s, kernel_ref), (gain_one_s, gain_one_ref), (gain_two_s, gain_two_ref))
+    copies = [pltpu.make_async_copy(*pair, small_sems.at[i]) for i, pair in enumerate(pairs)]
+    for copy in copies:
+        copy.start()
+    half = 1 - place_ref[1]
+    write_half(half, other_ref, qkv_ref, out_ref, up_ref, down_ref, tall, wide, sems)
+    for copy in copies:
+        copy.wait()
 
 
 VMEM = pl.BlockSpec(memory_space=pltpu.VMEM)
 SMEM = pl.BlockSpec(memory_space=pltpu.SMEM)
+HBM = pl.BlockSpec(memory_space=pl.ANY)
 
 
 def call(kernel, outs, operands, scratch=(), scalars=0, flops=0, moved=0, limit=24):
@@ -641,7 +669,7 @@
     factor = 1.0 / math.sqrt(TOKENS * 128)
     (partial,) = call(
         lambda x_ref, out_ref: partial_kernel(factor, x_ref, out_ref),
-        [((SHARE, C), F32)],
+        [((SHARE, C), BF16)],
         [back],
     )
     main, edges = (jnp.asarray(t, BF16) for t in pieces_to_tile())
@@ -656,7 +684,7 @@
         [((4, 8 * SHARE, C), BF16)],
         [partial, swap(partial, "yh")],
     )
-    mine = exchange(shared.reshape(32, SHARE, C)).reshape(4, 8 * SHARE, C)
+    mine = exchange(shared.reshape(32, SHARE, C))
     (input_grad,) = call(
         tile_kernel,
         [((1, 16, 64, C), F32)],
@@ -665,22 +693,29 @@
     )
     mine, input_grad = lax.optimization_barrier((mine, input_grad))
     other = swap(mine, "core")
-    kernel_grad, gain_one_grad, qkv_grad, out_sum, gain_two_sum, up_grad, down_grad = call(
+    large = tuple(jax.ShapeDtypeStruct(n, F32) for n in ((C, 3 * C), (C, C), (C, FF), (FF, C)))
+    small = tuple(jax.ShapeDtypeStruct(n, F32) for n in ((3, 3, C), (1, C), (1, C)))
+    scratch = [pltpu.VMEM((FF, C), F32), pltpu.VMEM((C, FF), F32), pltpu.SemaphoreType.DMA((3,))]
+    settings = dict(compiler_params=pltpu.CompilerParams(vmem_limit_bytes=24 * 2**20))
+    begun = pl.pallas_call(
+        first_outputs_kernel,
+        out_shape=large,
+        in_specs=[SMEM, VMEM],
+        out_specs=(HBM,) * 4,
+        scratch_shapes=scratch,
+        **settings,
+    )(place, mine)
+    kernel_grad, gain_one_grad, gain_two_sum, qkv_grad, out_sum, up_grad, down_grad = pl.pallas_call(
         outputs_kernel,
-        [
-            ((3, 3, C), F32),
-            ((1, C), F32),
-            ((C, 3 * C), F32),
-            ((C, C), F32),
-            ((1, C), F32),
-            ((C, FF), F32),
-            ((FF, C), F32),
-        ],
-        [place, mine, other],
-        scalars=1,
-        flops=10**6,
-        moved=5 * 10**6,
-    )
+        out_shape=small + large,
+        in_specs=[SMEM, VMEM, VMEM] + [HBM] * 4,
+        out_specs=(HBM,) * 7,
+        scratch_shapes=scratch
+        + [pltpu.VMEM(part.shape, F32) for part in small]
+        + [pltpu.SemaphoreType.DMA((3,))],
+        input_output_aliases={3: 3, 4: 4, 5: 5, 6: 6},
+        **settings,
+    )(place, mine, other, *begun)
     return (
         input_grad,
         kernel_grad,

time: 113 us -> 113 us (level)
  waiting for transfers between devices: 35.2 us -> 33 us
    pallas_call x0 -> x2, Pallas kernels: none -> 3.68 us  [the longest x1 1.86 us: local(): pl.pallas_call(outputs_kernel, out_shape=small + large, in_specs=[SMEM, V...]
    pallas_call x10 -> x9, Pallas kernels: 26.5 us -> 23.9 us  [call(): pl.pallas_call(kernel, out_shape=tuple((jax.ShapeDtypeStruct(shape, dtype...]
    ppermute x4, waiting for transfers between devices: 5.26 us -> 3.13 us  [swap(): return lax.ppermute(values, axis, [(0, 1), (1, 0)])]
  transfers between devices with their start and end apart: 8 -> 8, of which waited for: 6 -> 6; matrix products, arithmetic and copies ran while one was open for 0% -> 0% of each run, Pallas kernels for 8% -> 10%
where the time goes in v5:
time: 113 us; the launch traced here: 111 us
  waiting for transfers between devices  33 us (29%)
  Pallas kernels  27.6 us (24%)
  blocking collectives  27.1 us (24%)
  starting transfers between devices  22.3 us (20%)
    all_to_all x1, blocking collectives, exchange(): lax.all_to_all(stacked, ('row', 'col'), split_axis=0, concat_axis=0, tile...  27.1 us
    all_to_all x2, waiting for transfers between devices, exchange(): lax.all_to_all(stacked, ('row', 'col'), split_axis=0, concat_axis=0, tile...  24 us
    pallas_call x9, Pallas kernels, call(): pl.pallas_call(kernel, out_shape=tuple((jax.ShapeDtypeStruct(shape, dtype...  23.9 us
    all_to_all x2, starting transfers between devices, exchange(): lax.all_to_all(stacked, ('row', 'col'), split_axis=0, concat_axis=0, tile...  13.5 us
    ppermute x2, waiting for transfers between devices, shift(): return lax.ppermute(values, axis, pairs)  5.86 us
    ppermute x2, starting transfers between devices, shift(): return lax.ppermute(values, axis, pairs)  4.99 us
    ppermute x4, starting transfers between devices, swap(): return lax.ppermute(values, axis, [(0, 1), (1, 0)])  3.81 us
    ppermute x4, waiting for transfers between devices, swap(): return lax.ppermute(values, axis, [(0, 1), (1, 0)])  3.13 us
  transfers between devices with their start and end apart: 8, of which 6 were waited for; matrix products, arithmetic and copies ran while one was open for 0% of the time, Pallas kernels for 10%

profile of v5, /device:TPU:0, one launch (start us, length us, event | category | flops | bytes accessed | tf_op | source)
XLA Modules:
  0.0 111.2 jit_solution(16458246600408427037)
XLA Ops:
  0.6 2.8 %shard_map.179 = bf16[32,6,16,256]{3,2,1,0:T(8,128)(2,1)} custom-call(bf16[16,64,256]{2,1,0:T(8,128)(2,1)} %bitcast.17, bf16[16,64,256]{2,1,0:T(8,128)(2,1)} %bitcast.18), custom_call_target="tpu_custom_call" | custom-call | flops 400000000 | bytes 4000000 | tf_op jit(solution)/shard_map/pallas_call | solution.py:564
  3.4 0.0 copy-start.9
  3.4 0.0 copy-start
  3.5 0.0 copy-start.4
  3.5 0.0 copy-start.5
  3.5 0.0 copy-start.6
  3.5 0.0 copy-start.7
  3.5 0.0 copy-start.8
  3.5 9.4 %all-to-all-start = ((bf16[32,6,16,256]{3,2,1,0:T(8,128)(2,1)}), bf16[32,6,16,256]{3,2,1,0:T(8,128)(2,1)S(1)}, u32[]{:S(2)}, u32[]{:S(2)}) async-start(bf16[32,6,16,256]{3,2,1,0:T(8,128)(2,1)} %shard_map.179), calls=%async_computation | async-start | bytes 3145728 | tf_op jit(solution)/shard_map/all_to_all | solution.py:582
  12.9 0.0 copy-done.9
  12.9 0.1 pad_add_fusion.place_ref
  13.0 22.8 %all-to-all-done.x_ref = bf16[32,6,16,256]{3,2,1,0:T(8,128)(2,1)S(1)} async-done(((bf16[32,6,16,256]{3,2,1,0:T(8,128)(2,1)}), bf16[32,6,16,256]{3,2,1,0:T(8,128)(2,1)S(1)}, u32[]{:S(2)}, u32[]{:S(2)}) %all-to-all-start) | async-done | bytes 1572896 | tf_op jit(solution)/shard_map/all_to_all | solution.py:582
  35.8 0.0 copy-done
  35.8 0.0 copy-done.4
  35.8 0.0 copy-done.5
  35.8 0.0 copy-done.6
  35.9 0.0 copy-done.7
  35.9 0.0 copy-done.8
  35.9 10.2 %shard_map.180 = (bf16[4,10,64,256]{3,2,1,0:T(8,128)(2,1)S(1)}, bf16[1024,256]{1,0:T(8,128)(2,1)S(1)}, bf16[1024,256]{1,0:T(8,128)(2,1)S(1)}, bf16[1024,768]{1,0...) custom-call(s32[2]{0:T(128)S(1)} %pad_add_fusion.place_ref, ...), custom_call_target="tpu_custom_call" | custom-call | flops 8000000000 | bytes 12000000 | tf_op jit(solution)/shard_map/pallas_call | solution.py:564
  46.1 0.3 collective-permute-start
  46.3 4.8 %shard_map.181 = (bf16[1024,768]{1,0:T(8,128)(2,1)S(1)}, bf16[512,256]{1,0:T(8,128)(2,1)S(1)}, bf16[512,256]{1,0:T(8,128)(2,1)S(1)}) custom-call(s32[2]{0:T(128)S(1)} %pad_add_fusion.place_ref, bf16[1024,256]{1,0:T(8,128)(2,1)S(1)} %get-tuple-element.43.inputs_ref, bf16[1024,768]{1,0:T(8,128)(2,1)S(1)} %get-tuple-element.44.proj_ref, ...), custom_call_target="tpu_custom_call" | custom-call | flops 5000000000 | bytes 8000000 | tf_op jit(solution)/shard_map/pallas_call | solution.py:564
  51.1 0.6 collective-permute-start.1
  51.7 1.9 %shard_map.182 = (f32[1024,256]{1,0:T(8,128)S(1)}, f32[16,256]{1,0:T(8,128)S(1)}) custom-call(bf16[4,10,64,256]{3,2,1,0:T(8,128)(2,1)S(1)} %get-tuple-element.41.xs_ref, bf16[1024,256]{1,0:T(8,128)(2,1)S(1)} %get-tuple-element.42.in_ref, bf16[1024,768]{1,0:T(8,128)(2,1)S(1)} %get-tuple-element.49.proj_grad_ref, ...), custom_call_target="tpu_custom_call" | custom-call | tf_op jit(solution)/shard_map/pallas_call | solution.py:564
  53.6 0.0 collective-permute-done.1.other_head_ref
  53.6 0.0 collective-permute-done.other_tail_ref
  53.6 0.0 copy-done.1
  53.6 0.7 shard_map.183
  54.3 27.1 %all_to_all.15 = bf16[32,88,256]{2,1,0:T(8,128)(2,1)S(1)} all-to-all(bf16[32,88,256]{2,1,0:T(8,128)(2,1)S(1)} %bitcast.13), channel_id=1, replica_groups=mesh['yh'=2,'core'=2,'row'=4,'col'=8] {'row','col'}, dimensions={0} | all-to-all | bytes 2883584 | tf_op jit(solution)/shard_map/all_to_all | solution.py:582
  81.4 0.1 shard_map.184.mine_ref
  81.5 0.0 copy-start.2
  81.6 0.0 copy-start.3
  81.6 3.0 %collective-permute-start.2 = (bf16[56,256]{1,0:T(8,128)(2,1)S(1)}, bf16[56,256]{1,0:T(8,128)(2,1)S(1)}, u32[]{:S(2)}, u32[]{:S(2)}) collective-permute-start(bf16[56,256]{1,0:T(8,128)(2,1)S(1)} %shard_map.184.mine_ref), channel_id=1, source_target_pairs={{0,64},{64,0},{1,65},{65,1},{2,66},{66,2},{3,67},{67,3},{4,68},{68... | collective-permute-start | bytes 86024 | tf_op jit(solution)/shard_map/ppermute | solution.py:585
  84.5 2.5 %collective-permute-done.2.other_ref = bf16[56,256]{1,0:T(8,128)(2,1)S(1)} collective-permute-done((bf16[56,256]{1,0:T(8,128)(2,1)S(1)}, bf16[56,256]{1,0:T(8,128)(2,1)S(1)}, u32[]{:S(2)}, u32[]{:S(2)}) %collective-permute-start.2) | collective-permute-done | bytes 28704 | tf_op jit(solution)/shard_map/ppermute | solution.py:585
  87.0 1.0 shard_map.185
  88.0 4.1 %all-to-all-start.2 = ((bf16[32,56,256]{2,1,0:T(8,128)(2,1)}), bf16[32,56,256]{2,1,0:T(8,128)(2,1)S(1)}, u32[]{:S(2)}, u32[]{:S(2)}) async-start(bf16[32,56,256]{2,1,0:T(8,128)(2,1)} %bitcast.8), calls=%async_computation.2 | async-start | bytes 1835008 | tf_op jit(solution)/shard_map/all_to_all | solution.py:582
  92.1 0.0 copy-done.2
  92.1 0.0 copy-done.3
  92.1 0.5 shard_map.186
  92.6 3.7 %collective-permute-start.3 = (bf16[32,256]{1,0:T(8,128)(2,1)S(1)}, bf16[32,256]{1,0:T(8,128)(2,1)S(1)}, u32[]{:S(2)}, u32[]{:S(2)}) collective-permute-start(bf16[32,256]{1,0:T(8,128)(2,1)S(1)} %get-tuple-element.59), channel_id=1, source_target_pairs={{0,1},{1,2},{2,3},{3,4},{4,5},{5,6},{6,7},{8,9},{9,10},{10,11},{11... | collective-permute-start | bytes 49160 | tf_op jit(solution)/shard_map/ppermute | solution.py:590
  96.3 1.3 %collective-permute-start.4 = (bf16[32,256]{1,0:T(8,128)(2,1)S(1)}, bf16[32,256]{1,0:T(8,128)(2,1)S(1)}, u32[]{:S(2)}, u32[]{:S(2)}) collective-permute-start(bf16[32,256]{1,0:T(8,128)(2,1)S(1)} %get-tuple-element.60), channel_id=1, source_target_pairs={{1,0},{2,1},{3,2},{4,3},{5,4},{6,5},{7,6},{9,8},{10,9},{11,10},{12... | collective-permute-start | bytes 49160 | tf_op jit(solution)/shard_map/ppermute | solution.py:590
  97.6 1.2 %collective-permute-done.3.left_ref = bf16[32,256]{1,0:T(8,128)(2,1)S(1)} collective-permute-done((bf16[32,256]{1,0:T(8,128)(2,1)S(1)}, bf16[32,256]{1,0:T(8,128)(2,1)S(1)}, u32[]{:S(2)}, u32[]{:S(2)}) %collective-permute-start.3) | collective-permute-done | bytes 16416 | tf_op jit(solution)/shard_map/ppermute | solution.py:590
  98.8 4.7 %collective-permute-done.4.right_ref = bf16[32,256]{1,0:T(8,128)(2,1)S(1)} collective-permute-done((bf16[32,256]{1,0:T(8,128)(2,1)S(1)}, bf16[32,256]{1,0:T(8,128)(2,1)S(1)}, u32[]{:S(2)}, u32[]{:S(2)}) %collective-permute-start.4) | collective-permute-done | bytes 16416 | tf_op jit(solution)/shard_map/ppermute | solution.py:590
  103.5 2.0 %shard_map.187 = f32[1,16,64,256]{3,2,1,0:T(8,128)} custom-call(bf16[18,64,256]{2,1,0:T(8,128)(2,1)S(1)} %get-tuple-element.58.tile_ref, bf16[32,256]{1,0:T(8,128)(2,1)S(1)} %collective-permute-done.3.left_ref, bf16[32,256]{1,0:T(8,128)(2,1)S(1)} %collective-permute-done.4.right_ref, f32[9,256]{1,0:T(8,128)S(1)} %reshape.48.dw_ref), custom_call_target="tpu_custom_call" | custom-call | tf_op jit(solution)/shard_map/pallas_call | solution.py:564
  105.5 1.2 %all-to-all-done.2.mine_ref = bf16[32,56,256]{2,1,0:T(8,128)(2,1)S(1)} async-done(((bf16[32,56,256]{2,1,0:T(8,128)(2,1)}), bf16[32,56,256]{2,1,0:T(8,128)(2,1)S(1)}, u32[]{:S(2)}, u32[]{:S(2)}) %all-to-all-start.2) | async-done | bytes 917536 | tf_op jit(solution)/shard_map/all_to_all | solution.py:582
  106.7 0.0 collective-permute-start.5
  106.7 1.8 %shard_map.188 = (f32[256,768]{1,0:T(8,128)}, f32[256,256]{1,0:T(8,128)}, f32[256,1024]{1,0:T(8,128)}, f32[1024,256]{1,0:T(8,128)}) custom-call(s32[2]{0:T(128)S(1)} %pad_add_fusion.place_ref, bf16[32,56,256]{2,1,0:T(8,128)(2,1)S(1)} %all-to-all-done.2.mine_ref), custom_call_target="tpu_custom_call" | custom-call | tf_op jit(solution)/shard_map/pallas_call | solution.py:700
  108.5 0.6 collective-permute-done.5.other_ref
  109.2 1.9 %shard_map.189 = (f32[3,3,256]{2,1,0:T(4,128)}, f32[1,256]{1,0:T(1,128)}, f32[1,256]{1,0:T(1,128)}, f32[256,768]{1,0:T(8,128)}, f32[256,256]{1,0:T(8,128)}, /*index=5*/f32[256,1024]{1,0:T(8,128)}, f32[1024,256]{1,0:T(8,128)}) custom-call(s32[2]{0:T(128)S(1)} %pad_add_fusion.place_ref, ...), custom_call_target="tpu_custom_call", output_to_operand_aliasing={{3}: (3, {}), {4}: (4, {}), {5}: (5, {}), {6}: (6, {})} | custom-call | tf_op jit(solution)/shard_map/pallas_call | solution.py:708
  (2 shorter events, 0.0 us)
Async XLA Ops:
  3.4 9.5 %copy-start.9 = (bf16[3,3,256]{2,1,0:T(4,128)(2,1)S(1)}, bf16[3,3,256]{2,1,0:T(4,128)(2,1)}, u32[]{:S(2)}) copy-start(bf16[3,3,256]{2,1,0:T(4,128)(2,1)} %param.13) | copy-start | bytes 13828
  3.4 32.4 %copy-start = (bf16[256,768]{1,0:T(8,128)(2,1)S(1)}, bf16[256,768]{1,0:T(8,128)(2,1)}, u32[]{:S(2)}) copy-start(bf16[256,768]{1,0:T(8,128)(2,1)} %w_qkv_ref.3) | copy-start | bytes 1179652
  3.5 32.4 %copy-start.4 = (f32[256]{0:T(256)S(1)}, f32[256]{0:T(256)}, u32[]{:S(2)}) copy-start(f32[256]{0:T(256)} %param.14) | copy-start | bytes 3076
  3.5 32.4 %copy-start.5 = (bf16[256,1024]{1,0:T(8,128)(2,1)S(1)}, bf16[256,1024]{1,0:T(8,128)(2,1)}, u32[]{:S(2)}) copy-start(bf16[256,1024]{1,0:T(8,128)(2,1)} %w_up_ref.1) | copy-start | bytes 1572868
  3.5 32.4 %copy-start.6 = (bf16[1024,256]{1,0:T(8,128)(2,1)S(1)}, bf16[1024,256]{1,0:T(8,128)(2,1)}, u32[]{:S(2)}) copy-start(bf16[1024,256]{1,0:T(8,128)(2,1)} %w_down_ref.1) | copy-start | bytes 1572868
  3.5 32.4 %copy-start.7 = (bf16[256,256]{1,0:T(8,128)(2,1)S(1)}, bf16[256,256]{1,0:T(8,128)(2,1)}, u32[]{:S(2)}) copy-start(bf16[256,256]{1,0:T(8,128)(2,1)} %w_out_ref.1) | copy-start | bytes 393220
  3.5 32.4 %copy-start.8 = (f32[256]{0:T(256)S(1)}, f32[256]{0:T(256)}, u32[]{:S(2)}) copy-start(f32[256]{0:T(256)} %param.17) | copy-start | bytes 3076
  3.5 32.3 %all-to-all-start = ((bf16[32,6,16,256]{3,2,1,0:T(8,128)(2,1)}), bf16[32,6,16,256]{3,2,1,0:T(8,128)(2,1)S(1)}, u32[]{:S(2)}, u32[]{:S(2)}) async-start(bf16[32,6,16,256]{3,2,1,0:T(8,128)(2,1)} %shard_map.179), calls=%async_computation | async-start | bytes 3145728 | tf_op jit(solution)/shard_map/all_to_all | solution.py:582
  46.1 7.5 %collective-permute-start = (bf16[1024,256]{1,0:T(8,128)(2,1)S(1)}, bf16[1024,256]{1,0:T(8,128)(2,1)S(1)}, u32[]{:S(2)}, u32[]{:S(2)}) collective-permute-start(bf16[1024,256]{1,0:T(8,128)(2,1)S(1)} %get-tuple-element.55), channel_id=1, source_target_pairs={{0,32},{32,0},{1,33},{33,1},{2,34},{34,2},{3,35},{35,3},{4,36},{36... | collective-permute-start | bytes 1572872 | tf_op jit(solution)/shard_map/ppermute | solution.py:585
  51.1 2.5 %collective-permute-start.1 = (bf16[512,256]{1,0:T(8,128)(2,1)S(1)}, bf16[512,256]{1,0:T(8,128)(2,1)S(1)}, u32[]{:S(2)}, u32[]{:S(2)}) collective-permute-start(bf16[512,256]{1,0:T(8,128)(2,1)S(1)} %get-tuple-element.57), channel_id=1, source_target_pairs={{0,32},{32,0},{1,33},{33,1},{2,34},{34,2},{3,35},{35,3},{4,36},{36... | collective-permute-start | bytes 786440 | tf_op jit(solution)/shard_map/ppermute | solution.py:585
  51.7 1.9 %copy-start.1 = (bf16[320,384]{1,0:T(8,128)(2,1)S(1)}, bf16[320,384]{1,0:T(8,128)(2,1)}, u32[]{:S(2)}) copy-start(bf16[320,384]{1,0:T(8,128)(2,1)} %constant.22.clone.perm_ref) | copy-start | bytes 737284
  81.5 10.5 %copy-start.2 = (bf16[288,320]{1,0:T(8,128)(2,1)S(1)}, bf16[288,320]{1,0:T(8,128)(2,1)}, u32[]{:S(2)}) copy-start(bf16[288,320]{1,0:T(8,128)(2,1)} %constant.23.clone.main_ref) | copy-start | bytes 552964
  81.6 10.5 %copy-start.3 = (bf16[2,32,320]{2,1,0:T(8,128)(2,1)S(1)}, bf16[2,32,320]{2,1,0:T(8,128)(2,1)}, u32[]{:S(2)}) copy-start(bf16[2,32,320]{2,1,0:T(8,128)(2,1)} %constant.24.clone.edges_ref) | copy-start | bytes 122884
  81.6 5.5 %collective-permute-start.2 = (bf16[56,256]{1,0:T(8,128)(2,1)S(1)}, bf16[56,256]{1,0:T(8,128)(2,1)S(1)}, u32[]{:S(2)}, u32[]{:S(2)}) collective-permute-start(bf16[56,256]{1,0:T(8,128)(2,1)S(1)} %shard_map.184.mine_ref), channel_id=1, source_target_pairs={{0,64},{64,0},{1,65},{65,1},{2,66},{66,2},{3,67},{67,3},{4,68},{68... | collective-permute-start | bytes 86024 | tf_op jit(solution)/shard_map/ppermute | solution.py:585
  88.0 18.7 %all-to-all-start.2 = ((bf16[32,56,256]{2,1,0:T(8,128)(2,1)}), bf16[32,56,256]{2,1,0:T(8,128)(2,1)S(1)}, u32[]{:S(2)}, u32[]{:S(2)}) async-start(bf16[32,56,256]{2,1,0:T(8,128)(2,1)} %bitcast.8), calls=%async_computation.2 | async-start | bytes 1835008 | tf_op jit(solution)/shard_map/all_to_all | solution.py:582
  92.6 6.2 %collective-permute-start.3 = (bf16[32,256]{1,0:T(8,128)(2,1)S(1)}, bf16[32,256]{1,0:T(8,128)(2,1)S(1)}, u32[]{:S(2)}, u32[]{:S(2)}) collective-permute-start(bf16[32,256]{1,0:T(8,128)(2,1)S(1)} %get-tuple-element.59), channel_id=1, source_target_pairs={{0,1},{1,2},{2,3},{3,4},{4,5},{5,6},{6,7},{8,9},{9,10},{10,11},{11... | collective-permute-start | bytes 49160 | tf_op jit(solution)/shard_map/ppermute | solution.py:590
  96.3 7.2 %collective-permute-start.4 = (bf16[32,256]{1,0:T(8,128)(2,1)S(1)}, bf16[32,256]{1,0:T(8,128)(2,1)S(1)}, u32[]{:S(2)}, u32[]{:S(2)}) collective-permute-start(bf16[32,256]{1,0:T(8,128)(2,1)S(1)} %get-tuple-element.60), channel_id=1, source_target_pairs={{1,0},{2,1},{3,2},{4,3},{5,4},{6,5},{7,6},{9,8},{10,9},{11,10},{12... | collective-permute-start | bytes 49160 | tf_op jit(solution)/shard_map/ppermute | solution.py:590
  106.7 2.5 %collective-permute-start.5 = (bf16[32,56,256]{2,1,0:T(8,128)(2,1)S(1)}, bf16[32,56,256]{2,1,0:T(8,128)(2,1)S(1)}, u32[]{:S(2)}, u32[]{:S(2)}) collective-permute-start(bf16[32,56,256]{2,1,0:T(8,128)(2,1)S(1)} %all-to-all-done.2.mine_ref), channel_id=1, source_target_pairs={{0,32},{32,0},{1,33},{33,1},{2,34},{34,2},{3,35},{35,3},{4,36},{36... | collective-permute-start | bytes 2752520 | tf_op jit(solution)/shard_map/ppermute | solution.py:585

commit v6 on v5

--- a/solution.py
+++ b/solution.py
@@ -22,7 +22,7 @@
 HEAD_SCALE = 1.0 / math.sqrt(C // HEADS)
 TOKENS = 1024
 AHEAD = 8
-CHUNK = 1024
+CHUNK = 512
 ROWS = 64
 SPAN = 16
 
@@ -286,25 +286,28 @@
 
     gain_two = gain_two_ref[...]
 
-    def tail(i, gain_grad):
-        rows = pl.ds(pl.multiple_of(i * CHUNK, CHUNK), CHUNK)
-        narrow_s[...] = dot(mixed_s[rows, :], w_out_ref[...])
-        inverses = []
-        for n in range(CHUNK // ROWS):
-            part = slice(ROWS * n, ROWS * n + ROWS)
-            own = pl.ds(pl.multiple_of(i * CHUNK + ROWS * n, ROWS), ROWS)
-            normed, inverse = norm(in_ref[own, :].astype(F32) + narrow_s[part, :])
-            inverses.append(inverse)
-            normed_s[part, :] = normed
+    inverses = {}
+
+    def resid_part(start):
+        rows = slice(start, start + CHUNK)
+        narrow_s[rows, :] = dot(mixed_s[rows, :], w_out_ref[...])
+        for first in range(start, start + CHUNK, ROWS):
+            own = slice(first, first + ROWS)
+            normed, inverses[first] = norm(in_ref[own, :].astype(F32) + narrow_s[own, :])
+            normed_s[own, :] = normed
             two_s[own, :] = (normed * gain_two).astype(BF16)
-        wide_s[...] = dot(two_s[rows, :], w_up_ref[...])
-        cot_wide_s[...] = dot_nt(cot_s[rows, :], w_down_ref[...])
-        for n in range(CHUNK // SPAN):
-            part = slice(SPAN * n, SPAN * n + SPAN)
-            own = pl.ds(pl.multiple_of(i * CHUNK + SPAN * n, SPAN), SPAN)
+
+    def wide_part(start):
+        rows = slice(start, start + CHUNK)
+        wide_s[rows, :] = dot(two_s[rows, :], w_up_ref[...])
+        cot_wide_s[rows, :] = dot_nt(cot_s[rows, :], w_down_ref[...])
+
+    def gelu_part(start):
+        for first in range(start, start + CHUNK, SPAN):
+            own = slice(first, first + SPAN)
             for block in range(4):
                 columns = slice(256 * block, 256 * block + 256)
-                pre = wide_s[part, columns]
+                pre = wide_s[own, columns]
                 square = pre * pre
                 tangent = jnp.tanh(pre * (gelu_coef + (gelu_coef * cubic_coef) * square))
                 half = 0.5 + 0.5 * tangent
@@ -313,24 +316,42 @@
                 slope = half + (act - act * half) * (
                     2.0 * gelu_coef + (6.0 * gelu_coef * cubic_coef) * square
                 )
-                pre_s[own, columns] = (cot_wide_s[part, columns] * slope).astype(BF16)
-        narrow_s[...] = dot_nt(pre_s[rows, :], w_up_ref[...])
-        for n in range(CHUNK // ROWS):
-            part = slice(ROWS * n, ROWS * n + ROWS)
-            own = pl.ds(pl.multiple_of(i * CHUNK + ROWS * n, ROWS), ROWS)
-            in_grad = narrow_s[part, :]
-            normed = normed_s[part, :]
-            back = norm_back(in_grad, normed, inverses[n], gain_two)
+                pre_s[own, columns] = (cot_wide_s[own, columns] * slope).astype(BF16)
+
+    def narrow_part(start):
+        rows = slice(start, start + CHUNK)
+        narrow_s[rows, :] = dot_nt(pre_s[rows, :], w_up_ref[...])
+
+    def back_part(start, gain_grad):
+        for first in range(start, start + CHUNK, ROWS):
+            own = slice(first, first + ROWS)
+            in_grad = narrow_s[own, :]
+            normed = normed_s[own, :]
+            back = norm_back(in_grad, normed, inverses[first], gain_two)
             resid_grad = cot_s[own, :].astype(F32) + back
             resid_grad_ref[own, :] = resid_grad
             low_s[own, :] = resid_grad.astype(BF16)
             gain_grad = gain_grad + fold_rows(in_grad * normed)
+        return gain_grad
+
+    def last_part(start):
+        rows = slice(start, start + CHUNK)
         mixed_grad_ref[rows, :] = dot_nt(low_s[rows, :], w_out_ref[...]).astype(BF16)
-        return gain_grad
-
-    gain_grad = lax.fori_loop(0, TOKENS // CHUNK, tail, jnp.zeros((8, C), F32))
-    gain_grad_ref[...] = gain_grad
-
+
+    gain_grad = jnp.zeros((8, C), F32)
+    starts = list(range(0, TOKENS, CHUNK))
+    steps = len(starts)
+    resid_part(starts[0])
+    wide_part(starts[0])
+    for n in range(steps):
+        if n + 1 < steps:
+            resid_part(starts[n + 1])
+            wide_part(starts[n + 1])
+        gelu_part(starts[n])
+        narrow_part(starts[n])
+        if n > 0:
+            gain_grad = back_part(starts[n - 1], gain_grad)
+            last_part(starts[n - 1])
     cot_turned = cot_s[...].T
     two_turned = two_s[...].T
     for block in range(4):
@@ -338,6 +359,10 @@
         down = dot(cot_turned, act_s[:, columns]).T
         up = dot(two_turned, pre_s[:, columns])
         store_halves(core, down, up, keep_ref, send_ref, slice(256 * block, 256 * block + 256))
+    gain_grad = back_part(starts[-1], gain_grad)
+    last_part(starts[-1])
+    gain_grad_ref[...] = gain_grad
+
     out_grad_ref[...] = dot(mixed_turned_s[...], low_s[...])
 
 
@@ -631,10 +656,10 @@
             ((TOKENS, FF), BF16),
             ((2 * C, TOKENS), BF16),
             ((C, TOKENS), BF16),
-            ((CHUNK, C), F32),
-            ((CHUNK, C), F32),
-            ((CHUNK, FF), F32),
-            ((CHUNK, FF), F32),
+            ((TOKENS, C), F32),
+            ((TOKENS, C), F32),
+            ((TOKENS, FF), F32),
+            ((TOKENS, FF), F32),
         ],
         scalars=1,
         flops=8 * 10**9,

time: 113 us -> 112 us (level)
  no operation moved by 1% of the time
where the time goes in v6:
time: 112 us; the launch traced here: 111 us
  waiting for transfers between devices  33 us (29%)
  blocking collectives  27.1 us (24%)
  Pallas kernels  27 us (24%)
  starting transfers between devices  22.3 us (20%)
    all_to_all x1, blocking collectives, exchange(): lax.all_to_all(stacked, ('row', 'col'), split_axis=0, concat_axis=0, tile...  27.1 us
    all_to_all x2, waiting for transfers between devices, exchange(): lax.all_to_all(stacked, ('row', 'col'), split_axis=0, concat_axis=0, tile...  24 us
    pallas_call x9, Pallas kernels, call(): pl.pallas_call(kernel, out_shape=tuple((jax.ShapeDtypeStruct(shape, dtype...  23.3 us
    all_to_all x2, starting transfers between devices, exchange(): lax.all_to_all(stacked, ('row', 'col'), split_axis=0, concat_axis=0, tile...  13.5 us
    ppermute x2, waiting for transfers between devices, shift(): return lax.ppermute(values, axis, pairs)  5.86 us
    ppermute x2, starting transfers between devices, shift(): return lax.ppermute(values, axis, pairs)  4.99 us
    ppermute x4, starting transfers between devices, swap(): return lax.ppermute(values, axis, [(0, 1), (1, 0)])  3.81 us
    ppermute x4, waiting for transfers between devices, swap(): return lax.ppermute(values, axis, [(0, 1), (1, 0)])  3.13 us
  transfers between devices with their start and end apart: 8, of which 6 were waited for; matrix products, arithmetic and copies ran while one was open for 0% of the time, Pallas kernels for 10%

profile of v6, /device:TPU:0, one launch (start us, length us, event | category | flops | bytes accessed | tf_op | source)
XLA Modules:
  0.0 110.6 jit_solution(16721127575609129095)
XLA Ops:
  0.6 2.8 %shard_map.179 = bf16[32,6,16,256]{3,2,1,0:T(8,128)(2,1)} custom-call(bf16[16,64,256]{2,1,0:T(8,128)(2,1)} %bitcast.17, bf16[16,64,256]{2,1,0:T(8,128)(2,1)} %bitcast.18), custom_call_target="tpu_custom_call" | custom-call | flops 400000000 | bytes 4000000 | tf_op jit(solution)/shard_map/pallas_call | solution.py:589
  3.4 0.0 copy-start
  3.5 0.0 copy-start.4
  3.5 0.0 copy-start.5
  3.5 0.0 copy-start.6
  3.5 0.0 copy-start.7
  3.5 0.0 copy-start.8
  3.5 9.4 %all-to-all-start = ((bf16[32,6,16,256]{3,2,1,0:T(8,128)(2,1)}), bf16[32,6,16,256]{3,2,1,0:T(8,128)(2,1)S(1)}, u32[]{:S(2)}, u32[]{:S(2)}) async-start(bf16[32,6,16,256]{3,2,1,0:T(8,128)(2,1)} %shard_map.179), calls=%async_computation | async-start | bytes 3145728 | tf_op jit(solution)/shard_map/all_to_all | solution.py:607
  12.9 0.0 copy-done.9
  12.9 0.1 pad_add_fusion.place_ref
  13.0 22.8 %all-to-all-done.x_ref = bf16[32,6,16,256]{3,2,1,0:T(8,128)(2,1)S(1)} async-done(((bf16[32,6,16,256]{3,2,1,0:T(8,128)(2,1)}), bf16[32,6,16,256]{3,2,1,0:T(8,128)(2,1)S(1)}, u32[]{:S(2)}, u32[]{:S(2)}) %all-to-all-start) | async-done | bytes 1572896 | tf_op jit(solution)/shard_map/all_to_all | solution.py:607
  35.8 0.0 copy-done
  35.8 0.0 copy-done.4
  35.8 0.0 copy-done.5
  35.8 0.0 copy-done.6
  35.9 0.0 copy-done.7
  35.9 0.0 copy-done.8
  35.9 9.6 %shard_map.180 = (bf16[4,10,64,256]{3,2,1,0:T(8,128)(2,1)S(1)}, bf16[1024,256]{1,0:T(8,128)(2,1)S(1)}, bf16[1024,256]{1,0:T(8,128)(2,1)S(1)}, bf16[1024,768]{1,0...) custom-call(s32[2]{0:T(128)S(1)} %pad_add_fusion.place_ref, ...), custom_call_target="tpu_custom_call" | custom-call | flops 8000000000 | bytes 12000000 | tf_op jit(solution)/shard_map/pallas_call | solution.py:589
  45.5 0.3 collective-permute-start
  45.8 4.8 %shard_map.181 = (bf16[1024,768]{1,0:T(8,128)(2,1)S(1)}, bf16[512,256]{1,0:T(8,128)(2,1)S(1)}, bf16[512,256]{1,0:T(8,128)(2,1)S(1)}) custom-call(s32[2]{0:T(128)S(1)} %pad_add_fusion.place_ref, bf16[1024,256]{1,0:T(8,128)(2,1)S(1)} %get-tuple-element.43.inputs_ref, bf16[1024,768]{1,0:T(8,128)(2,1)S(1)} %get-tuple-element.44.proj_ref, ...), custom_call_target="tpu_custom_call" | custom-call | flops 5000000000 | bytes 8000000 | tf_op jit(solution)/shard_map/pallas_call | solution.py:589
  50.5 0.6 collective-permute-start.1
  51.1 0.0 copy-start.1
  51.1 1.9 %shard_map.182 = (f32[1024,256]{1,0:T(8,128)S(1)}, f32[16,256]{1,0:T(8,128)S(1)}) custom-call(bf16[4,10,64,256]{3,2,1,0:T(8,128)(2,1)S(1)} %get-tuple-element.41.xs_ref, bf16[1024,256]{1,0:T(8,128)(2,1)S(1)} %get-tuple-element.42.in_ref, bf16[1024,768]{1,0:T(8,128)(2,1)S(1)} %get-tuple-element.49.proj_grad_ref, ...), custom_call_target="tpu_custom_call" | custom-call | tf_op jit(solution)/shard_map/pallas_call | solution.py:589
  53.0 0.0 collective-permute-done.1.other_head_ref
  53.0 0.0 collective-permute-done.other_tail_ref
  53.0 0.0 copy-done.1
  53.0 0.7 shard_map.183
  53.7 27.1 %all_to_all.15 = bf16[32,88,256]{2,1,0:T(8,128)(2,1)S(1)} all-to-all(bf16[32,88,256]{2,1,0:T(8,128)(2,1)S(1)} %bitcast.13), channel_id=1, replica_groups=mesh['yh'=2,'core'=2,'row'=4,'col'=8] {'row','col'}, dimensions={0} | all-to-all | bytes 2883584 | tf_op jit(solution)/shard_map/all_to_all | solution.py:607
  80.9 0.1 shard_map.184.mine_ref
  81.0 0.0 copy-start.2
  81.0 0.0 copy-start.3
  81.0 3.0 %collective-permute-start.2 = (bf16[56,256]{1,0:T(8,128)(2,1)S(1)}, bf16[56,256]{1,0:T(8,128)(2,1)S(1)}, u32[]{:S(2)}, u32[]{:S(2)}) collective-permute-start(bf16[56,256]{1,0:T(8,128)(2,1)S(1)} %shard_map.184.mine_ref), channel_id=1, source_target_pairs={{0,64},{64,0},{1,65},{65,1},{2,66},{66,2},{3,67},{67,3},{4,68},{68... | collective-permute-start | bytes 86024 | tf_op jit(solution)/shard_map/ppermute | solution.py:610
  84.0 2.5 %collective-permute-done.2.other_ref = bf16[56,256]{1,0:T(8,128)(2,1)S(1)} collective-permute-done((bf16[56,256]{1,0:T(8,128)(2,1)S(1)}, bf16[56,256]{1,0:T(8,128)(2,1)S(1)}, u32[]{:S(2)}, u32[]{:S(2)}) %collective-permute-start.2) | collective-permute-done | bytes 28704 | tf_op jit(solution)/shard_map/ppermute | solution.py:610
  86.5 1.0 shard_map.185
  87.5 4.1 %all-to-all-start.2 = ((bf16[32,56,256]{2,1,0:T(8,128)(2,1)}), bf16[32,56,256]{2,1,0:T(8,128)(2,1)S(1)}, u32[]{:S(2)}, u32[]{:S(2)}) async-start(bf16[32,56,256]{2,1,0:T(8,128)(2,1)} %bitcast.8), calls=%async_computation.2 | async-start | bytes 1835008 | tf_op jit(solution)/shard_map/all_to_all | solution.py:607
  91.5 0.0 copy-done.2
  91.5 0.0 copy-done.3
  91.5 0.5 shard_map.186
  92.1 3.7 %collective-permute-start.3 = (bf16[32,256]{1,0:T(8,128)(2,1)S(1)}, bf16[32,256]{1,0:T(8,128)(2,1)S(1)}, u32[]{:S(2)}, u32[]{:S(2)}) collective-permute-start(bf16[32,256]{1,0:T(8,128)(2,1)S(1)} %get-tuple-element.59), channel_id=1, source_target_pairs={{0,1},{1,2},{2,3},{3,4},{4,5},{5,6},{6,7},{8,9},{9,10},{10,11},{11... | collective-permute-start | bytes 49160 | tf_op jit(solution)/shard_map/ppermute | solution.py:615
  95.8 1.3 %collective-permute-start.4 = (bf16[32,256]{1,0:T(8,128)(2,1)S(1)}, bf16[32,256]{1,0:T(8,128)(2,1)S(1)}, u32[]{:S(2)}, u32[]{:S(2)}) collective-permute-start(bf16[32,256]{1,0:T(8,128)(2,1)S(1)} %get-tuple-element.60), channel_id=1, source_target_pairs={{1,0},{2,1},{3,2},{4,3},{5,4},{6,5},{7,6},{9,8},{10,9},{11,10},{12... | collective-permute-start | bytes 49160 | tf_op jit(solution)/shard_map/ppermute | solution.py:615
  97.1 1.2 %collective-permute-done.3.left_ref = bf16[32,256]{1,0:T(8,128)(2,1)S(1)} collective-permute-done((bf16[32,256]{1,0:T(8,128)(2,1)S(1)}, bf16[32,256]{1,0:T(8,128)(2,1)S(1)}, u32[]{:S(2)}, u32[]{:S(2)}) %collective-permute-start.3) | collective-permute-done | bytes 16416 | tf_op jit(solution)/shard_map/ppermute | solution.py:615
  98.2 4.7 %collective-permute-done.4.right_ref = bf16[32,256]{1,0:T(8,128)(2,1)S(1)} collective-permute-done((bf16[32,256]{1,0:T(8,128)(2,1)S(1)}, bf16[32,256]{1,0:T(8,128)(2,1)S(1)}, u32[]{:S(2)}, u32[]{:S(2)}) %collective-permute-start.4) | collective-permute-done | bytes 16416 | tf_op jit(solution)/shard_map/ppermute | solution.py:615
  102.9 2.0 %shard_map.187 = f32[1,16,64,256]{3,2,1,0:T(8,128)} custom-call(bf16[18,64,256]{2,1,0:T(8,128)(2,1)S(1)} %get-tuple-element.58.tile_ref, bf16[32,256]{1,0:T(8,128)(2,1)S(1)} %collective-permute-done.3.left_ref, bf16[32,256]{1,0:T(8,128)(2,1)S(1)} %collective-permute-done.4.right_ref, f32[9,256]{1,0:T(8,128)S(1)} %reshape.48.dw_ref), custom_call_target="tpu_custom_call" | custom-call | tf_op jit(solution)/shard_map/pallas_call | solution.py:589
  104.9 1.2 %all-to-all-done.2.mine_ref = bf16[32,56,256]{2,1,0:T(8,128)(2,1)S(1)} async-done(((bf16[32,56,256]{2,1,0:T(8,128)(2,1)}), bf16[32,56,256]{2,1,0:T(8,128)(2,1)S(1)}, u32[]{:S(2)}, u32[]{:S(2)}) %all-to-all-start.2) | async-done | bytes 917536 | tf_op jit(solution)/shard_map/all_to_all | solution.py:607
  106.1 0.0 collective-permute-start.5
  106.1 1.8 %shard_map.188 = (f32[256,768]{1,0:T(8,128)}, f32[256,256]{1,0:T(8,128)}, f32[256,1024]{1,0:T(8,128)}, f32[1024,256]{1,0:T(8,128)}) custom-call(s32[2]{0:T(128)S(1)} %pad_add_fusion.place_ref, bf16[32,56,256]{2,1,0:T(8,128)(2,1)S(1)} %all-to-all-done.2.mine_ref), custom_call_target="tpu_custom_call" | custom-call | tf_op jit(solution)/shard_map/pallas_call | solution.py:725
  107.9 0.6 collective-permute-done.5.other_ref
  108.6 1.9 %shard_map.189 = (f32[3,3,256]{2,1,0:T(4,128)}, f32[1,256]{1,0:T(1,128)}, f32[1,256]{1,0:T(1,128)}, f32[256,768]{1,0:T(8,128)}, f32[256,256]{1,0:T(8,128)}, /*index=5*/f32[256,1024]{1,0:T(8,128)}, f32[1024,256]{1,0:T(8,128)}) custom-call(s32[2]{0:T(128)S(1)} %pad_add_fusion.place_ref, ...), custom_call_target="tpu_custom_call", output_to_operand_aliasing={{3}: (3, {}), {4}: (4, {}), {5}: (5, {}), {6}: (6, {})} | custom-call | tf_op jit(solution)/shard_map/pallas_call | solution.py:733
  (2 shorter events, 0.0 us)
Async XLA Ops:
  3.4 9.5 %copy-start.9 = (bf16[3,3,256]{2,1,0:T(4,128)(2,1)S(1)}, bf16[3,3,256]{2,1,0:T(4,128)(2,1)}, u32[]{:S(2)}) copy-start(bf16[3,3,256]{2,1,0:T(4,128)(2,1)} %param.13) | copy-start | bytes 13828
  3.4 32.4 %copy-start = (bf16[256,768]{1,0:T(8,128)(2,1)S(1)}, bf16[256,768]{1,0:T(8,128)(2,1)}, u32[]{:S(2)}) copy-start(bf16[256,768]{1,0:T(8,128)(2,1)} %w_qkv_ref.3) | copy-start | bytes 1179652
  3.5 32.4 %copy-start.4 = (f32[256]{0:T(256)S(1)}, f32[256]{0:T(256)}, u32[]{:S(2)}) copy-start(f32[256]{0:T(256)} %param.14) | copy-start | bytes 3076
  3.5 32.4 %copy-start.5 = (bf16[256,1024]{1,0:T(8,128)(2,1)S(1)}, bf16[256,1024]{1,0:T(8,128)(2,1)}, u32[]{:S(2)}) copy-start(bf16[256,1024]{1,0:T(8,128)(2,1)} %w_up_ref.1) | copy-start | bytes 1572868
  3.5 32.4 %copy-start.6 = (bf16[1024,256]{1,0:T(8,128)(2,1)S(1)}, bf16[1024,256]{1,0:T(8,128)(2,1)}, u32[]{:S(2)}) copy-start(bf16[1024,256]{1,0:T(8,128)(2,1)} %w_down_ref.1) | copy-start | bytes 1572868
  3.5 32.4 %copy-start.7 = (bf16[256,256]{1,0:T(8,128)(2,1)S(1)}, bf16[256,256]{1,0:T(8,128)(2,1)}, u32[]{:S(2)}) copy-start(bf16[256,256]{1,0:T(8,128)(2,1)} %w_out_ref.1) | copy-start | bytes 393220
  3.5 32.4 %copy-start.8 = (f32[256]{0:T(256)S(1)}, f32[256]{0:T(256)}, u32[]{:S(2)}) copy-start(f32[256]{0:T(256)} %param.17) | copy-start | bytes 3076
  3.5 32.3 %all-to-all-start = ((bf16[32,6,16,256]{3,2,1,0:T(8,128)(2,1)}), bf16[32,6,16,256]{3,2,1,0:T(8,128)(2,1)S(1)}, u32[]{:S(2)}, u32[]{:S(2)}) async-start(bf16[32,6,16,256]{3,2,1,0:T(8,128)(2,1)} %shard_map.179), calls=%async_computation | async-start | bytes 3145728 | tf_op jit(solution)/shard_map/all_to_all | solution.py:607
  45.5 7.5 %collective-permute-start = (bf16[1024,256]{1,0:T(8,128)(2,1)S(1)}, bf16[1024,256]{1,0:T(8,128)(2,1)S(1)}, u32[]{:S(2)}, u32[]{:S(2)}) collective-permute-start(bf16[1024,256]{1,0:T(8,128)(2,1)S(1)} %get-tuple-element.55), channel_id=1, source_target_pairs={{0,32},{32,0},{1,33},{33,1},{2,34},{34,2},{3,35},{35,3},{4,36},{36... | collective-permute-start | bytes 1572872 | tf_op jit(solution)/shard_map/ppermute | solution.py:610
  50.5 2.5 %collective-permute-start.1 = (bf16[512,256]{1,0:T(8,128)(2,1)S(1)}, bf16[512,256]{1,0:T(8,128)(2,1)S(1)}, u32[]{:S(2)}, u32[]{:S(2)}) collective-permute-start(bf16[512,256]{1,0:T(8,128)(2,1)S(1)} %get-tuple-element.57), channel_id=1, source_target_pairs={{0,32},{32,0},{1,33},{33,1},{2,34},{34,2},{3,35},{35,3},{4,36},{36... | collective-permute-start | bytes 786440 | tf_op jit(solution)/shard_map/ppermute | solution.py:610
  51.1 1.9 %copy-start.1 = (bf16[320,384]{1,0:T(8,128)(2,1)S(1)}, bf16[320,384]{1,0:T(8,128)(2,1)}, u32[]{:S(2)}) copy-start(bf16[320,384]{1,0:T(8,128)(2,1)} %constant.22.clone.perm_ref) | copy-start | bytes 737284
  81.0 10.5 %copy-start.2 = (bf16[288,320]{1,0:T(8,128)(2,1)S(1)}, bf16[288,320]{1,0:T(8,128)(2,1)}, u32[]{:S(2)}) copy-start(bf16[288,320]{1,0:T(8,128)(2,1)} %constant.23.clone.main_ref) | copy-start | bytes 552964
  81.0 10.5 %copy-start.3 = (bf16[2,32,320]{2,1,0:T(8,128)(2,1)S(1)}, bf16[2,32,320]{2,1,0:T(8,128)(2,1)}, u32[]{:S(2)}) copy-start(bf16[2,32,320]{2,1,0:T(8,128)(2,1)} %constant.24.clone.edges_ref) | copy-start | bytes 122884
  81.0 5.5 %collective-permute-start.2 = (bf16[56,256]{1,0:T(8,128)(2,1)S(1)}, bf16[56,256]{1,0:T(8,128)(2,1)S(1)}, u32[]{:S(2)}, u32[]{:S(2)}) collective-permute-start(bf16[56,256]{1,0:T(8,128)(2,1)S(1)} %shard_map.184.mine_ref), channel_id=1, source_target_pairs={{0,64},{64,0},{1,65},{65,1},{2,66},{66,2},{3,67},{67,3},{4,68},{68... | collective-permute-start | bytes 86024 | tf_op jit(solution)/shard_map/ppermute | solution.py:610
  87.5 18.7 %all-to-all-start.2 = ((bf16[32,56,256]{2,1,0:T(8,128)(2,1)}), bf16[32,56,256]{2,1,0:T(8,128)(2,1)S(1)}, u32[]{:S(2)}, u32[]{:S(2)}) async-start(bf16[32,56,256]{2,1,0:T(8,128)(2,1)} %bitcast.8), calls=%async_computation.2 | async-start | bytes 1835008 | tf_op jit(solution)/shard_map/all_to_all | solution.py:607
  92.1 6.2 %collective-permute-start.3 = (bf16[32,256]{1,0:T(8,128)(2,1)S(1)}, bf16[32,256]{1,0:T(8,128)(2,1)S(1)}, u32[]{:S(2)}, u32[]{:S(2)}) collective-permute-start(bf16[32,256]{1,0:T(8,128)(2,1)S(1)} %get-tuple-element.59), channel_id=1, source_target_pairs={{0,1},{1,2},{2,3},{3,4},{4,5},{5,6},{6,7},{8,9},{9,10},{10,11},{11... | collective-permute-start | bytes 49160 | tf_op jit(solution)/shard_map/ppermute | solution.py:615
  95.8 7.2 %collective-permute-start.4 = (bf16[32,256]{1,0:T(8,128)(2,1)S(1)}, bf16[32,256]{1,0:T(8,128)(2,1)S(1)}, u32[]{:S(2)}, u32[]{:S(2)}) collective-permute-start(bf16[32,256]{1,0:T(8,128)(2,1)S(1)} %get-tuple-element.60), channel_id=1, source_target_pairs={{1,0},{2,1},{3,2},{4,3},{5,4},{6,5},{7,6},{9,8},{10,9},{11,10},{12... | collective-permute-start | bytes 49160 | tf_op jit(solution)/shard_map/ppermute | solution.py:615
  106.1 2.5 %collective-permute-start.5 = (bf16[32,56,256]{2,1,0:T(8,128)(2,1)S(1)}, bf16[32,56,256]{2,1,0:T(8,128)(2,1)S(1)}, u32[]{:S(2)}, u32[]{:S(2)}) collective-permute-start(bf16[32,56,256]{2,1,0:T(8,128)(2,1)S(1)} %all-to-all-done.2.mine_ref), channel_id=1, source_target_pairs={{0,32},{32,0},{1,33},{33,1},{2,34},{34,2},{3,35},{35,3},{4,36},{36... | collective-permute-start | bytes 2752520 | tf_op jit(solution)/shard_map/ppermute | solution.py:610

commit v7 on v6

--- a/solution.py
+++ b/solution.py
@@ -394,10 +394,8 @@
                     upstream_s[lanes, rows],
                 )
                 units.append((side, lanes, rows, parts))
-        results = [
-            attend_unit_back(*parts, lower, mask, turned_mask, wide_mask) for _, _, _, parts in units
-        ]
-        for (side, lanes, rows, _), grads in zip(units, results):
+        for side, lanes, rows, parts in units:
+            grads = attend_unit_back(*parts, lower, mask, turned_mask, wide_mask)
             query_grad_s[lanes, rows] = grads[0]
             proj_grad_ref[rows, 256 + 128 * side : 384 + 128 * side] = grads[1]
             proj_grad_ref[rows, 512 + 128 * side : 640 + 128 * side] = grads[2]
@@ -525,34 +523,45 @@
 
 
 def write_half(half, rows, qkv_ref, out_ref, up_ref, down_ref, tall, wide, sems):
-    values = rows[...].astype(F32)
-    tail = values[:, 0:32].reshape(1024, C)
-    head = values[:, 32:48].reshape(512, C)
-
-    def run(pairs):
-        copies = [pltpu.make_async_copy(*pair, sems.at[i]) for i, pair in enumerate(pairs)]
-        for copy in copies:
-            copy.start()
+    def run(copies):
         for copy in copies:
             copy.wait()
 
+    def start(copies, source, target):
+        copies.append(pltpu.make_async_copy(source, target, sems.at[len(copies)]))
+        copies[-1].start()
+
+    def part(block):
+        values = rows[8 * block : 8 * block + 8].astype(F32)
+        return values[:, 0:32].reshape(256, C), values[:, 32:48].reshape(128, C)
+
     @pl.when(half == 0)
     def _():
-        tall[...] = tail
-        wide[:, 0:256] = head[0:256]
-        wide[:, 256:512] = head[256:512]
-        run([(tall, down_ref), (wide.at[:, 0:512], qkv_ref.at[:, 0:512])])
+        copies = []
+        for block in range(4):
+            tail, head = part(block)
+            own = slice(256 * block, 256 * block + 256)
+            tall[own, :] = tail
+            start(copies, tall.at[own, :], down_ref.at[own, :])
+            own = slice(128 * (block % 2), 128 * (block % 2) + 128)
+            wide[own, 256 * (block // 2) : 256 * (block // 2) + 256] = head
+        start(copies, wide.at[:, 0:512], qkv_ref.at[:, 0:512])
+        run(copies)
 
     @pl.when(half == 1)
     def _():
+        copies = []
         for block in range(4):
-            wide[:, 256 * block : 256 * block + 256] = tail[256 * block : 256 * block + 256]
-        tall[0:512, :] = head
-        run([
-            (wide, up_ref),
-            (tall.at[0:256, :], qkv_ref.at[:, 512:768]),
-            (tall.at[256:512, :], out_ref),
-        ])
+            tail, head = part(block)
+            wide[:, 256 * block : 256 * block + 256] = tail
+            tall[128 * block : 128 * block + 128, :] = head
+            if block == 1:
+                start(copies, tall.at[0:256, :], qkv_ref.at[:, 512:768])
+        for block in range(4):
+            own = slice(64 * block, 64 * block + 64)
+            start(copies, wide.at[own, :], up_ref.at[own, :])
+        start(copies, tall.at[256:512, :], out_ref)
+        run(copies)
 
 
 def first_outputs_kernel(place_ref, mine_ref, *refs):
@@ -720,7 +729,7 @@
     other = swap(mine, "core")
     large = tuple(jax.ShapeDtypeStruct(n, F32) for n in ((C, 3 * C), (C, C), (C, FF), (FF, C)))
     small = tuple(jax.ShapeDtypeStruct(n, F32) for n in ((3, 3, C), (1, C), (1, C)))
-    scratch = [pltpu.VMEM((FF, C), F32), pltpu.VMEM((C, FF), F32), pltpu.SemaphoreType.DMA((3,))]
+    scratch = [pltpu.VMEM((FF, C), F32), pltpu.VMEM((C, FF), F32), pltpu.SemaphoreType.DMA((6,))]
     settings = dict(compiler_params=pltpu.CompilerParams(vmem_limit_bytes=24 * 2**20))
     begun = pl.pallas_call(
         first_outputs_kernel,

time: 112 us -> 112 us (level)
  no operation moved by 1% of the time
where the time goes in v7:
time: 112 us; the launch traced here: 111 us
  waiting for transfers between devices  33.1 us (30%)
  blocking collectives  27.1 us (24%)
  Pallas kernels  26.9 us (24%)
  starting transfers between devices  22.3 us (20%)
    all_to_all x1, blocking collectives, exchange(): lax.all_to_all(stacked, ('row', 'col'), split_axis=0, concat_axis=0, tile...  27.1 us
    all_to_all x2, waiting for transfers between devices, exchange(): lax.all_to_all(stacked, ('row', 'col'), split_axis=0, concat_axis=0, tile...  24 us
    pallas_call x9, Pallas kernels, call(): pl.pallas_call(kernel, out_shape=tuple((jax.ShapeDtypeStruct(shape, dtype...  23.3 us
    all_to_all x2, starting transfers between devices, exchange(): lax.all_to_all(stacked, ('row', 'col'), split_axis=0, concat_axis=0, tile...  13.5 us
    ppermute x2, waiting for transfers between devices, shift(): return lax.ppermute(values, axis, pairs)  5.86 us
    ppermute x2, starting transfers between devices, shift(): return lax.ppermute(values, axis, pairs)  4.99 us
    ppermute x4, starting transfers between devices, swap(): return lax.ppermute(values, axis, [(0, 1), (1, 0)])  3.81 us
    ppermute x4, waiting for transfers between devices, swap(): return lax.ppermute(values, axis, [(0, 1), (1, 0)])  3.2 us
  transfers between devices with their start and end apart: 8, of which 6 were waited for; matrix products, arithmetic and copies ran while one was open for 0% of the time, Pallas kernels for 10%

profile of v7, /device:TPU:0, one launch (start us, length us, event | category | flops | bytes accessed | tf_op | source)
XLA Modules:
  0.0 110.6 jit_solution(15022726967051459824)
XLA Ops:
  0.6 2.8 %shard_map.179 = bf16[32,6,16,256]{3,2,1,0:T(8,128)(2,1)} custom-call(bf16[16,64,256]{2,1,0:T(8,128)(2,1)} %bitcast.17, bf16[16,64,256]{2,1,0:T(8,128)(2,1)} %bitcast.18), custom_call_target="tpu_custom_call" | custom-call | flops 400000000 | bytes 4000000 | tf_op jit(solution)/shard_map/pallas_call | solution.py:598
  3.4 0.0 copy-start
  3.5 0.0 copy-start.4
  3.5 0.0 copy-start.5
  3.5 0.0 copy-start.6
  3.5 0.0 copy-start.7
  3.5 0.0 copy-start.8
  3.5 9.4 %all-to-all-start = ((bf16[32,6,16,256]{3,2,1,0:T(8,128)(2,1)}), bf16[32,6,16,256]{3,2,1,0:T(8,128)(2,1)S(1)}, u32[]{:S(2)}, u32[]{:S(2)}) async-start(bf16[32,6,16,256]{3,2,1,0:T(8,128)(2,1)} %shard_map.179), calls=%async_computation | async-start | bytes 3145728 | tf_op jit(solution)/shard_map/all_to_all | solution.py:616
  12.9 0.0 copy-done.9
  12.9 0.1 pad_add_fusion.place_ref
  13.0 22.8 %all-to-all-done.x_ref = bf16[32,6,16,256]{3,2,1,0:T(8,128)(2,1)S(1)} async-done(((bf16[32,6,16,256]{3,2,1,0:T(8,128)(2,1)}), bf16[32,6,16,256]{3,2,1,0:T(8,128)(2,1)S(1)}, u32[]{:S(2)}, u32[]{:S(2)}) %all-to-all-start) | async-done | bytes 1572896 | tf_op jit(solution)/shard_map/all_to_all | solution.py:616
  35.8 0.0 copy-done
  35.8 0.0 copy-done.4
  35.8 0.0 copy-done.5
  35.8 0.0 copy-done.6
  35.9 0.0 copy-done.7
  35.9 0.0 copy-done.8
  35.9 9.6 %shard_map.180 = (bf16[4,10,64,256]{3,2,1,0:T(8,128)(2,1)S(1)}, bf16[1024,256]{1,0:T(8,128)(2,1)S(1)}, bf16[1024,256]{1,0:T(8,128)(2,1)S(1)}, bf16[1024,768]{1,0...) custom-call(s32[2]{0:T(128)S(1)} %pad_add_fusion.place_ref, ...), custom_call_target="tpu_custom_call" | custom-call | flops 8000000000 | bytes 12000000 | tf_op jit(solution)/shard_map/pallas_call | solution.py:598
  45.5 0.3 collective-permute-start
  45.8 4.8 %shard_map.181 = (bf16[1024,768]{1,0:T(8,128)(2,1)S(1)}, bf16[512,256]{1,0:T(8,128)(2,1)S(1)}, bf16[512,256]{1,0:T(8,128)(2,1)S(1)}) custom-call(s32[2]{0:T(128)S(1)} %pad_add_fusion.place_ref, bf16[1024,256]{1,0:T(8,128)(2,1)S(1)} %get-tuple-element.43.inputs_ref, bf16[1024,768]{1,0:T(8,128)(2,1)S(1)} %get-tuple-element.44.proj_ref, ...), custom_call_target="tpu_custom_call" | custom-call | flops 5000000000 | bytes 8000000 | tf_op jit(solution)/shard_map/pallas_call | solution.py:598
  50.5 0.6 collective-permute-start.1
  51.1 0.0 copy-start.1
  51.1 1.9 %shard_map.182 = (f32[1024,256]{1,0:T(8,128)S(1)}, f32[16,256]{1,0:T(8,128)S(1)}) custom-call(bf16[4,10,64,256]{3,2,1,0:T(8,128)(2,1)S(1)} %get-tuple-element.41.xs_ref, bf16[1024,256]{1,0:T(8,128)(2,1)S(1)} %get-tuple-element.42.in_ref, bf16[1024,768]{1,0:T(8,128)(2,1)S(1)} %get-tuple-element.49.proj_grad_ref, ...), custom_call_target="tpu_custom_call" | custom-call | tf_op jit(solution)/shard_map/pallas_call | solution.py:598
  53.0 0.0 collective-permute-done.1.other_head_ref
  53.0 0.0 collective-permute-done.other_tail_ref
  53.0 0.0 copy-done.1
  53.0 0.7 shard_map.183
  53.7 27.1 %all_to_all.15 = bf16[32,88,256]{2,1,0:T(8,128)(2,1)S(1)} all-to-all(bf16[32,88,256]{2,1,0:T(8,128)(2,1)S(1)} %bitcast.13), channel_id=1, replica_groups=mesh['yh'=2,'core'=2,'row'=4,'col'=8] {'row','col'}, dimensions={0} | all-to-all | bytes 2883584 | tf_op jit(solution)/shard_map/all_to_all | solution.py:616
  80.9 0.1 shard_map.184.mine_ref
  81.0 0.0 copy-start.2
  81.0 0.0 copy-start.3
  81.0 3.0 %collective-permute-start.2 = (bf16[56,256]{1,0:T(8,128)(2,1)S(1)}, bf16[56,256]{1,0:T(8,128)(2,1)S(1)}, u32[]{:S(2)}, u32[]{:S(2)}) collective-permute-start(bf16[56,256]{1,0:T(8,128)(2,1)S(1)} %shard_map.184.mine_ref), channel_id=1, source_target_pairs={{0,64},{64,0},{1,65},{65,1},{2,66},{66,2},{3,67},{67,3},{4,68},{68... | collective-permute-start | bytes 86024 | tf_op jit(solution)/shard_map/ppermute | solution.py:619
  84.0 2.5 %collective-permute-done.2.other_ref = bf16[56,256]{1,0:T(8,128)(2,1)S(1)} collective-permute-done((bf16[56,256]{1,0:T(8,128)(2,1)S(1)}, bf16[56,256]{1,0:T(8,128)(2,1)S(1)}, u32[]{:S(2)}, u32[]{:S(2)}) %collective-permute-start.2) | collective-permute-done | bytes 28704 | tf_op jit(solution)/shard_map/ppermute | solution.py:619
  86.5 1.0 shard_map.185
  87.5 4.1 %all-to-all-start.2 = ((bf16[32,56,256]{2,1,0:T(8,128)(2,1)}), bf16[32,56,256]{2,1,0:T(8,128)(2,1)S(1)}, u32[]{:S(2)}, u32[]{:S(2)}) async-start(bf16[32,56,256]{2,1,0:T(8,128)(2,1)} %bitcast.8), calls=%async_computation.2 | async-start | bytes 1835008 | tf_op jit(solution)/shard_map/all_to_all | solution.py:616
  91.5 0.0 copy-done.2
  91.5 0.0 copy-done.3
  91.5 0.5 shard_map.186
  92.1 3.7 %collective-permute-start.3 = (bf16[32,256]{1,0:T(8,128)(2,1)S(1)}, bf16[32,256]{1,0:T(8,128)(2,1)S(1)}, u32[]{:S(2)}, u32[]{:S(2)}) collective-permute-start(bf16[32,256]{1,0:T(8,128)(2,1)S(1)} %get-tuple-element.59), channel_id=1, source_target_pairs={{0,1},{1,2},{2,3},{3,4},{4,5},{5,6},{6,7},{8,9},{9,10},{10,11},{11... | collective-permute-start | bytes 49160 | tf_op jit(solution)/shard_map/ppermute | solution.py:624
  95.8 1.3 %collective-permute-start.4 = (bf16[32,256]{1,0:T(8,128)(2,1)S(1)}, bf16[32,256]{1,0:T(8,128)(2,1)S(1)}, u32[]{:S(2)}, u32[]{:S(2)}) collective-permute-start(bf16[32,256]{1,0:T(8,128)(2,1)S(1)} %get-tuple-element.60), channel_id=1, source_target_pairs={{1,0},{2,1},{3,2},{4,3},{5,4},{6,5},{7,6},{9,8},{10,9},{11,10},{12... | collective-permute-start | bytes 49160 | tf_op jit(solution)/shard_map/ppermute | solution.py:624
  97.1 1.2 %collective-permute-done.3.left_ref = bf16[32,256]{1,0:T(8,128)(2,1)S(1)} collective-permute-done((bf16[32,256]{1,0:T(8,128)(2,1)S(1)}, bf16[32,256]{1,0:T(8,128)(2,1)S(1)}, u32[]{:S(2)}, u32[]{:S(2)}) %collective-permute-start.3) | collective-permute-done | bytes 16416 | tf_op jit(solution)/shard_map/ppermute | solution.py:624
  98.2 4.7 %collective-permute-done.4.right_ref = bf16[32,256]{1,0:T(8,128)(2,1)S(1)} collective-permute-done((bf16[32,256]{1,0:T(8,128)(2,1)S(1)}, bf16[32,256]{1,0:T(8,128)(2,1)S(1)}, u32[]{:S(2)}, u32[]{:S(2)}) %collective-permute-start.4) | collective-permute-done | bytes 16416 | tf_op jit(solution)/shard_map/ppermute | solution.py:624
  102.9 2.0 %shard_map.187 = f32[1,16,64,256]{3,2,1,0:T(8,128)} custom-call(bf16[18,64,256]{2,1,0:T(8,128)(2,1)S(1)} %get-tuple-element.58.tile_ref, bf16[32,256]{1,0:T(8,128)(2,1)S(1)} %collective-permute-done.3.left_ref, bf16[32,256]{1,0:T(8,128)(2,1)S(1)} %collective-permute-done.4.right_ref, f32[9,256]{1,0:T(8,128)S(1)} %reshape.48.dw_ref), custom_call_target="tpu_custom_call" | custom-call | tf_op jit(solution)/shard_map/pallas_call | solution.py:598
  104.9 1.2 %all-to-all-done.2.mine_ref = bf16[32,56,256]{2,1,0:T(8,128)(2,1)S(1)} async-done(((bf16[32,56,256]{2,1,0:T(8,128)(2,1)}), bf16[32,56,256]{2,1,0:T(8,128)(2,1)S(1)}, u32[]{:S(2)}, u32[]{:S(2)}) %all-to-all-start.2) | async-done | bytes 917536 | tf_op jit(solution)/shard_map/all_to_all | solution.py:616
  106.1 0.0 collective-permute-start.5
  106.1 1.8 %shard_map.188 = (f32[256,768]{1,0:T(8,128)}, f32[256,256]{1,0:T(8,128)}, f32[256,1024]{1,0:T(8,128)}, f32[1024,256]{1,0:T(8,128)}) custom-call(s32[2]{0:T(128)S(1)} %pad_add_fusion.place_ref, bf16[32,56,256]{2,1,0:T(8,128)(2,1)S(1)} %all-to-all-done.2.mine_ref), custom_call_target="tpu_custom_call" | custom-call | tf_op jit(solution)/shard_map/pallas_call | solution.py:734
  107.9 0.7 collective-permute-done.5.other_ref
  108.6 1.8 %shard_map.189 = (f32[3,3,256]{2,1,0:T(4,128)}, f32[1,256]{1,0:T(1,128)}, f32[1,256]{1,0:T(1,128)}, f32[256,768]{1,0:T(8,128)}, f32[256,256]{1,0:T(8,128)}, /*index=5*/f32[256,1024]{1,0:T(8,128)}, f32[1024,256]{1,0:T(8,128)}) custom-call(s32[2]{0:T(128)S(1)} %pad_add_fusion.place_ref, ...), custom_call_target="tpu_custom_call", output_to_operand_aliasing={{3}: (3, {}), {4}: (4, {}), {5}: (5, {}), {6}: (6, {})} | custom-call | tf_op jit(solution)/shard_map/pallas_call | solution.py:742
  (2 shorter events, 0.0 us)
Async XLA Ops:
  3.4 9.5 %copy-start.9 = (bf16[3,3,256]{2,1,0:T(4,128)(2,1)S(1)}, bf16[3,3,256]{2,1,0:T(4,128)(2,1)}, u32[]{:S(2)}) copy-start(bf16[3,3,256]{2,1,0:T(4,128)(2,1)} %param.13) | copy-start | bytes 13828
  3.4 32.4 %copy-start = (bf16[256,768]{1,0:T(8,128)(2,1)S(1)}, bf16[256,768]{1,0:T(8,128)(2,1)}, u32[]{:S(2)}) copy-start(bf16[256,768]{1,0:T(8,128)(2,1)} %w_qkv_ref.3) | copy-start | bytes 1179652
  3.5 32.4 %copy-start.4 = (f32[256]{0:T(256)S(1)}, f32[256]{0:T(256)}, u32[]{:S(2)}) copy-start(f32[256]{0:T(256)} %param.14) | copy-start | bytes 3076
  3.5 32.4 %copy-start.5 = (bf16[256,1024]{1,0:T(8,128)(2,1)S(1)}, bf16[256,1024]{1,0:T(8,128)(2,1)}, u32[]{:S(2)}) copy-start(bf16[256,1024]{1,0:T(8,128)(2,1)} %w_up_ref.1) | copy-start | bytes 1572868
  3.5 32.4 %copy-start.6 = (bf16[1024,256]{1,0:T(8,128)(2,1)S(1)}, bf16[1024,256]{1,0:T(8,128)(2,1)}, u32[]{:S(2)}) copy-start(bf16[1024,256]{1,0:T(8,128)(2,1)} %w_down_ref.1) | copy-start | bytes 1572868
  3.5 32.4 %copy-start.7 = (bf16[256,256]{1,0:T(8,128)(2,1)S(1)}, bf16[256,256]{1,0:T(8,128)(2,1)}, u32[]{:S(2)}) copy-start(bf16[256,256]{1,0:T(8,128)(2,1)} %w_out_ref.1) | copy-start | bytes 393220
  3.5 32.4 %copy-start.8 = (f32[256]{0:T(256)S(1)}, f32[256]{0:T(256)}, u32[]{:S(2)}) copy-start(f32[256]{0:T(256)} %param.17) | copy-start | bytes 3076
  3.5 32.3 %all-to-all-start = ((bf16[32,6,16,256]{3,2,1,0:T(8,128)(2,1)}), bf16[32,6,16,256]{3,2,1,0:T(8,128)(2,1)S(1)}, u32[]{:S(2)}, u32[]{:S(2)}) async-start(bf16[32,6,16,256]{3,2,1,0:T(8,128)(2,1)} %shard_map.179), calls=%async_computation | async-start | bytes 3145728 | tf_op jit(solution)/shard_map/all_to_all | solution.py:616
  45.5 7.5 %collective-permute-start = (bf16[1024,256]{1,0:T(8,128)(2,1)S(1)}, bf16[1024,256]{1,0:T(8,128)(2,1)S(1)}, u32[]{:S(2)}, u32[]{:S(2)}) collective-permute-start(bf16[1024,256]{1,0:T(8,128)(2,1)S(1)} %get-tuple-element.55), channel_id=1, source_target_pairs={{0,32},{32,0},{1,33},{33,1},{2,34},{34,2},{3,35},{35,3},{4,36},{36... | collective-permute-start | bytes 1572872 | tf_op jit(solution)/shard_map/ppermute | solution.py:619
  50.5 2.5 %collective-permute-start.1 = (bf16[512,256]{1,0:T(8,128)(2,1)S(1)}, bf16[512,256]{1,0:T(8,128)(2,1)S(1)}, u32[]{:S(2)}, u32[]{:S(2)}) collective-permute-start(bf16[512,256]{1,0:T(8,128)(2,1)S(1)} %get-tuple-element.57), channel_id=1, source_target_pairs={{0,32},{32,0},{1,33},{33,1},{2,34},{34,2},{3,35},{35,3},{4,36},{36... | collective-permute-start | bytes 786440 | tf_op jit(solution)/shard_map/ppermute | solution.py:619
  51.1 1.9 %copy-start.1 = (bf16[320,384]{1,0:T(8,128)(2,1)S(1)}, bf16[320,384]{1,0:T(8,128)(2,1)}, u32[]{:S(2)}) copy-start(bf16[320,384]{1,0:T(8,128)(2,1)} %constant.22.clone.perm_ref) | copy-start | bytes 737284
  81.0 10.5 %copy-start.2 = (bf16[288,320]{1,0:T(8,128)(2,1)S(1)}, bf16[288,320]{1,0:T(8,128)(2,1)}, u32[]{:S(2)}) copy-start(bf16[288,320]{1,0:T(8,128)(2,1)} %constant.23.clone.main_ref) | copy-start | bytes 552964
  81.0 10.5 %copy-start.3 = (bf16[2,32,320]{2,1,0:T(8,128)(2,1)S(1)}, bf16[2,32,320]{2,1,0:T(8,128)(2,1)}, u32[]{:S(2)}) copy-start(bf16[2,32,320]{2,1,0:T(8,128)(2,1)} %constant.24.clone.edges_ref) | copy-start | bytes 122884
  81.0 5.5 %collective-permute-start.2 = (bf16[56,256]{1,0:T(8,128)(2,1)S(1)}, bf16[56,256]{1,0:T(8,128)(2,1)S(1)}, u32[]{:S(2)}, u32[]{:S(2)}) collective-permute-start(bf16[56,256]{1,0:T(8,128)(2,1)S(1)} %shard_map.184.mine_ref), channel_id=1, source_target_pairs={{0,64},{64,0},{1,65},{65,1},{2,66},{66,2},{3,67},{67,3},{4,68},{68... | collective-permute-start | bytes 86024 | tf_op jit(solution)/shard_map/ppermute | solution.py:619
  87.5 18.7 %all-to-all-start.2 = ((bf16[32,56,256]{2,1,0:T(8,128)(2,1)}), bf16[32,56,256]{2,1,0:T(8,128)(2,1)S(1)}, u32[]{:S(2)}, u32[]{:S(2)}) async-start(bf16[32,56,256]{2,1,0:T(8,128)(2,1)} %bitcast.8), calls=%async_computation.2 | async-start | bytes 1835008 | tf_op jit(solution)/shard_map/all_to_all | solution.py:616
  92.1 6.2 %collective-permute-start.3 = (bf16[32,256]{1,0:T(8,128)(2,1)S(1)}, bf16[32,256]{1,0:T(8,128)(2,1)S(1)}, u32[]{:S(2)}, u32[]{:S(2)}) collective-permute-start(bf16[32,256]{1,0:T(8,128)(2,1)S(1)} %get-tuple-element.59), channel_id=1, source_target_pairs={{0,1},{1,2},{2,3},{3,4},{4,5},{5,6},{6,7},{8,9},{9,10},{10,11},{11... | collective-permute-start | bytes 49160 | tf_op jit(solution)/shard_map/ppermute | solution.py:624
  95.8 7.2 %collective-permute-start.4 = (bf16[32,256]{1,0:T(8,128)(2,1)S(1)}, bf16[32,256]{1,0:T(8,128)(2,1)S(1)}, u32[]{:S(2)}, u32[]{:S(2)}) collective-permute-start(bf16[32,256]{1,0:T(8,128)(2,1)S(1)} %get-tuple-element.60), channel_id=1, source_target_pairs={{1,0},{2,1},{3,2},{4,3},{5,4},{6,5},{7,6},{9,8},{10,9},{11,10},{12... | collective-permute-start | bytes 49160 | tf_op jit(solution)/shard_map/ppermute | solution.py:624
  106.1 2.5 %collective-permute-start.5 = (bf16[32,56,256]{2,1,0:T(8,128)(2,1)S(1)}, bf16[32,56,256]{2,1,0:T(8,128)(2,1)S(1)}, u32[]{:S(2)}, u32[]{:S(2)}) collective-permute-start(bf16[32,56,256]{2,1,0:T(8,128)(2,1)S(1)} %all-to-all-done.2.mine_ref), channel_id=1, source_target_pairs={{0,32},{32,0},{1,33},{33,1},{2,34},{34,2},{3,35},{35,3},{4,36},{36... | collective-permute-start | bytes 2752520 | tf_op jit(solution)/shard_map/ppermute | solution.py:619

commit v8 on v6

--- a/solution.py
+++ b/solution.py
@@ -622,6 +622,7 @@
         moved=4 * 10**6,
         limit=60,
     )
+    packed, place, dw_rows = lax.optimization_barrier((packed, place, dw_rows))
     arrived = exchange(packed)
 
     (

time: 112 us -> 111 us (level)
  blocking collectives: 27.1 us -> 58.1 us
  waiting for transfers between devices: 33 us -> 10.2 us
  starting transfers between devices: 22.3 us -> 12.9 us
    all_to_all x1 -> x2, blocking collectives: 27.1 us -> 58.1 us  [exchange(): lax.all_to_all(stacked, ('row', 'col'), split_axis=0, concat_axis=0, tile...]
    all_to_all x2 -> x1, waiting for transfers between devices: 24 us -> 1.23 us  [exchange(): lax.all_to_all(stacked, ('row', 'col'), split_axis=0, concat_axis=0, tile...]
    all_to_all x2 -> x1, starting transfers between devices: 13.5 us -> 4.06 us  [exchange(): lax.all_to_all(stacked, ('row', 'col'), split_axis=0, concat_axis=0, tile...]
  transfers between devices with their start and end apart: 8 -> 7, of which waited for: 6 -> 5; matrix products, arithmetic and copies ran while one was open for 0% -> 0% of each run, Pallas kernels for 10% -> 10%
where the time goes in v8:
time: 111 us; the launch traced here: 110 us
  blocking collectives  58.1 us (52%)
  Pallas kernels  26.9 us (24%)
  starting transfers between devices  12.9 us (12%)
  waiting for transfers between devices  10.2 us (9%)
    all_to_all x2, blocking collectives, exchange(): lax.all_to_all(stacked, ('row', 'col'), split_axis=0, concat_axis=0, tile...  58.1 us
    pallas_call x9, Pallas kernels, call(): pl.pallas_call(kernel, out_shape=tuple((jax.ShapeDtypeStruct(shape, dtype...  23.3 us
    ppermute x2, waiting for transfers between devices, shift(): return lax.ppermute(values, axis, pairs)  5.86 us
    ppermute x2, starting transfers between devices, shift(): return lax.ppermute(values, axis, pairs)  4.98 us
    all_to_all x1, starting transfers between devices, exchange(): lax.all_to_all(stacked, ('row', 'col'), split_axis=0, concat_axis=0, tile...  4.06 us
    ppermute x4, starting transfers between devices, swap(): return lax.ppermute(values, axis, [(0, 1), (1, 0)])  3.82 us
    ppermute x4, waiting for transfers between devices, swap(): return lax.ppermute(values, axis, [(0, 1), (1, 0)])  3.13 us
  transfers between devices with their start and end apart: 7, of which 5 were waited for; matrix products, arithmetic and copies ran while one was open for 0% of the time, Pallas kernels for 10%

profile of v8, /device:TPU:0, one launch (start us, length us, event | category | flops | bytes accessed | tf_op | source)
XLA Modules:
  0.0 110.0 jit_solution(18167380705530137870)
XLA Ops:
  0.6 0.7 reshape.48.dw_ref
  1.3 0.1 pad_add_fusion.place_ref
  1.4 2.8 %shard_map.179 = bf16[32,6,16,256]{3,2,1,0:T(8,128)(2,1)} custom-call(bf16[16,64,256]{2,1,0:T(8,128)(2,1)} %bitcast.17, bf16[16,64,256]{2,1,0:T(8,128)(2,1)} %bitcast.18), custom_call_target="tpu_custom_call" | custom-call | flops 400000000 | bytes 4000000 | tf_op jit(solution)/shard_map/pallas_call | solution.py:589
  4.2 0.0 copy-start
  4.2 0.0 copy-start.4
  4.2 0.0 copy-start.5
  4.2 0.0 copy-start.6
  4.2 0.0 copy-start.7
  4.2 0.0 copy-start.8
  4.3 32.7 %all_to_all.15.x_ref = bf16[32,6,16,256]{3,2,1,0:T(8,128)(2,1)S(1)} all-to-all(bf16[32,6,16,256]{3,2,1,0:T(8,128)(2,1)} %shard_map.179), channel_id=1, replica_groups=mesh['yh'=2,'core'=2,'row'=4,'col'=8] {'row','col'}, dimensions={0} | all-to-all | bytes 3145728 | tf_op jit(solution)/shard_map/all_to_all | solution.py:607
  36.9 0.0 copy-done
  36.9 0.0 copy-done.4
  37.0 0.0 copy-done.5
  37.0 0.0 copy-done.6
  37.0 0.0 copy-done.7
  37.0 0.0 copy-done.8
  37.0 9.6 %shard_map.180 = (bf16[4,10,64,256]{3,2,1,0:T(8,128)(2,1)S(1)}, bf16[1024,256]{1,0:T(8,128)(2,1)S(1)}, bf16[1024,256]{1,0:T(8,128)(2,1)S(1)}, bf16[1024,768]{1,0...) custom-call(s32[2]{0:T(128)S(1)} %pad_add_fusion.place_ref, ...), custom_call_target="tpu_custom_call" | custom-call | flops 8000000000 | bytes 12000000 | tf_op jit(solution)/shard_map/pallas_call | solution.py:589
  46.6 0.3 collective-permute-start
  46.9 4.7 %shard_map.181 = (bf16[1024,768]{1,0:T(8,128)(2,1)S(1)}, bf16[512,256]{1,0:T(8,128)(2,1)S(1)}, bf16[512,256]{1,0:T(8,128)(2,1)S(1)}) custom-call(s32[2]{0:T(128)S(1)} %pad_add_fusion.place_ref, bf16[1024,256]{1,0:T(8,128)(2,1)S(1)} %get-tuple-element.49.inputs_ref, bf16[1024,768]{1,0:T(8,128)(2,1)S(1)} %get-tuple-element.50.proj_ref, ...), custom_call_target="tpu_custom_call" | custom-call | flops 5000000000 | bytes 8000000 | tf_op jit(solution)/shard_map/pallas_call | solution.py:589
  51.6 0.6 collective-permute-start.1
  52.2 0.0 copy-start.1
  52.2 1.9 %shard_map.182 = (f32[1024,256]{1,0:T(8,128)S(1)}, f32[16,256]{1,0:T(8,128)S(1)}) custom-call(bf16[4,10,64,256]{3,2,1,0:T(8,128)(2,1)S(1)} %get-tuple-element.47.xs_ref, bf16[1024,256]{1,0:T(8,128)(2,1)S(1)} %get-tuple-element.48.in_ref, bf16[1024,768]{1,0:T(8,128)(2,1)S(1)} %get-tuple-element.55.proj_grad_ref, ...), custom_call_target="tpu_custom_call" | custom-call | tf_op jit(solution)/shard_map/pallas_call | solution.py:589
  54.1 0.0 collective-permute-done.1.other_head_ref
  54.1 0.0 collective-permute-done.other_tail_ref
  54.1 0.0 copy-done.1
  54.1 0.6 shard_map.183
  54.8 25.5 %all_to_all.16 = bf16[32,88,256]{2,1,0:T(8,128)(2,1)S(1)} all-to-all(bf16[32,88,256]{2,1,0:T(8,128)(2,1)S(1)} %bitcast.13), channel_id=1, replica_groups=mesh['yh'=2,'core'=2,'row'=4,'col'=8] {'row','col'}, dimensions={0} | all-to-all | bytes 2883584 | tf_op jit(solution)/shard_map/all_to_all | solution.py:607
  80.2 0.1 shard_map.184.mine_ref
  80.3 0.0 copy-start.2
  80.3 0.0 copy-start.3
  80.4 3.0 %collective-permute-start.2 = (bf16[56,256]{1,0:T(8,128)(2,1)S(1)}, bf16[56,256]{1,0:T(8,128)(2,1)S(1)}, u32[]{:S(2)}, u32[]{:S(2)}) collective-permute-start(bf16[56,256]{1,0:T(8,128)(2,1)S(1)} %shard_map.184.mine_ref), channel_id=1, source_target_pairs={{0,64},{64,0},{1,65},{65,1},{2,66},{66,2},{3,67},{67,3},{4,68},{68... | collective-permute-start | bytes 86024 | tf_op jit(solution)/shard_map/ppermute | solution.py:610
  83.3 2.5 %collective-permute-done.2.other_ref = bf16[56,256]{1,0:T(8,128)(2,1)S(1)} collective-permute-done((bf16[56,256]{1,0:T(8,128)(2,1)S(1)}, bf16[56,256]{1,0:T(8,128)(2,1)S(1)}, u32[]{:S(2)}, u32[]{:S(2)}) %collective-permute-start.2) | collective-permute-done | bytes 28704 | tf_op jit(solution)/shard_map/ppermute | solution.py:610
  85.8 1.0 shard_map.185
  86.8 4.1 %all-to-all-start.2 = ((bf16[32,56,256]{2,1,0:T(8,128)(2,1)}), bf16[32,56,256]{2,1,0:T(8,128)(2,1)S(1)}, u32[]{:S(2)}, u32[]{:S(2)}) async-start(bf16[32,56,256]{2,1,0:T(8,128)(2,1)} %bitcast.8), calls=%async_computation.2 | async-start | bytes 1835008 | tf_op jit(solution)/shard_map/all_to_all | solution.py:607
  90.9 0.0 copy-done.2
  90.9 0.0 copy-done.3
  90.9 0.5 shard_map.186
  91.4 3.7 %collective-permute-start.3 = (bf16[32,256]{1,0:T(8,128)(2,1)S(1)}, bf16[32,256]{1,0:T(8,128)(2,1)S(1)}, u32[]{:S(2)}, u32[]{:S(2)}) collective-permute-start(bf16[32,256]{1,0:T(8,128)(2,1)S(1)} %get-tuple-element.65), channel_id=1, source_target_pairs={{0,1},{1,2},{2,3},{3,4},{4,5},{5,6},{6,7},{8,9},{9,10},{10,11},{11... | collective-permute-start | bytes 49160 | tf_op jit(solution)/shard_map/ppermute | solution.py:615
  95.1 1.3 %collective-permute-start.4 = (bf16[32,256]{1,0:T(8,128)(2,1)S(1)}, bf16[32,256]{1,0:T(8,128)(2,1)S(1)}, u32[]{:S(2)}, u32[]{:S(2)}) collective-permute-start(bf16[32,256]{1,0:T(8,128)(2,1)S(1)} %get-tuple-element.66), channel_id=1, source_target_pairs={{1,0},{2,1},{3,2},{4,3},{5,4},{6,5},{7,6},{9,8},{10,9},{11,10},{12... | collective-permute-start | bytes 49160 | tf_op jit(solution)/shard_map/ppermute | solution.py:615
  96.4 1.2 %collective-permute-done.3.left_ref = bf16[32,256]{1,0:T(8,128)(2,1)S(1)} collective-permute-done((bf16[32,256]{1,0:T(8,128)(2,1)S(1)}, bf16[32,256]{1,0:T(8,128)(2,1)S(1)}, u32[]{:S(2)}, u32[]{:S(2)}) %collective-permute-start.3) | collective-permute-done | bytes 16416 | tf_op jit(solution)/shard_map/ppermute | solution.py:615
  97.6 4.7 %collective-permute-done.4.right_ref = bf16[32,256]{1,0:T(8,128)(2,1)S(1)} collective-permute-done((bf16[32,256]{1,0:T(8,128)(2,1)S(1)}, bf16[32,256]{1,0:T(8,128)(2,1)S(1)}, u32[]{:S(2)}, u32[]{:S(2)}) %collective-permute-start.4) | collective-permute-done | bytes 16416 | tf_op jit(solution)/shard_map/ppermute | solution.py:615
  102.3 2.0 %shard_map.187 = f32[1,16,64,256]{3,2,1,0:T(8,128)} custom-call(bf16[18,64,256]{2,1,0:T(8,128)(2,1)S(1)} %get-tuple-element.64.tile_ref, bf16[32,256]{1,0:T(8,128)(2,1)S(1)} %collective-permute-done.3.left_ref, bf16[32,256]{1,0:T(8,128)(2,1)S(1)} %collective-permute-done.4.right_ref, f32[9,256]{1,0:T(8,128)S(1)} %reshape.48.dw_ref), custom_call_target="tpu_custom_call" | custom-call | tf_op jit(solution)/shard_map/pallas_call | solution.py:589
  104.2 1.2 %all-to-all-done.2.mine_ref = bf16[32,56,256]{2,1,0:T(8,128)(2,1)S(1)} async-done(((bf16[32,56,256]{2,1,0:T(8,128)(2,1)}), bf16[32,56,256]{2,1,0:T(8,128)(2,1)S(1)}, u32[]{:S(2)}, u32[]{:S(2)}) %all-to-all-start.2) | async-done | bytes 917536 | tf_op jit(solution)/shard_map/all_to_all | solution.py:607
  105.5 0.0 collective-permute-start.5
  105.5 1.8 %shard_map.188 = (f32[256,768]{1,0:T(8,128)}, f32[256,256]{1,0:T(8,128)}, f32[256,1024]{1,0:T(8,128)}, f32[1024,256]{1,0:T(8,128)}) custom-call(s32[2]{0:T(128)S(1)} %pad_add_fusion.place_ref, bf16[32,56,256]{2,1,0:T(8,128)(2,1)S(1)} %all-to-all-done.2.mine_ref), custom_call_target="tpu_custom_call" | custom-call | tf_op jit(solution)/shard_map/pallas_call | solution.py:726
  107.3 0.6 collective-permute-done.5.other_ref
  107.9 1.9 %shard_map.189 = (f32[3,3,256]{2,1,0:T(4,128)}, f32[1,256]{1,0:T(1,128)}, f32[1,256]{1,0:T(1,128)}, f32[256,768]{1,0:T(8,128)}, f32[256,256]{1,0:T(8,128)}, /*index=5*/f32[256,1024]{1,0:T(8,128)}, f32[1024,256]{1,0:T(8,128)}) custom-call(s32[2]{0:T(128)S(1)} %pad_add_fusion.place_ref, ...), custom_call_target="tpu_custom_call", output_to_operand_aliasing={{3}: (3, {}), {4}: (4, {}), {5}: (5, {}), {6}: (6, {})} | custom-call | tf_op jit(solution)/shard_map/pallas_call | solution.py:734
Async XLA Ops:
  4.2 32.7 %copy-start = (bf16[256,768]{1,0:T(8,128)(2,1)S(1)}, bf16[256,768]{1,0:T(8,128)(2,1)}, u32[]{:S(2)}) copy-start(bf16[256,768]{1,0:T(8,128)(2,1)} %w_qkv_ref.3) | copy-start | bytes 1179652
  4.2 32.7 %copy-start.4 = (f32[256]{0:T(256)S(1)}, f32[256]{0:T(256)}, u32[]{:S(2)}) copy-start(f32[256]{0:T(256)} %param.14) | copy-start | bytes 3076
  4.2 32.7 %copy-start.5 = (bf16[256,1024]{1,0:T(8,128)(2,1)S(1)}, bf16[256,1024]{1,0:T(8,128)(2,1)}, u32[]{:S(2)}) copy-start(bf16[256,1024]{1,0:T(8,128)(2,1)} %w_up_ref.1) | copy-start | bytes 1572868
  4.2 32.7 %copy-start.6 = (bf16[1024,256]{1,0:T(8,128)(2,1)S(1)}, bf16[1024,256]{1,0:T(8,128)(2,1)}, u32[]{:S(2)}) copy-start(bf16[1024,256]{1,0:T(8,128)(2,1)} %w_down_ref.1) | copy-start | bytes 1572868
  4.2 32.7 %copy-start.7 = (bf16[256,256]{1,0:T(8,128)(2,1)S(1)}, bf16[256,256]{1,0:T(8,128)(2,1)}, u32[]{:S(2)}) copy-start(bf16[256,256]{1,0:T(8,128)(2,1)} %w_out_ref.1) | copy-start | bytes 393220
  4.2 32.7 %copy-start.8 = (f32[256]{0:T(256)S(1)}, f32[256]{0:T(256)}, u32[]{:S(2)}) copy-start(f32[256]{0:T(256)} %param.17) | copy-start | bytes 3076
  46.6 7.5 %collective-permute-start = (bf16[1024,256]{1,0:T(8,128)(2,1)S(1)}, bf16[1024,256]{1,0:T(8,128)(2,1)S(1)}, u32[]{:S(2)}, u32[]{:S(2)}) collective-permute-start(bf16[1024,256]{1,0:T(8,128)(2,1)S(1)} %get-tuple-element.61), channel_id=1, source_target_pairs={{0,32},{32,0},{1,33},{33,1},{2,34},{34,2},{3,35},{35,3},{4,36},{36... | collective-permute-start | bytes 1572872 | tf_op jit(solution)/shard_map/ppermute | solution.py:610
  51.6 2.4 %collective-permute-start.1 = (bf16[512,256]{1,0:T(8,128)(2,1)S(1)}, bf16[512,256]{1,0:T(8,128)(2,1)S(1)}, u32[]{:S(2)}, u32[]{:S(2)}) collective-permute-start(bf16[512,256]{1,0:T(8,128)(2,1)S(1)} %get-tuple-element.63), channel_id=1, source_target_pairs={{0,32},{32,0},{1,33},{33,1},{2,34},{34,2},{3,35},{35,3},{4,36},{36... | collective-permute-start | bytes 786440 | tf_op jit(solution)/shard_map/ppermute | solution.py:610
  52.2 1.9 %copy-start.1 = (bf16[320,384]{1,0:T(8,128)(2,1)S(1)}, bf16[320,384]{1,0:T(8,128)(2,1)}, u32[]{:S(2)}) copy-start(bf16[320,384]{1,0:T(8,128)(2,1)} %constant.22.clone.perm_ref) | copy-start | bytes 737284
  80.3 10.5 %copy-start.2 = (bf16[288,320]{1,0:T(8,128)(2,1)S(1)}, bf16[288,320]{1,0:T(8,128)(2,1)}, u32[]{:S(2)}) copy-start(bf16[288,320]{1,0:T(8,128)(2,1)} %constant.23.clone.main_ref) | copy-start | bytes 552964
  80.3 10.5 %copy-start.3 = (bf16[2,32,320]{2,1,0:T(8,128)(2,1)S(1)}, bf16[2,32,320]{2,1,0:T(8,128)(2,1)}, u32[]{:S(2)}) copy-start(bf16[2,32,320]{2,1,0:T(8,128)(2,1)} %constant.24.clone.edges_ref) | copy-start | bytes 122884
  80.4 5.5 %collective-permute-start.2 = (bf16[56,256]{1,0:T(8,128)(2,1)S(1)}, bf16[56,256]{1,0:T(8,128)(2,1)S(1)}, u32[]{:S(2)}, u32[]{:S(2)}) collective-permute-start(bf16[56,256]{1,0:T(8,128)(2,1)S(1)} %shard_map.184.mine_ref), channel_id=1, source_target_pairs={{0,64},{64,0},{1,65},{65,1},{2,66},{66,2},{3,67},{67,3},{4,68},{68... | collective-permute-start | bytes 86024 | tf_op jit(solution)/shard_map/ppermute | solution.py:610
  86.8 18.7 %all-to-all-start.2 = ((bf16[32,56,256]{2,1,0:T(8,128)(2,1)}), bf16[32,56,256]{2,1,0:T(8,128)(2,1)S(1)}, u32[]{:S(2)}, u32[]{:S(2)}) async-start(bf16[32,56,256]{2,1,0:T(8,128)(2,1)} %bitcast.8), calls=%async_computation.2 | async-start | bytes 1835008 | tf_op jit(solution)/shard_map/all_to_all | solution.py:607
  91.4 6.2 %collective-permute-start.3 = (bf16[32,256]{1,0:T(8,128)(2,1)S(1)}, bf16[32,256]{1,0:T(8,128)(2,1)S(1)}, u32[]{:S(2)}, u32[]{:S(2)}) collective-permute-start(bf16[32,256]{1,0:T(8,128)(2,1)S(1)} %get-tuple-element.65), channel_id=1, source_target_pairs={{0,1},{1,2},{2,3},{3,4},{4,5},{5,6},{6,7},{8,9},{9,10},{10,11},{11... | collective-permute-start | bytes 49160 | tf_op jit(solution)/shard_map/ppermute | solution.py:615
  95.1 7.2 %collective-permute-start.4 = (bf16[32,256]{1,0:T(8,128)(2,1)S(1)}, bf16[32,256]{1,0:T(8,128)(2,1)S(1)}, u32[]{:S(2)}, u32[]{:S(2)}) collective-permute-start(bf16[32,256]{1,0:T(8,128)(2,1)S(1)} %get-tuple-element.66), channel_id=1, source_target_pairs={{1,0},{2,1},{3,2},{4,3},{5,4},{6,5},{7,6},{9,8},{10,9},{11,10},{12... | collective-permute-start | bytes 49160 | tf_op jit(solution)/shard_map/ppermute | solution.py:615
  105.5 2.5 %collective-permute-start.5 = (bf16[32,56,256]{2,1,0:T(8,128)(2,1)S(1)}, bf16[32,56,256]{2,1,0:T(8,128)(2,1)S(1)}, u32[]{:S(2)}, u32[]{:S(2)}) collective-permute-start(bf16[32,56,256]{2,1,0:T(8,128)(2,1)S(1)} %all-to-all-done.2.mine_ref), channel_id=1, source_target_pairs={{0,32},{32,0},{1,33},{33,1},{2,34},{34,2},{3,35},{35,3},{4,36},{36... | collective-permute-start | bytes 2752520 | tf_op jit(solution)/shard_map/ppermute | solution.py:610
